TPU v7x, 128 devices: a whole 4x4x4 slice. The times are simulated.
128 devices in a mesh: fsdp: 64 (over z, x, y), layer: 2 (over core).
Axes of the slice: x: 4, y: 4, z: 4, core: 2. Of those that a mesh axis runs over, the one named last changes fastest.
Arguments:
- gradients: bfloat16 [4, 5120, 25600], P('layer', 'fsdp')
- sketch: bfloat16 [5120, 512], P('fsdp'), may hold values from -0.078125 to 0.078125
- rank_lists: int32 [4, 256], P('layer'), may hold values from 0 to 511, as said below
- old_basis: bfloat16 [4, 25600, 256], P('layer', 'fsdp'), may hold values from -6 to 6
- first_moment: float32 [4, 5120, 256], P('layer', 'fsdp'), may hold values from -6 to 6
- second_moment: float32 [4, 5120, 256], P('layer', 'fsdp'), may hold values from 0.1 to 4
Outputs:
- new_basis: bfloat16 [4, 25600, 256], P('layer', 'fsdp')
- projected: bfloat16 [4, 5120, 256], P('layer', 'fsdp')
- moment_one: float32 [4, 5120, 256], P('layer', 'fsdp')
- moment_two: float32 [4, 5120, 256], P('layer', 'fsdp')
- scores: float32 [512], replicated
Inputs may be any that keep to these rules, and one draw needn't show every extreme that they name: `rank_lists`: each row holds 256 different column numbers, among them 0 and 511.
All inputs are finite; a program needn't handle non-finite values.
Results may differ from a plain program's by a relative error of at most 0.0065.
Values may be sent and summed in bfloat16 or wider, within the bound.
No kernel may reach another device: no remote copies, remote signals or barrier semaphores. Data moves between devices by JAX's collectives and lax.ppermute only.
A program may use at most 128 MiB of HBM per device.

v0:
```python
import math

import jax
import jax.numpy as jnp
from jax import lax
from jax.sharding import PartitionSpec as P

FF = 25600
KS = 512
RANK = 256


highest = lax.Precision.HIGHEST


def refresh_panel(panel_cols, full_sketch, chosen, previous, moment_first, moment_second):
    columns_dims = (((0,), (0,)), ((), ()))
    sketched = lax.dot_general(
        panel_cols, full_sketch, columns_dims, preferred_element_type=jnp.float32
    ).astype(jnp.bfloat16)
    gram_part = lax.dot_general(
        sketched, sketched, columns_dims, preferred_element_type=jnp.float32
    )
    gram = lax.psum(gram_part, "fsdp")
    trace_sum = jnp.sum(jnp.diagonal(gram))
    unit_matrix = jnp.eye(KS, dtype=jnp.float32)
    corrected = 1.5 * unit_matrix - 0.5 * KS / trace_sum * gram
    picker = (lax.broadcasted_iota(jnp.int32, (KS, RANK), 0) == chosen[None, :]).astype(jnp.float32)
    scale_rms = jnp.sqrt(trace_sum / (FF * KS))
    factor = (jnp.dot(corrected, picker, precision=highest) / scale_rms).astype(jnp.bfloat16)
    basis_full = jnp.dot(sketched, factor, preferred_element_type=jnp.float32)
    basis_new = basis_full.astype(jnp.bfloat16)
    correlation_part = lax.dot_general(
        previous.astype(jnp.float32), basis_full, columns_dims, precision=highest
    )
    correlation = lax.psum(correlation_part, "fsdp") / math.sqrt(FF * RANK)
    summed = lax.psum_scatter(
        jnp.dot(panel_cols, basis_new, preferred_element_type=jnp.float32),
        "fsdp",
        scatter_dimension=0,
        tiled=True,
    )
    projected = (summed / math.sqrt(FF)).astype(jnp.bfloat16)
    moment_new = jnp.dot(moment_first, correlation, precision=highest)
    moment_sq = jnp.dot(moment_second, correlation * correlation, precision=highest)
    layer_scores = jnp.diagonal(gram) / FF
    return (basis_new, projected, moment_new, moment_sq, layer_scores)


def shards(gradients, sketch, rank_lists, old_basis, first_moment, second_moment):
    layer_count = gradients.shape[0]
    full_sketch = lax.all_gather(sketch, "fsdp", axis=0, tiled=True)
    panels = lax.all_to_all(gradients, "fsdp", split_axis=2, concat_axis=1, tiled=True)
    basis_list = []
    projected_list = []
    first_list = []
    second_list = []
    score_total = jnp.zeros((KS,), jnp.float32)
    for position in range(layer_count):
        panel_cols = panels[position]
        basis_new, projected, moment_new, moment_sq, layer_scores = refresh_panel(
            panel_cols,
            full_sketch,
            rank_lists[position],
            old_basis[position],
            first_moment[position],
            second_moment[position],
        )
        basis_list.append(basis_new)
        projected_list.append(projected)
        first_list.append(moment_new)
        second_list.append(moment_sq)
        score_total = score_total + layer_scores
    scores = lax.psum(score_total, "layer")
    return (
        jnp.stack(basis_list, 0),
        jnp.stack(projected_list, 0),
        jnp.stack(first_list, 0),
        jnp.stack(second_list, 0),
        scores,
    )


def solution(mesh):
    placed = (
        P("layer", "fsdp", None),
        P("fsdp", None),
        P("layer", None),
        P("layer", "fsdp", None),
        P("layer", "fsdp", None),
        P("layer", "fsdp", None),
    )
    return jax.shard_map(
        shards,
        mesh=mesh,
        in_specs=placed,
        out_specs=(
            P("layer", "fsdp", None),
            P("layer", "fsdp", None),
            P("layer", "fsdp", None),
            P("layer", "fsdp", None),
            P(),
        ),
        check_vma=False,
    )
```

profile of v0, /device:TPU:0, one launch (start us, length us, event | category | flops | bytes accessed | tf_op | source)
XLA Modules:
  0.0 1274.1 jit_solution(17908592910934508395)
XLA Ops:
  7.9 27.1 %copy.14 = bf16[2,80,25600]{1,0,2:T(2,128)(2,1)} copy(bf16[2,80,25600]{2,1,0:T(8,128)(2,1)} %param.6) | data formatting | bytes 16384000 | tf_op args[0]
  35.0 176.2 %all_to_all.15 = bf16[2,80,25600]{1,0,2:T(2,128)(2,1)} all-to-all(bf16[2,80,25600]{1,0,2:T(2,128)(2,1)} %copy.14), channel_id=1, replica_groups=mesh['fsdp'=64,'layer'=2] {'fsdp'}, dimensions={2} | all-to-all | bytes 16384000 | tf_op jit(solution)/shard_map/all_to_all | solution.py:53
  211.2 33.8 %copy.15 = bf16[2,80,64,400]{3,1,2,0:T(8,128)(2,1)} copy(bf16[2,80,64,400]{1,0,3,2:T(2,128)(2,1)} %bitcast.81) | data formatting | bytes 16384000 | tf_op jit(solution)/shard_map/all_to_all | solution.py:53
  245.0 8.7 fusion.46
  253.7 6.5 convolution_convert_fusion.1
  260.2 1.4 fusion.48
  261.6 2.3 convolution_convert_fusion
  263.9 1.4 fusion.50
  265.5 131.2 %all-reduce.7.cloned.1.call-done = (f32[512,512]{1,0:T(8,128)}, f32[512,512]{1,0:T(8,128)}) async-done(((f32[512,512]{1,0:T(8,128)}, f32[512,512]{1,0:T(8,128)}), (f32[512,512]{1,0:T(8,128)}, f32[512,512]{1,0:T(8,128)})) %all-reduce.7.cloned.1.call-update) | async-done | bytes 2097168 | tf_op jit(solution)/shard_map/psum | solution.py:24
  396.7 8.4 gather_fusion
  405.1 8.5 gather_fusion.1
  416.9 2.0 fusion
  420.3 1.3 convolution_bitcast_fusion.3
  423.2 6.4 convolution_bitcast_fusion.1
  429.7 5.9 copy.17
  435.7 6.4 convolution_bitcast_fusion
  442.1 5.9 copy.19
  448.1 3.2 psum.39
  452.1 95.8 %all-reduce.5.cloned.1.call-done = (f32[256,256]{0,1:T(8,128)}, f32[256,256]{0,1:T(8,128)}) async-done(((f32[256,256]{0,1:T(8,128)}, f32[256,256]{0,1:T(8,128)}), (f32[256,256]{0,1:T(8,128)}, f32[256,256]{0,1:T(8,128)})) %all-reduce.5.cloned.1.call-update) | async-done | bytes 524304 | tf_op jit(solution)/shard_map/psum | solution.py:36
  549.2 1.3 convolution_bitcast_fusion.7
  550.5 1.3 convolution_bitcast_fusion.4
  551.9 1.3 convolution_bitcast_fusion.5
  553.9 354.2 %reduce-scatter.7.cloned.1.call-done = f32[80,256]{1,0:T(8,128)} async-done(((f32[5120,256]{1,0:T(8,128)}), f32[80,256]{1,0:T(8,128)}) %reduce-scatter.7.cloned.1.call-update) | async-done | bytes 81936
  909.1 356.7 %reduce-scatter.9.cloned.1.call-done = f32[80,256]{1,0:T(8,128)} async-done(((f32[5120,256]{1,0:T(8,128)}), f32[80,256]{1,0:T(8,128)}) %reduce-scatter.9.cloned.1.call-update) | async-done | bytes 81936
  (43 shorter events, 10.1 us)
Async XLA Ops:
  7.2 246.5 %all-gather.2.cloned.1.call-start = ((), (), s32[]{:S(2)}) async-start(), calls=%async_computation.3 | async-start | bytes 5324800 | tf_op jit(solution)/shard_map/all_gather | solution.py:52
  7.9 388.8 %all-reduce.7.cloned.1.call-start = ((), (), s32[]{:S(2)}) async-start(), calls=%async_computation.7 | async-start | bytes 4194304 | tf_op jit(solution)/shard_map/psum | solution.py:24
  253.7 7.9 copy-start
  253.7 7.9 copy-start.1
  261.6 3.8 copy-start.6
  265.4 282.5 %all-reduce.5.cloned.1.call-start = ((), (), s32[]{:S(2)}) async-start(), calls=%async_computation.6 | async-start | bytes 1048576 | tf_op jit(solution)/shard_map/psum | solution.py:36
  396.7 22.6 %copy-start.2 = (f32[512,512]{1,0:T(8,128)S(1)}, f32[512,512]{1,0:T(8,128)}, u32[]{:S(2)}) copy-start(f32[512,512]{1,0:T(8,128)} %get-tuple-element.22) | copy-start | bytes 3145732
  405.1 15.2 %copy-start.3 = (bf16[2,400,256]{2,1,0:T(8,128)(2,1)S(1)}, bf16[2,400,256]{2,1,0:T(8,128)(2,1)}, u32[]{:S(2)}) copy-start(bf16[2,400,256]{2,1,0:T(8,128)(2,1)} %param.9) | copy-start | bytes 1228804
  423.0 485.1 %reduce-scatter.7.cloned.1.call-start = ((), (), s32[]{:S(2)}) async-start(), calls=%async_computation.4 | async-start | bytes 5324800
  435.6 830.2 %reduce-scatter.9.cloned.1.call-start = ((), (), s32[]{:S(2)}) async-start(), calls=%async_computation.5 | async-start | bytes 5324800
  448.0 99.8 %copy-start.4 = (f32[2,80,256]{2,1,0:T(8,128)S(1)}, f32[2,80,256]{2,1,0:T(8,128)}, u32[]{:S(2)}) copy-start(f32[2,80,256]{2,1,0:T(8,128)} %param.10) | copy-start | bytes 491524
  448.0 102.5 %copy-start.5 = (f32[2,80,256]{2,1,0:T(8,128)S(1)}, f32[2,80,256]{2,1,0:T(8,128)}, u32[]{:S(2)}) copy-start(f32[2,80,256]{2,1,0:T(8,128)} %param.11) | copy-start | bytes 491524
Sparse Core Ops, SparseCore 0:
  10.9 190.6 all-gather.1
  265.5 131.1 all-reduce.6
  423.1 124.7 all-reduce.4
  550.2 357.8 reduce-scatter.6
  910.5 355.2 reduce-scatter.8
where the time goes:
time: 1280 us; the launch traced here: 1270 us
  waiting for transfers between devices  939 us (73%)
  blocking collectives  179 us (14%)
  local copies, waits for them, and re-layouts  101 us (8%)
  matrix products  35.8 us (3%)
  between operations  16.7 us (1%)
    unnamed x7, waiting for transfers between devices  712 us
    all_to_all x1, blocking collectives, shards(): lax.all_to_all(gradients, 'fsdp', split_axis=2, concat_axis=1, tiled=True)  176 us
    psum x1, waiting for transfers between devices, refresh_panel(): gram = lax.psum(gram_part, 'fsdp')  131 us
    psum x1, waiting for transfers between devices, refresh_panel(): correlation = lax.psum(correlation_part, 'fsdp') / math.sqrt(FF * RANK)  95.8 us
    unnamed x20, local copies, waits for them, and re-layouts  41.6 us
    all_to_all x1, local copies, waits for them, and re-layouts, shards(): lax.all_to_all(gradients, 'fsdp', split_axis=2, concat_axis=1, tiled=True)  33.8 us
  transfers between devices with their start and end apart: 5, of which 4 were waited for; matrix products, arithmetic and copies ran while one was open for 8% of the time, Pallas kernels for 0%

commit v1 on v0

v1 whole, which is shorter than its diff:
```python
import math

import jax
import jax.numpy as jnp
from jax import lax
from jax.experimental import pallas as pl
from jax.experimental.pallas import tpu as pltpu
from jax.sharding import Mesh, PartitionSpec as P

FF = 25600
KS = 512
RANK = 256
ROWS = 80
COLS = 400
NL = 2
N = 64

bf16 = jnp.bfloat16
f32 = jnp.float32
highest = lax.Precision.HIGHEST
AX = ("z", "x", "y")
VMEM = 56 * 1024 * 1024

ORDERS = (("z", "x", "y"), ("x", "y", "z"), ("y", "z", "x"))
PANEL = (176, 176, 160)
BACK = (208, 208, 224)
ISSUE = (
    ((0, 2), (1, 2), (2, 1), (2, 3), (2, 2), (0, 1), (0, 3), (1, 1), (1, 3)),
    ((1, 2), (2, 2), (0, 1), (0, 3), (0, 2), (1, 1), (1, 3), (2, 1), (2, 3)),
    ((2, 2), (0, 2), (1, 1), (1, 3), (1, 2), (2, 1), (2, 3), (0, 1), (0, 3)),
)
HBM = pl.BlockSpec(memory_space=pl.ANY)
SMEM = pl.BlockSpec(memory_space=pltpu.SMEM)
INNER = pl.BlockSpec(memory_space=pltpu.VMEM)


def rest_axes(t, stage):
    return [a for a in AX if a in ORDERS[t][stage:]]


def shifted(x, axis, k):
    return lax.ppermute(x, axis, [(s, (s - k) % 4) for s in range(4)])


def params():
    return pltpu.CompilerParams(vmem_limit_bytes=VMEM)


def cost(nbytes, flops=0):
    return pl.CostEstimate(flops=flops, bytes_accessed=nbytes, transcendentals=0)


def run_copies(copies):
    for c in copies:
        c.start()
    for c in copies:
        c.wait()


def pack_kernel(pos_ref, g_ref, *refs):
    outs, scr, sem = refs[:12], refs[12:15], refs[15]
    g = pl.program_id(0)
    here = [pos_ref[i] for i in range(3)]
    for j in range(8):
        there = [g // 2, 2 * lax.rem(g, 2) + j // 4, j % 4]
        tails = []
        for l in range(NL):
            rest = g_ref[l, :, COLS * j + 384 : COLS * (j + 1)]
            tails.append(
                jnp.concatenate(
                    [rest[16 * i : 16 * i + 16] for i in range(5)] + [jnp.zeros((16, 48), bf16)], axis=1
                )
            )
        for t in range(3):
            first = AX.index(ORDERS[t][0])
            other = [i for i in range(3) if i != first]
            k = lax.rem(here[first] - there[first] + 4, 4)
            at = there[other[0]] * 4 + there[other[1]]
            for l in range(NL):
                scr[t][k, at, pl.ds(ROWS * l, ROWS), :] = g_ref[
                    l, :, COLS * j + 128 * t : COLS * j + 128 * (t + 1)
                ]
            if t < 2:
                scr[t][k, at, pl.ds(160, 16), :] = tails[t]

    @pl.when(g == 7)
    def _():
        run_copies(
            [
                pltpu.make_async_copy(scr[t].at[k], outs[4 * t + k], sem.at[4 * t + k])
                for t in range(3)
                for k in range(4)
            ]
        )


def pack(pos, g):
    outs = pl.pallas_call(
        pack_kernel,
        grid=(8,),
        in_specs=[SMEM, pl.BlockSpec((NL, ROWS, 8 * COLS), lambda i: (0, 0, i))],
        out_specs=[HBM] * 12,
        out_shape=[jax.ShapeDtypeStruct((16, n, 128), bf16) for n in PANEL for _ in range(4)],
        scratch_shapes=[pltpu.VMEM((4, 16, n, 128), bf16) for n in PANEL] + [pltpu.SemaphoreType.DMA((12,))],
        compiler_params=params(),
        cost_estimate=cost(17_000_000),
    )(pos, g)
    return [[o.reshape((4, 4) + o.shape[1:]) for o in outs[4 * t : 4 * t + 4]] for t in range(3)]


def permute_stage(bufs, stage, orders=ISSUE):
    got = [[b[0], None, None, None] for b in bufs]
    for t, k in orders[stage]:
        got[t][k] = shifted(bufs[t][k], ORDERS[t][stage], k)
    return got


def flat(got, stage):
    return [got[t][k] for t, k in ISSUE[stage]] + [got[t][0] for t in range(3)]


def unflat(refs, stage):
    got = [[None] * 4 for _ in range(3)]
    for (t, k), r in zip(ISSUE[stage], refs[:9]):
        got[t][k] = r
    for t in range(3):
        got[t][0] = refs[9 + t]
    return got


def second_kernel(pos_ref, *refs):
    first = unflat(refs[:12], 0)
    outs, sem = refs[12:21], refs[21]
    here = [pos_ref[i] for i in range(3)]
    copies = []
    for at, (t, k) in enumerate(ISSUE[1]):
        axis = ORDERS[t][1]
        place = lax.rem(here[AX.index(axis)] + 4 - k, 4)
        for k1 in range(4):
            src = first[t][k1]
            src = src.at[place] if rest_axes(t, 1).index(axis) == 0 else src.at[:, place]
            copies.append(pltpu.make_async_copy(src, outs[at].at[k1], sem.at[4 * at + k1]))
    run_copies(copies)


def second(pos, got):
    outs = pl.pallas_call(
        second_kernel,
        in_specs=[SMEM] + [HBM] * 12,
        out_specs=[HBM] * 9,
        out_shape=[jax.ShapeDtypeStruct((4, 4, PANEL[t], 128), bf16) for t, _ in ISSUE[1]],
        scratch_shapes=[pltpu.SemaphoreType.DMA((36,))],
        compiler_params=params(),
        cost_estimate=cost(13_000_000),
    )(pos, *flat(got, 0))
    bufs = [[None] * 4 for _ in range(3)]
    for (t, k), o in zip(ISSUE[1], outs):
        bufs[t][k] = o
    return bufs


def third_kernel(pos_ref, *refs):
    first = unflat(refs[:12], 0)
    later = [[None] * 4 for _ in range(3)]
    for (t, k), r in zip(ISSUE[1], refs[12:21]):
        later[t][k] = r
    outs, sem = refs[21:33], refs[33]
    here = [pos_ref[i] for i in range(3)]
    copies = []
    for at, (t, k) in enumerate(ISSUE[2] + ((0, 0), (1, 0), (2, 0))):
        axis2, axis3 = ORDERS[t][1], ORDERS[t][2]
        own = here[AX.index(axis2)]
        place = lax.rem(here[AX.index(axis3)] + 4 - k, 4)
        for k1 in range(4):
            src = first[t][k1]
            src = src.at[own, place] if rest_axes(t, 1).index(axis2) == 0 else src.at[place, own]
            copies.append(pltpu.make_async_copy(src, outs[at].at[0, k1], sem.at[len(copies)]))
        for k2 in range(1, 4):
            copies.append(
                pltpu.make_async_copy(later[t][k2].at[:, place], outs[at].at[k2], sem.at[len(copies)])
            )
    run_copies(copies)


def third(pos, got1, got2):
    order = ISSUE[2] + ((0, 0), (1, 0), (2, 0))
    outs = pl.pallas_call(
        third_kernel,
        in_specs=[SMEM] + [HBM] * 21,
        out_specs=[HBM] * 12,
        out_shape=[jax.ShapeDtypeStruct((4, 4, PANEL[t], 128), bf16) for t, _ in order],
        scratch_shapes=[pltpu.SemaphoreType.DMA((84,))],
        compiler_params=params(),
        cost_estimate=cost(17_000_000),
    )(pos, *flat(got1, 0), *[got2[t][k] for t, k in ISSUE[1]])
    bufs = [[None] * 4 for _ in range(3)]
    for (t, k), o in zip(order, outs):
        bufs[t][k] = o
    return bufs


def panel_kernel(pos_ref, *refs):
    got = unflat(refs[:12], 2)
    s_ref, old_ref, pick_ref = refs[12:15]
    back = refs[15:27]
    sk_ref, sums_ref, diag_ref = refs[27:30]
    scr_in, scr_out = refs[30:33], refs[33:36]
    x_ref, s_vmem, acc_ref, skt_ref, sem, sem_s, sem_out = refs[36:]
    here = [pos_ref[i] for i in range(3)]

    loads = [
        pltpu.make_async_copy(got[t][k], scr_in[t].at[k], sem.at[4 * t + k]) for t in range(3) for k in range(4)
    ]
    loads.append(pltpu.make_async_copy(s_ref, s_vmem, sem_s))
    run_copies(loads)

    def lay(src, _):
        there = [src // 16, lax.rem(src // 4, 4), lax.rem(src, 4)]
        k = {a: lax.rem(there[i] + 4 - here[i], 4) for i, a in enumerate(AX)}
        row = pl.multiple_of(src * ROWS, 16)
        for t in range(3):
            o1, o2, o3 = ORDERS[t]
            block = scr_in[t].at[k[o3], k[o2], k[o1]]
            for l in range(NL):
                x_ref[pl.ds(row, ROWS), 512 * l + 128 * t : 512 * l + 128 * (t + 1)] = block[
                    ROWS * l : ROWS * (l + 1), :
                ]
            if t < 2:
                tail = block[160:176, :]
                for i in range(5):
                    x_ref[pl.ds(pl.multiple_of(row + 16 * i, 16), 16), 512 * t + 384 : 512 * t + 512] = (
                        jnp.concatenate([tail[:, 16 * i : 16 * i + 16], jnp.zeros((16, 112), bf16)], axis=1)
                    )
        return 0

    lax.fori_loop(0, N, lay, 0)

    acc_ref[...] = jnp.zeros_like(acc_ref)

    def add(i, _):
        rows = pl.ds(pl.multiple_of(i * 640, 640), 640)
        acc_ref[...] += lax.dot_general(
            s_vmem[rows, :], x_ref[rows, :], (((0,), (0,)), ((), ())), preferred_element_type=f32
        )
        return 0

    lax.fori_loop(0, 8, add, 0)
    for l in range(NL):
        wide = acc_ref[:, 512 * l : 512 * (l + 1)]
        skt = wide.astype(bf16)
        skt_ref[...] = skt
        sk = jnp.transpose(skt.astype(f32), (1, 0))
        diag_ref[l : l + 1, :] = jnp.sum(sk * sk, axis=0, keepdims=True)
        sk_ref[l] = sk.astype(bf16)
        chosen = jnp.dot(sk_ref[l], pick_ref[l], preferred_element_type=f32).astype(bf16)
        sums_ref[l, :, 0:RANK] = jnp.dot(skt_ref[...], chosen, preferred_element_type=f32).astype(bf16)
        sums_ref[l, :, RANK:KS] = jnp.dot(
            skt_ref[:, 0:COLS], old_ref[l], preferred_element_type=f32
        ).astype(bf16)

    def out(i, _):
        kz, kx = lax.rem(i // 4 + 4 - here[0], 4), lax.rem(lax.rem(i, 4) + 4 - here[1], 4)
        rows = pl.ds(pl.multiple_of(i * 4 * ROWS, 64), 4 * ROWS)
        for l in range(NL):
            part = jnp.dot(
                x_ref[rows, 512 * l : 512 * (l + 1)], sk_ref[l], preferred_element_type=f32
            ).astype(bf16)
            for y in range(4):
                ky = lax.rem(y + 4 - here[2], 4)
                one = part[ROWS * y : ROWS * (y + 1)]
                for t in range(3):
                    scr_out[t][kz, kx, ky, ROWS * l : ROWS * (l + 1), :] = one[:, 128 * t : 128 * (t + 1)]
                last = one[:, 384:512]
                if l == 0:
                    scr_out[0][kz, kx, ky, 160:208, :] = last[0:48]
                    scr_out[1][kz, kx, ky, 160:192, :] = last[48:80]
                else:
                    scr_out[1][kz, kx, ky, 192:208, :] = last[0:16]
                    scr_out[2][kz, kx, ky, 160:224, :] = last[16:80]
        return 0

    lax.fori_loop(0, 16, out, 0)
    stores = []
    for t in range(3):
        for k in range(4):
            src = scr_out[t]
            first = AX.index(ORDERS[t][0])
            src = (src.at[k], src.at[:, k], src.at[:, :, k])[first]
            stores.append(pltpu.make_async_copy(src, back[4 * t + k], sem_out.at[4 * t + k]))
    run_copies(stores)


def panel_products(pos, got, s, old, picker):
    outs = pl.pallas_call(
        panel_kernel,
        in_specs=[SMEM] + [HBM] * 13 + [INNER] * 2,
        out_specs=[HBM] * 12 + [INNER] * 3,
        out_shape=[jax.ShapeDtypeStruct((4, 4, n, 128), bf16) for n in BACK for _ in range(4)]
        + [
            jax.ShapeDtypeStruct((NL, KS, KS), bf16),
            jax.ShapeDtypeStruct((NL, KS, KS), bf16),
            jax.ShapeDtypeStruct((NL, KS), f32),
        ],
        scratch_shapes=[pltpu.VMEM((4, 4, 4, n, 128), bf16) for n in PANEL]
        + [pltpu.VMEM((4, 4, 4, n, 128), bf16) for n in BACK]
        + [
            pltpu.VMEM((N * ROWS, NL * 512), bf16),
            pltpu.VMEM((N * ROWS, KS), bf16),
            pltpu.VMEM((KS, NL * 512), f32),
            pltpu.VMEM((KS, 512), bf16),
            pltpu.SemaphoreType.DMA((12,)),
            pltpu.SemaphoreType.DMA,
            pltpu.SemaphoreType.DMA((12,)),
        ],
        compiler_params=params(),
        cost_estimate=cost(26_000_000, 11_000_000_000),
    )(pos, *flat(got, 2), s, old, picker)
    return [list(outs[4 * t : 4 * t + 4]) for t in range(3)], outs[12], outs[13], outs[14]


def reduce_kernel(stage, *refs):
    got = unflat(refs[:12], stage)
    outs = refs[12:]
    for t in range(3):
        axis = ORDERS[t][stage + 1]
        dim = rest_axes(t, stage + 1).index(axis)
        for k in range(4):
            out = outs[4 * t + k]
            if stage == 0:
                for i in range(4):
                    at = (k, i) if dim == 0 else (i, k)
                    out[i] = sum(got[t][j][at].astype(f32) for j in range(4)).astype(bf16)
            else:
                out[...] = sum(got[t][j][k].astype(f32) for j in range(4)).astype(bf16)


def reduce_stage(got, stage):
    lead = (4,) if stage == 0 else ()
    outs = pl.pallas_call(
        lambda *refs: reduce_kernel(stage, *refs),
        in_specs=[INNER] * 12,
        out_specs=[INNER] * 12,
        out_shape=[jax.ShapeDtypeStruct(lead + (n, 128), bf16) for n in BACK for _ in range(4)],
        compiler_params=params(),
        cost_estimate=cost(13_000_000 if stage == 0 else 3_300_000),
    )(*flat(got, stage))
    return [list(outs[4 * t : 4 * t + 4]) for t in range(3)]


def shift_back(bufs, stage):
    got = [[b[0], None, None, None] for b in bufs]
    for t, k in ISSUE[stage]:
        got[t][k] = shifted(bufs[t][4 - k], ORDERS[t][stage], k)
    return got


def shards(gradients, sketch, rank_lists, old_basis, first_moment, second_moment):
    full_sketch = lax.all_gather(sketch, AX, axis=0, tiled=True)
    pos = jnp.stack([lax.axis_index(a) for a in AX]).astype(jnp.int32)
    got1 = permute_stage(pack(pos, gradients), 0)
    got2 = permute_stage(second(pos, got1), 1)
    got3 = permute_stage(third(pos, got1, got2), 2)
    picker = (lax.broadcasted_iota(jnp.int32, (NL, KS, RANK), 1) == rank_lists[:, None, :]).astype(bf16)
    parts, sketched, sums, diag = panel_products(pos, got3, full_sketch, old_basis, picker)

    high = diag.astype(bf16)
    rest = diag - high.astype(f32)
    mid = rest.astype(bf16)
    low = (rest - mid.astype(f32)).astype(bf16)
    pieces = jnp.concatenate([high, mid, low, jnp.zeros((2, KS), bf16)], 0)
    blocks = sums.reshape(NL, N, 8, KS).transpose(1, 0, 2, 3).reshape(N, NL * 8, KS)
    send = jnp.concatenate([blocks, jnp.broadcast_to(pieces[None], (N, 8, KS))], 1)
    got = lax.all_to_all(send, AX, 0, 0, tiled=True)
    total = jnp.sum(got.astype(f32), axis=0)
    row_sums = total[: NL * 8].reshape(NL, 8, KS)
    diag = total[16:18] + total[18:20] + total[20:22]
    trace = jnp.sum(diag, axis=1)

    me = (lax.axis_index("z") * 4 + lax.axis_index("x")) * 4 + lax.axis_index("y")
    my_rows = me * 8 + lax.broadcasted_iota(jnp.int32, (8, RANK), 0)
    owned = []
    for l in range(NL):
        scale = 0.5 * KS / trace[l]
        rms = jnp.sqrt(trace[l] / (FF * KS))
        my_diag = lax.dynamic_slice_in_dim(diag[l], me * 8, 8, 0)[:, None]
        corrected = jnp.where(
            my_rows == rank_lists[l][None, :], 1.5 - scale * my_diag, -scale * row_sums[l][:, :RANK]
        )
        owned.append(
            jnp.concatenate([(corrected / rms).astype(bf16), row_sums[l][:, RANK:].astype(bf16)], 1)
        )
    mine = jnp.concatenate(owned, 0)
    everyone = lax.all_to_all(jnp.broadcast_to(mine[None], (N, NL * 8, KS)), AX, 0, 0, tiled=True)

    back = shift_back(parts, 0)
    back = shift_back(reduce_stage(back, 0), 1)
    back = shift_back(reduce_stage(back, 1), 2)
    t0, t1, t2 = [sum(p.astype(f32) for p in back[t]) for t in range(3)]
    last = (jnp.concatenate([t0[160:], t1[160:192]], 0), jnp.concatenate([t1[192:], t2[160:]], 0))

    basis_list, projected_list, first_list, second_list = [], [], [], []
    for l in range(NL):
        both = everyone[:, 8 * l : 8 * l + 8].reshape(KS, KS)
        factor, inner = both[:, :RANK], both[:, RANK:]
        basis_list.append(
            jnp.dot(sketched[l, :COLS], factor, preferred_element_type=f32).astype(bf16)
        )
        correlation = lax.dot_general(
            inner, factor, (((0,), (0,)), ((), ())), preferred_element_type=f32
        ) / math.sqrt(FF * RANK)
        rows = slice(ROWS * l, ROWS * (l + 1))
        t_rows = jnp.concatenate([t0[rows], t1[rows], t2[rows], last[l]], 1)
        projected_list.append(
            (jnp.dot(t_rows, factor.astype(f32), precision=highest) / math.sqrt(FF)).astype(bf16)
        )
        first_list.append(jnp.dot(first_moment[l], correlation, precision=highest))
        second_list.append(jnp.dot(second_moment[l], correlation * correlation, precision=highest))
    scores = lax.psum((diag[0] + diag[1]) / FF, "layer")
    return (
        jnp.stack(basis_list, 0),
        jnp.stack(projected_list, 0),
        jnp.stack(first_list, 0),
        jnp.stack(second_list, 0),
        scores,
    )


def solution(mesh):
    cube = Mesh(mesh.devices.reshape(4, 4, 4, 2), AX + ("layer",))
    rows = P("layer", AX, None)
    return jax.shard_map(
        shards,
        mesh=cube,
        in_specs=(rows, P(AX, None), P("layer", None), rows, rows, rows),
        out_specs=(rows, rows, rows, rows, P()),
        check_vma=False,
    )
```

time: 1280 us -> 849 us (0.66)
  waiting for transfers between devices: 939 us -> 194 us
  Pallas kernels: 0 us -> 505 us
  blocking collectives: 179 us -> 3.04 us
  starting transfers between devices: 0.38 us -> 107 us
  local copies, waits for them, and re-layouts: 101 us -> 11.1 us
  matrix products: 35.8 us -> 2.78 us
    unnamed x7 -> x1, waiting for transfers between devices: 712 us -> 0.68 us
    pallas_call x0 -> x6, Pallas kernels: none -> 505 us  [the longest x1 257 us: third(): pl.pallas_call(third_kernel, in_specs=[SMEM] + [HBM] * 21, out_specs=[HBM...]
    psum x2 -> x0, waiting for transfers between devices: 227 us -> none  [the longest x1 131 us: refresh_panel(): gram = lax.psum(gram_part, 'fsdp')]
    ppermute x0 -> x54, waiting for transfers between devices: none -> 193 us  [shifted(): return lax.ppermute(x, axis, [(s, (s - k) % 4) for s in range(4)])]
    all_to_all x1 -> x0, blocking collectives: 176 us -> none  [shards(): lax.all_to_all(gradients, 'fsdp', split_axis=2, concat_axis=1, tiled=True)]
    ppermute x0 -> x54, starting transfers between devices: none -> 88.1 us  [shifted(): return lax.ppermute(x, axis, [(s, (s - k) % 4) for s in range(4)])]
    unnamed x20 -> x98, local copies, waits for them, and re-layouts: 41.6 us -> 7.84 us
    all_to_all x1 -> x0, local copies, waits for them, and re-layouts: 33.8 us -> none  [shards(): lax.all_to_all(gradients, 'fsdp', split_axis=2, concat_axis=1, tiled=True)]
  transfers between devices with their start and end apart: 5 -> 57, of which waited for: 4 -> 23; matrix products, arithmetic and copies ran while one was open for 8% -> 1% of each run, Pallas kernels for 0% -> 55%
where the time goes in v1:
time: 849 us
  Pallas kernels  505 us (59%)
  waiting for transfers between devices  194 us (23%)
  starting transfers between devices  107 us (13%)
  between operations  17.5 us (2%)
  local copies, waits for them, and re-layouts  11.1 us (1%)
    pallas_call x1, Pallas kernels, third(): pl.pallas_call(third_kernel, in_specs=[SMEM] + [HBM] * 21, out_specs=[HBM...  257 us
    pallas_call x1, Pallas kernels, second(): pl.pallas_call(second_kernel, in_specs=[SMEM] + [HBM] * 12, out_specs=[HB...  193 us
    ppermute x54, waiting for transfers between devices, shifted(): return lax.ppermute(x, axis, [(s, (s - k) % 4) for s in range(4)])  193 us
    ppermute x54, starting transfers between devices, shifted(): return lax.ppermute(x, axis, [(s, (s - k) % 4) for s in range(4)])  88.1 us
    pallas_call x1, Pallas kernels, panel_products(): pl.pallas_call(panel_kernel, in_specs=[SMEM] + [HBM] * 13 + [INNER] * 2,...  35.9 us
  transfers between devices with their start and end apart: 57, of which 23 were waited for; matrix products, arithmetic and copies ran while one was open for 1% of the time, Pallas kernels for 55%

profile of v1, /device:TPU:0, one launch (start us, length us, event | category | flops | bytes accessed | tf_op | source)
XLA Modules:
  0.0 848.7 jit_solution(2361471867534474177)
XLA Ops:
  8.5 11.4 %shard_map.101 = (bf16[16,176,128]{2,1,0:T(8,128)(2,1)}, bf16[16,176,128]{2,1,0:T(8,128)(2,1)}, bf16[16,176,128]{2,1,0:T(8,128)(2,1)}, bf16[16,176,128]{2,1,0:T(...) custom-call(s32[3]{0:T(128)} %pad_add_fusion.pos_ref, ...), custom_call_target="tpu_custom_call" | custom-call | bytes 17000000 | tf_op jit(solution)/shard_map/pallas_call | solution.py:98
  32.2 24.6 %collective-permute-done.2.refs_2_ = bf16[4,4,160,128]{3,2,1,0:T(8,128)(2,1)S(1)} collective-permute-done((bf16[4,4,160,128]{3,2,1,0:T(8,128)(2,1)}, bf16[4,4,160,128]{3,2,1,0:T(8,128)(2,1)S(1)}, u32[]{:S(2)}, u32[]{:S(2)}) %collective-permute-start.2) | collective-permute-done | bytes 655392 | tf_op jit(solution)/shard_map/ppermute | solution.py:42
  64.0 6.7 collective-permute-done.5.refs_5_
  70.7 5.0 collective-permute-done.6.refs_6_
  75.7 4.9 collective-permute-done.7.refs_7_
  84.5 192.7 %shard_map.102 = (bf16[4,4,176,128]{3,2,1,0:T(8,128)(2,1)}, bf16[4,4,160,128]{3,2,1,0:T(8,128)(2,1)}, bf16[4,4,176,128]{3,2,1,0:T(8,128)(2,1)}, bf16[4,4,176,128...) custom-call(s32[3]{0:T(128)} %pad_add_fusion.pos_ref, ...), custom_call_target="tpu_custom_call" | custom-call | bytes 13000000 | tf_op jit(solution)/shard_map/pallas_call | solution.py:147
  282.1 13.9 %collective-permute-done.10.refs_13_ = bf16[4,4,160,128]{3,2,1,0:T(8,128)(2,1)S(1)} collective-permute-done((bf16[4,4,160,128]{3,2,1,0:T(8,128)(2,1)}, bf16[4,4,160,128]{3,2,1,0:T(8,128)(2,1)S(1)}, u32[]{:S(2)}, u32[]{:S(2)}) %collective-permute-start.10) | collective-permute-done | bytes 655392 | tf_op jit(solution)/shard_map/ppermute | solution.py:42
  296.8 4.5 collective-permute-done.16.refs_19_
  301.3 6.3 collective-permute-start.14
  309.5 27.9 %collective-permute-done.14.refs_17_ = bf16[4,4,176,128]{3,2,1,0:T(8,128)(2,1)S(1)} collective-permute-done((bf16[4,4,176,128]{3,2,1,0:T(8,128)(2,1)}, bf16[4,4,176,128]{3,2,1,0:T(8,128)(2,1)S(1)}, u32[]{:S(2)}, u32[]{:S(2)}) %collective-permute-start.14) | collective-permute-done | bytes 720928 | tf_op jit(solution)/shard_map/ppermute | solution.py:42
  342.1 256.7 %shard_map.103 = (bf16[4,4,160,128]{3,2,1,0:T(8,128)(2,1)}, bf16[4,4,176,128]{3,2,1,0:T(8,128)(2,1)}, bf16[4,4,176,128]{3,2,1,0:T(8,128)(2,1)}, bf16[4,4,176,128...) custom-call(s32[3]{0:T(128)} %pad_add_fusion.pos_ref, ...), custom_call_target="tpu_custom_call" | custom-call | bytes 17000000 | tf_op jit(solution)/shard_map/pallas_call | solution.py:187
  605.5 12.8 %collective-permute-done.18.refs_0_ = bf16[4,4,160,128]{3,2,1,0:T(8,128)(2,1)S(1)} collective-permute-done((bf16[4,4,160,128]{3,2,1,0:T(8,128)(2,1)}, bf16[4,4,160,128]{3,2,1,0:T(8,128)(2,1)S(1)}, u32[]{:S(2)}, u32[]{:S(2)}) %collective-permute-start.18) | collective-permute-done | bytes 655392 | tf_op jit(solution)/shard_map/ppermute | solution.py:42
  621.3 7.4 collective-permute-done.23.refs_5_
  637.0 13.6 %collective-permute-done.22.refs_4_ = bf16[4,4,176,128]{3,2,1,0:T(8,128)(2,1)S(1)} collective-permute-done((bf16[4,4,176,128]{3,2,1,0:T(8,128)(2,1)}, bf16[4,4,176,128]{3,2,1,0:T(8,128)(2,1)S(1)}, u32[]{:S(2)}, u32[]{:S(2)}) %collective-permute-start.22) | collective-permute-done | bytes 720928 | tf_op jit(solution)/shard_map/ppermute | solution.py:42
  651.5 35.9 %shard_map.104 = (bf16[4,4,208,128]{3,2,1,0:T(8,128)(2,1)}, bf16[4,4,208,128]{3,2,1,0:T(8,128)(2,1)}, bf16[4,4,208,128]{3,2,1,0:T(8,128)(2,1)}, bf16[4,4,208,128...) custom-call(s32[3]{0:T(128)} %pad_add_fusion.pos_ref, ...), custom_call_target="tpu_custom_call" | custom-call | flops 11000000512 | bytes 26000000 | tf_op jit(solution)/shard_map/pallas_call | solution.py:294
  696.2 14.9 %collective-permute-done.27.refs_0_ = bf16[4,4,208,128]{3,2,1,0:T(8,128)(2,1)S(1)} collective-permute-done((bf16[4,4,208,128]{3,2,1,0:T(8,128)(2,1)}, bf16[4,4,208,128]{3,2,1,0:T(8,128)(2,1)S(1)}, u32[]{:S(2)}, u32[]{:S(2)}) %collective-permute-start.27) | collective-permute-done | bytes 852000 | tf_op jit(solution)/shard_map/ppermute | solution.py:42
  714.4 12.8 %collective-permute-done.32.refs_5_ = bf16[4,4,208,128]{3,2,1,0:T(8,128)(2,1)S(1)} collective-permute-done((bf16[4,4,208,128]{3,2,1,0:T(8,128)(2,1)}, bf16[4,4,208,128]{3,2,1,0:T(8,128)(2,1)S(1)}, u32[]{:S(2)}, u32[]{:S(2)}) %collective-permute-start.32) | collective-permute-done | bytes 852000 | tf_op jit(solution)/shard_map/ppermute | solution.py:42
  731.5 9.2 %all-to-all-start = ((bf16[64,24,512]{2,1,0:T(8,128)(2,1)}), bf16[64,24,512]{2,1,0:T(8,128)(2,1)S(1)}, u32[]{:S(2)}, u32[]{:S(2)}) async-start(bf16[64,24,512]{2,1,0:T(8,128)(2,1)} %pad_maximum_fusion), calls=%async_computation | async-start | bytes 3145728 | tf_op jit(solution)/shard_map/all_to_all | solution.py:373
  740.7 11.0 %collective-permute-done.34.refs_7_ = bf16[4,4,208,128]{3,2,1,0:T(8,128)(2,1)} collective-permute-done((bf16[4,4,208,128]{3,2,1,0:T(8,128)(2,1)}, bf16[4,4,208,128]{3,2,1,0:T(8,128)(2,1)}, u32[]{:S(2)}, u32[]{:S(2)}) %collective-permute-start.34) | collective-permute-done | bytes 852000 | tf_op jit(solution)/shard_map/ppermute | solution.py:42
  757.2 6.0 shard_map.105
  765.6 5.1 collective-permute-start.38
  772.2 9.6 %collective-permute-start.37 = (bf16[4,224,128]{2,1,0:T(8,128)(2,1)}, bf16[4,224,128]{2,1,0:T(8,128)(2,1)S(1)}, u32[]{:S(2)}, u32[]{:S(2)}) collective-permute-start(bf16[4,224,128]{2,1,0:T(8,128)(2,1)} %get-tuple-element.126), channel_id=1, source_target_pairs={{0,64},{32,96},{64,0},{96,32},{1,65},{33,97},{65,1},{97,33},{2,66}... | collective-permute-start | bytes 688136 | tf_op jit(solution)/shard_map/ppermute | solution.py:42
  812.2 9.3 %all-to-all-start.1 = ((bf16[64,16,512]{2,1,0:T(8,128)(2,1)}), bf16[64,16,512]{2,1,0:T(8,128)(2,1)S(1)}, u32[]{:S(2)}, u32[]{:S(2)}) async-start(bf16[64,16,512]{2,1,0:T(8,128)(2,1)} %broadcast_in_dim.35), calls=%async_computation.1 | async-start | bytes 2097152 | tf_op jit(solution)/shard_map/all_to_all | solution.py:393
  823.3 8.6 %collective-permute-done.53 = bf16[224,128]{1,0:T(8,128)(2,1)S(1)} collective-permute-done((bf16[224,128]{1,0:T(8,128)(2,1)S(1)}, bf16[224,128]{1,0:T(8,128)(2,1)S(1)}, u32[]{:S(2)}, u32[]{:S(2)}) %collective-permute-start.53) | collective-permute-done | bytes 57376 | tf_op jit(solution)/shard_map/ppermute | solution.py:42
  (244 shorter events, 120.4 us)
Async XLA Ops:
  7.2 643.7 %all-gather.2.cloned.1.call-start = ((), (), s32[]{:S(2)}) async-start(), calls=%async_computation.2 | async-start | bytes 5324800 | tf_op jit(solution)/shard_map/all_gather | solution.py:358
  19.9 44.0 %collective-permute-start = (bf16[4,4,176,128]{3,2,1,0:T(8,128)(2,1)}, bf16[4,4,176,128]{3,2,1,0:T(8,128)(2,1)S(1)}, u32[]{:S(2)}, u32[]{:S(2)}) collective-permute-start(bf16[4,4,176,128]{3,2,1,0:T(8,128)(2,1)} %bitcast.95), channel_id=1, source_target_pairs={{0,64},{32,96},{64,0},{96,32},{1,65},{33,97},{65,1},{97,33},{2,66}... | collective-permute-start | bytes 2162696 | tf_op jit(solution)/shard_map/ppermute | solution.py:42
  24.0 32.9 %collective-permute-start.2 = (bf16[4,4,160,128]{3,2,1,0:T(8,128)(2,1)}, bf16[4,4,160,128]{3,2,1,0:T(8,128)(2,1)S(1)}, u32[]{:S(2)}, u32[]{:S(2)}) collective-permute-start(bf16[4,4,160,128]{3,2,1,0:T(8,128)(2,1)} %bitcast.98), channel_id=1, source_target_pairs={{0,6},{2,0},{4,2},{6,4},{1,7},{3,1},{5,3},{7,5},{8,14},{10,8},{12,... | collective-permute-start | bytes 1966088 | tf_op jit(solution)/shard_map/ppermute | solution.py:42
  27.0 33.3 %collective-permute-start.3 = (bf16[4,4,160,128]{3,2,1,0:T(8,128)(2,1)}, bf16[4,4,160,128]{3,2,1,0:T(8,128)(2,1)S(1)}, u32[]{:S(2)}, u32[]{:S(2)}) collective-permute-start(bf16[4,4,160,128]{3,2,1,0:T(8,128)(2,1)} %bitcast.97), channel_id=1, source_target_pairs={{0,2},{2,4},{4,6},{6,0},{1,3},{3,5},{5,7},{7,1},{8,10},{10,12},{12... | collective-permute-start | bytes 1966088 | tf_op jit(solution)/shard_map/ppermute | solution.py:42
  27.0 34.2 %collective-permute-start.4 = (bf16[4,4,160,128]{3,2,1,0:T(8,128)(2,1)}, bf16[4,4,160,128]{3,2,1,0:T(8,128)(2,1)S(1)}, u32[]{:S(2)}, u32[]{:S(2)}) collective-permute-start(bf16[4,4,160,128]{3,2,1,0:T(8,128)(2,1)} %bitcast.96), channel_id=1, source_target_pairs={{0,4},{2,6},{4,0},{6,2},{1,5},{3,7},{5,1},{7,3},{8,12},{10,14},{12... | collective-permute-start | bytes 1966088 | tf_op jit(solution)/shard_map/ppermute | solution.py:42
  29.2 34.7 %collective-permute-start.1 = (bf16[4,4,176,128]{3,2,1,0:T(8,128)(2,1)}, bf16[4,4,176,128]{3,2,1,0:T(8,128)(2,1)S(1)}, u32[]{:S(2)}, u32[]{:S(2)}) collective-permute-start(bf16[4,4,176,128]{3,2,1,0:T(8,128)(2,1)} %bitcast.94), channel_id=1, source_target_pairs={{0,16},{8,24},{16,0},{24,8},{1,17},{9,25},{17,1},{25,9},{2,18},{10... | collective-permute-start | bytes 2162696 | tf_op jit(solution)/shard_map/ppermute | solution.py:42
  277.2 30.4 %collective-permute-start.11 = (bf16[4,4,176,128]{3,2,1,0:T(8,128)(2,1)}, bf16[4,4,176,128]{3,2,1,0:T(8,128)(2,1)S(1)}, u32[]{:S(2)}, u32[]{:S(2)}) collective-permute-start(bf16[4,4,176,128]{3,2,1,0:T(8,128)(2,1)} %get-tuple-element.91), channel_id=1, source_target_pairs={{0,24},{8,0},{16,8},{24,16},{1,25},{9,1},{17,9},{25,17},{2,26},{10... | collective-permute-start | bytes 2162696 | tf_op jit(solution)/shard_map/ppermute | solution.py:42
  280.2 27.4 %collective-permute-start.17 = (bf16[4,4,160,128]{3,2,1,0:T(8,128)(2,1)}, bf16[4,4,160,128]{3,2,1,0:T(8,128)(2,1)S(1)}, u32[]{:S(2)}, u32[]{:S(2)}) collective-permute-start(bf16[4,4,160,128]{3,2,1,0:T(8,128)(2,1)} %get-tuple-element.97), channel_id=1, source_target_pairs={{0,32},{32,64},{64,96},{96,0},{1,33},{33,65},{65,97},{97,1},{2,34}... | collective-permute-start | bytes 1966088 | tf_op jit(solution)/shard_map/ppermute | solution.py:42
  280.2 29.3 %collective-permute-start.12 = (bf16[4,4,176,128]{3,2,1,0:T(8,128)(2,1)}, bf16[4,4,176,128]{3,2,1,0:T(8,128)(2,1)S(1)}, u32[]{:S(2)}, u32[]{:S(2)}) collective-permute-start(bf16[4,4,176,128]{3,2,1,0:T(8,128)(2,1)} %get-tuple-element.92), channel_id=1, source_target_pairs={{0,8},{8,16},{16,24},{24,0},{1,9},{9,17},{17,25},{25,1},{2,10},{10... | collective-permute-start | bytes 2162696 | tf_op jit(solution)/shard_map/ppermute | solution.py:42
  301.3 36.0 %collective-permute-start.14 = (bf16[4,4,176,128]{3,2,1,0:T(8,128)(2,1)}, bf16[4,4,176,128]{3,2,1,0:T(8,128)(2,1)S(1)}, u32[]{:S(2)}, u32[]{:S(2)}) collective-permute-start(bf16[4,4,176,128]{3,2,1,0:T(8,128)(2,1)} %get-tuple-element.94), channel_id=1, source_target_pairs={{0,6},{2,0},{4,2},{6,4},{1,7},{3,1},{5,3},{7,5},{8,14},{10,8},{12,... | collective-permute-start | bytes 2162696 | tf_op jit(solution)/shard_map/ppermute | solution.py:42
  307.6 29.7 %collective-permute-start.15 = (bf16[4,4,176,128]{3,2,1,0:T(8,128)(2,1)}, bf16[4,4,176,128]{3,2,1,0:T(8,128)(2,1)S(1)}, u32[]{:S(2)}, u32[]{:S(2)}) collective-permute-start(bf16[4,4,176,128]{3,2,1,0:T(8,128)(2,1)} %get-tuple-element.95), channel_id=1, source_target_pairs={{0,2},{2,4},{4,6},{6,0},{1,3},{3,5},{5,7},{7,1},{8,10},{10,12},{12... | collective-permute-start | bytes 2162696 | tf_op jit(solution)/shard_map/ppermute | solution.py:42
  307.6 33.5 %collective-permute-start.9 = (bf16[4,4,176,128]{3,2,1,0:T(8,128)(2,1)}, bf16[4,4,176,128]{3,2,1,0:T(8,128)(2,1)S(1)}, u32[]{:S(2)}, u32[]{:S(2)}) collective-permute-start(bf16[4,4,176,128]{3,2,1,0:T(8,128)(2,1)} %get-tuple-element.89), channel_id=1, source_target_pairs={{0,4},{2,6},{4,0},{6,2},{1,5},{3,7},{5,1},{7,3},{8,12},{10,14},{12... | collective-permute-start | bytes 2162696 | tf_op jit(solution)/shard_map/ppermute | solution.py:42
  598.7 32.5 %collective-permute-start.19 = (bf16[4,4,176,128]{3,2,1,0:T(8,128)(2,1)}, bf16[4,4,176,128]{3,2,1,0:T(8,128)(2,1)S(1)}, u32[]{:S(2)}, u32[]{:S(2)}) collective-permute-start(bf16[4,4,176,128]{3,2,1,0:T(8,128)(2,1)} %get-tuple-element.99), channel_id=1, source_target_pairs={{0,4},{2,6},{4,0},{6,2},{1,5},{3,7},{5,1},{7,3},{8,12},{10,14},{12... | collective-permute-start | bytes 2162696 | tf_op jit(solution)/shard_map/ppermute | solution.py:42
  599.8 28.9 %collective-permute-start.23 = (bf16[4,4,160,128]{3,2,1,0:T(8,128)(2,1)}, bf16[4,4,160,128]{3,2,1,0:T(8,128)(2,1)S(1)}, u32[]{:S(2)}, u32[]{:S(2)}) collective-permute-start(bf16[4,4,160,128]{3,2,1,0:T(8,128)(2,1)} %get-tuple-element.103), channel_id=1, source_target_pairs={{0,24},{8,0},{16,8},{24,16},{1,25},{9,1},{17,9},{25,17},{2,26},{10... | collective-permute-start | bytes 1966088 | tf_op jit(solution)/shard_map/ppermute | solution.py:42
  602.9 28.3 %collective-permute-start.24 = (bf16[4,4,160,128]{3,2,1,0:T(8,128)(2,1)}, bf16[4,4,160,128]{3,2,1,0:T(8,128)(2,1)S(1)}, u32[]{:S(2)}, u32[]{:S(2)}) collective-permute-start(bf16[4,4,160,128]{3,2,1,0:T(8,128)(2,1)} %get-tuple-element.104), channel_id=1, source_target_pairs={{0,8},{8,16},{16,24},{24,0},{1,9},{9,17},{17,25},{25,1},{2,10},{10... | collective-permute-start | bytes 1966088 | tf_op jit(solution)/shard_map/ppermute | solution.py:42
  602.9 31.5 %collective-permute-start.20 = (bf16[4,4,176,128]{3,2,1,0:T(8,128)(2,1)}, bf16[4,4,176,128]{3,2,1,0:T(8,128)(2,1)S(1)}, u32[]{:S(2)}, u32[]{:S(2)}) collective-permute-start(bf16[4,4,176,128]{3,2,1,0:T(8,128)(2,1)} %get-tuple-element.100), channel_id=1, source_target_pairs={{0,96},{32,0},{64,32},{96,64},{1,97},{33,1},{65,33},{97,65},{2,98}... | collective-permute-start | bytes 2162696 | tf_op jit(solution)/shard_map/ppermute | solution.py:42
  690.2 37.0 %collective-permute-start.32 = (bf16[4,4,208,128]{3,2,1,0:T(8,128)(2,1)}, bf16[4,4,208,128]{3,2,1,0:T(8,128)(2,1)S(1)}, u32[]{:S(2)}, u32[]{:S(2)}) collective-permute-start(bf16[4,4,208,128]{3,2,1,0:T(8,128)(2,1)} %get-tuple-element.118), channel_id=1, source_target_pairs={{0,96},{32,0},{64,32},{96,64},{1,97},{33,1},{65,33},{97,65},{2,98}... | collective-permute-start | bytes 2555912 | tf_op jit(solution)/shard_map/ppermute | solution.py:42
  693.6 35.6 %collective-permute-start.33 = (bf16[4,4,208,128]{3,2,1,0:T(8,128)(2,1)}, bf16[4,4,208,128]{3,2,1,0:T(8,128)(2,1)S(1)}, u32[]{:S(2)}, u32[]{:S(2)}) collective-permute-start(bf16[4,4,208,128]{3,2,1,0:T(8,128)(2,1)} %get-tuple-element.119), channel_id=1, source_target_pairs={{0,32},{32,64},{64,96},{96,0},{1,33},{33,65},{65,97},{97,1},{2,34}... | collective-permute-start | bytes 2555912 | tf_op jit(solution)/shard_map/ppermute | solution.py:42
  693.7 62.3 %collective-permute-start.29 = (bf16[4,4,224,128]{3,2,1,0:T(8,128)(2,1)}, bf16[4,4,224,128]{3,2,1,0:T(8,128)(2,1)S(1)}, u32[]{:S(2)}, u32[]{:S(2)}) collective-permute-start(bf16[4,4,224,128]{3,2,1,0:T(8,128)(2,1)} %get-tuple-element.115), channel_id=1, source_target_pairs={{0,6},{2,0},{4,2},{6,4},{1,7},{3,1},{5,3},{7,5},{8,14},{10,8},{12,... | collective-permute-start | bytes 2752520 | tf_op jit(solution)/shard_map/ppermute | solution.py:42
  711.1 44.8 %collective-permute-start.30 = (bf16[4,4,224,128]{3,2,1,0:T(8,128)(2,1)}, bf16[4,4,224,128]{3,2,1,0:T(8,128)(2,1)S(1)}, u32[]{:S(2)}, u32[]{:S(2)}) collective-permute-start(bf16[4,4,224,128]{3,2,1,0:T(8,128)(2,1)} %get-tuple-element.116), channel_id=1, source_target_pairs={{0,2},{2,4},{4,6},{6,0},{1,3},{3,5},{5,7},{7,1},{8,10},{10,12},{12... | collective-permute-start | bytes 2752520 | tf_op jit(solution)/shard_map/ppermute | solution.py:42
  713.1 42.9 %collective-permute-start.31 = (bf16[4,4,224,128]{3,2,1,0:T(8,128)(2,1)}, bf16[4,4,224,128]{3,2,1,0:T(8,128)(2,1)}, u32[]{:S(2)}, u32[]{:S(2)}) collective-permute-start(bf16[4,4,224,128]{3,2,1,0:T(8,128)(2,1)} %get-tuple-element.117), channel_id=1, source_target_pairs={{0,4},{2,6},{4,0},{6,2},{1,5},{3,7},{5,1},{7,3},{8,12},{10,14},{12... | collective-permute-start | bytes 2752520 | tf_op jit(solution)/shard_map/ppermute | solution.py:42
  727.2 24.6 %collective-permute-start.34 = (bf16[4,4,208,128]{3,2,1,0:T(8,128)(2,1)}, bf16[4,4,208,128]{3,2,1,0:T(8,128)(2,1)}, u32[]{:S(2)}, u32[]{:S(2)}) collective-permute-start(bf16[4,4,208,128]{3,2,1,0:T(8,128)(2,1)} %get-tuple-element.120), channel_id=1, source_target_pairs={{0,24},{8,0},{16,8},{24,16},{1,25},{9,1},{17,9},{25,17},{2,26},{10... | collective-permute-start | bytes 2555912 | tf_op jit(solution)/shard_map/ppermute | solution.py:42
  730.2 25.8 %collective-permute-start.35 = (bf16[4,4,208,128]{3,2,1,0:T(8,128)(2,1)}, bf16[4,4,208,128]{3,2,1,0:T(8,128)(2,1)}, u32[]{:S(2)}, u32[]{:S(2)}) collective-permute-start(bf16[4,4,208,128]{3,2,1,0:T(8,128)(2,1)} %get-tuple-element.121), channel_id=1, source_target_pairs={{0,8},{8,16},{16,24},{24,0},{1,9},{9,17},{17,25},{25,1},{2,10},{10... | collective-permute-start | bytes 2555912 | tf_op jit(solution)/shard_map/ppermute | solution.py:42
  731.5 75.7 %all-to-all-start = ((bf16[64,24,512]{2,1,0:T(8,128)(2,1)}), bf16[64,24,512]{2,1,0:T(8,128)(2,1)S(1)}, u32[]{:S(2)}, u32[]{:S(2)}) async-start(bf16[64,24,512]{2,1,0:T(8,128)(2,1)} %pad_maximum_fusion), calls=%async_computation | async-start | bytes 3145728 | tf_op jit(solution)/shard_map/all_to_all | solution.py:373
  (84 other events, 1548.1 us)
Sparse Core Ops, SparseCore 0:
  10.9 84.6 all-gather.1

commit v2 on v1

v2 whole, which is shorter than its diff:
```python
import math

import jax
import jax.numpy as jnp
from jax import lax
from jax.experimental import pallas as pl
from jax.experimental.pallas import tpu as pltpu
from jax.sharding import Mesh, PartitionSpec as P

FF = 25600
KS = 512
RANK = 256
ROWS = 80
COLS = 400
NL = 2
N = 64

bf16 = jnp.bfloat16
f32 = jnp.float32
highest = lax.Precision.HIGHEST
AX = ("z", "x", "y")
VMEM = 56 * 1024 * 1024

ORDERS = (("z", "x", "y"), ("x", "y", "z"), ("y", "z", "x"))
PANEL = (176, 176, 176)
BACK = (224, 224, 224)
ISSUE = ((0, 2), (1, 2), (2, 1), (2, 3), (0, 1), (0, 3), (1, 1), (1, 3), (2, 2))
HBM = pl.BlockSpec(memory_space=pl.ANY)
SMEM = pl.BlockSpec(memory_space=pltpu.SMEM)
INNER = pl.BlockSpec(memory_space=pltpu.VMEM)


def rest_axes(t, stage):
    return [a for a in AX if a in ORDERS[t][stage:]]


def shifted(x, axis, k):
    return lax.ppermute(x, axis, [(s, (s - k) % 4) for s in range(4)])


def params():
    return pltpu.CompilerParams(vmem_limit_bytes=VMEM)


def cost(nbytes, flops=0):
    return pl.CostEstimate(flops=flops, bytes_accessed=nbytes, transcendentals=0)


def run_copies(copies):
    for c in copies:
        c.start()
    for c in copies:
        c.wait()


def pass_on(loads, scr, outs, sem_out):
    for group in loads:
        for c in group:
            c.start()
    stores = []
    for at, group in enumerate(loads):
        for c in group:
            c.wait()
        stores.append(pltpu.make_async_copy(scr[at], outs[at], sem_out.at[at]))
        stores[-1].start()
    for c in stores:
        c.wait()


def pack_kernel(pos_ref, g_ref, *refs):
    outs, scr, sem = refs[:12], refs[12:15], refs[15]
    g = pl.program_id(0)
    here = [pos_ref[i] for i in range(3)]
    for j in range(8):
        there = [g // 2, 2 * lax.rem(g, 2) + j // 4, j % 4]
        tails = []
        for l in range(NL):
            rest = g_ref[l, :, COLS * j + 384 : COLS * (j + 1)]
            tails.append(
                jnp.concatenate(
                    [rest[16 * i : 16 * i + 16] for i in range(5)] + [jnp.zeros((16, 48), bf16)], axis=1
                )
            )
        for t in range(3):
            first = AX.index(ORDERS[t][0])
            other = [i for i in range(3) if i != first]
            k = lax.rem(here[first] - there[first] + 4, 4)
            at = there[other[0]] * 4 + there[other[1]]
            for l in range(NL):
                scr[t][k, at, pl.ds(ROWS * l, ROWS), :] = g_ref[
                    l, :, COLS * j + 128 * t : COLS * j + 128 * (t + 1)
                ]
            scr[t][k, at, pl.ds(160, 16), :] = tails[t] if t < 2 else jnp.zeros((16, 128), bf16)

    @pl.when(g == 7)
    def _():
        run_copies(
            [
                pltpu.make_async_copy(scr[t].at[k], outs[4 * t + k], sem.at[4 * t + k])
                for t in range(3)
                for k in range(4)
            ]
        )


def pack(pos, g):
    outs = pl.pallas_call(
        pack_kernel,
        grid=(8,),
        in_specs=[SMEM, pl.BlockSpec((NL, ROWS, 8 * COLS), lambda i: (0, 0, i))],
        out_specs=[HBM] * 12,
        out_shape=[jax.ShapeDtypeStruct((16, n, 128), bf16) for n in PANEL for _ in range(4)],
        scratch_shapes=[pltpu.VMEM((4, 16, n, 128), bf16) for n in PANEL] + [pltpu.SemaphoreType.DMA((12,))],
        compiler_params=params(),
        cost_estimate=cost(17_000_000),
    )(pos, g)
    return [[o.reshape((4, 4) + o.shape[1:]) for o in outs[4 * t : 4 * t + 4]] for t in range(3)]


def permute_stage(bufs, stage):
    got = [[b[0], None, None, None] for b in bufs]
    for t, k in ISSUE:
        got[t][k] = shifted(bufs[t][k], ORDERS[t][stage], k)
    return got


def flat(got, stage):
    return [got[t][k] for t, k in ISSUE] + [got[t][0] for t in range(3)]


def unflat(refs, stage):
    got = [[None] * 4 for _ in range(3)]
    for (t, k), r in zip(ISSUE, refs[:9]):
        got[t][k] = r
    for t in range(3):
        got[t][0] = refs[9 + t]
    return got


def second_kernel(pos_ref, *refs):
    first = unflat(refs[:12], 0)
    outs, scr, sem, sem_out = refs[12:21], refs[21:30], refs[30], refs[31]
    here = [pos_ref[i] for i in range(3)]
    loads = [[] for _ in outs]
    for at, (t, k) in enumerate(ISSUE):
        axis = ORDERS[t][1]
        place = lax.rem(here[AX.index(axis)] + 4 - k, 4)
        for k1 in range(4):
            src = first[t][k1]
            src = src.at[place] if rest_axes(t, 1).index(axis) == 0 else src.at[:, place]
            loads[at].append(pltpu.make_async_copy(src, scr[at].at[k1], sem.at[4 * at + k1]))
    pass_on(loads, scr, outs, sem_out)


def second(pos, got):
    outs = pl.pallas_call(
        second_kernel,
        in_specs=[SMEM] + [HBM] * 12,
        out_specs=[HBM] * 9,
        out_shape=[jax.ShapeDtypeStruct((4, 4, PANEL[t], 128), bf16) for t, _ in ISSUE],
        scratch_shapes=[pltpu.VMEM((4, 4, PANEL[t], 128), bf16) for t, _ in ISSUE]
        + [pltpu.SemaphoreType.DMA((36,)), pltpu.SemaphoreType.DMA((9,))],
        compiler_params=params(),
        cost_estimate=cost(13_000_000),
    )(pos, *flat(got, 0))
    bufs = [[None] * 4 for _ in range(3)]
    for (t, k), o in zip(ISSUE, outs):
        bufs[t][k] = o
    return bufs


def third_kernel(pos_ref, *refs):
    first = unflat(refs[:12], 0)
    later = [[None] * 4 for _ in range(3)]
    for (t, k), r in zip(ISSUE, refs[12:21]):
        later[t][k] = r
    outs, scr, sem, sem_out = refs[21:33], refs[33:45], refs[45], refs[46]
    here = [pos_ref[i] for i in range(3)]
    loads = [[] for _ in outs]
    for at, (t, k) in enumerate(ISSUE + ((0, 0), (1, 0), (2, 0))):
        axis2, axis3 = ORDERS[t][1], ORDERS[t][2]
        own = here[AX.index(axis2)]
        place = lax.rem(here[AX.index(axis3)] + 4 - k, 4)
        for k1 in range(4):
            src = first[t][k1]
            src = src.at[own, place] if rest_axes(t, 1).index(axis2) == 0 else src.at[place, own]
            loads[at].append(pltpu.make_async_copy(src, scr[at].at[0, k1], sem.at[7 * at + k1]))
        for k2 in range(1, 4):
            loads[at].append(
                pltpu.make_async_copy(later[t][k2].at[:, place], scr[at].at[k2], sem.at[7 * at + 3 + k2])
            )
    pass_on(loads, scr, outs, sem_out)


def third(pos, got1, got2):
    order = ISSUE + ((0, 0), (1, 0), (2, 0))
    outs = pl.pallas_call(
        third_kernel,
        in_specs=[SMEM] + [HBM] * 21,
        out_specs=[HBM] * 12,
        out_shape=[jax.ShapeDtypeStruct((4, 4, PANEL[t], 128), bf16) for t, _ in order],
        scratch_shapes=[pltpu.VMEM((4, 4, PANEL[t], 128), bf16) for t, _ in order]
        + [pltpu.SemaphoreType.DMA((84,)), pltpu.SemaphoreType.DMA((12,))],
        compiler_params=params(),
        cost_estimate=cost(17_000_000),
    )(pos, *flat(got1, 0), *[got2[t][k] for t, k in ISSUE])
    bufs = [[None] * 4 for _ in range(3)]
    for (t, k), o in zip(order, outs):
        bufs[t][k] = o
    return bufs


def panel_kernel(pos_ref, *refs):
    got = unflat(refs[:12], 2)
    s_ref, old_ref, pick_ref = refs[12:15]
    back = refs[15:27]
    sk_ref, send_ref = refs[27:29]
    scr_in, scr_out = refs[29:32], refs[32:35]
    x_ref, s_vmem, acc_ref, sem, sem_s, sem_out = refs[35:]
    here = [pos_ref[i] for i in range(3)]

    loads = [
        [pltpu.make_async_copy(got[t][k], scr_in[t].at[k], sem.at[4 * t + k]) for k in range(4)] for t in range(3)
    ]
    load_s = pltpu.make_async_copy(s_ref, s_vmem, sem_s)
    for c in loads[0] + loads[1] + loads[2] + [load_s]:
        c.start()
    acc_ref[...] = jnp.zeros_like(acc_ref)

    for t in range(3):
        for c in loads[t]:
            c.wait()

        def lay(src, _):
            there = [src // 16, lax.rem(src // 4, 4), lax.rem(src, 4)]
            k = {a: lax.rem(there[i] + 4 - here[i], 4) for i, a in enumerate(AX)}
            row = pl.multiple_of(src * ROWS, 16)
            o1, o2, o3 = ORDERS[t]
            block = scr_in[t].at[k[o3], k[o2], k[o1]]
            for l in range(NL):
                x_ref[pl.ds(row, ROWS), 512 * l + 128 * t : 512 * l + 128 * (t + 1)] = block[
                    ROWS * l : ROWS * (l + 1), :
                ]
            if t < 2:
                tail = block[160:176, :].astype(f32)
                for i in range(5):
                    turned = tail if i == 0 else pltpu.roll(tail, 128 - 16 * i, 1)
                    x_ref[pl.ds(pl.multiple_of(row + 16 * i, 16), 16), 512 * t + 384 : 512 * t + 512] = (
                        turned.astype(bf16)
                    )
            return 0

        lax.fori_loop(0, N, lay, 0)
    load_s.wait()

    def add(i, _):
        rows = pl.ds(pl.multiple_of(i * 640, 640), 640)
        acc_ref[...] += lax.dot_general(
            s_vmem[rows, :], x_ref[rows, :], (((0,), (0,)), ((), ())), preferred_element_type=f32
        )
        return 0

    lax.fori_loop(0, 8, add, 0)
    inside = lax.broadcasted_iota(jnp.int32, (KS, 512), 1) < COLS
    sums, pieces = [], []
    for l in range(NL):
        wide = jnp.where(inside, acc_ref[:, 512 * l : 512 * (l + 1)], 0.0)
        skt = wide.astype(bf16)
        sk = jnp.transpose(skt.astype(f32), (1, 0))
        diag = jnp.sum(sk * sk, axis=0, keepdims=True)
        high = diag.astype(bf16).astype(f32)
        for d in (high, diag - high):
            pieces += [d[:, 128 * i : 128 * (i + 1)] for i in range(4)]
        sk_ref[l] = sk.astype(bf16)
        chosen = jnp.dot(sk_ref[l], pick_ref[l], preferred_element_type=f32).astype(bf16)
        left = jnp.dot(skt, chosen, preferred_element_type=f32)
        right = jnp.dot(skt[:, 0:COLS], old_ref[l], preferred_element_type=f32)
        sums.append(jnp.concatenate([left, right], 1).reshape(N, 8, KS))
    send_ref[:, :, 0:KS] = jnp.concatenate(sums, 1).astype(bf16)
    send_ref[:, :, KS : KS + 128] = jnp.broadcast_to(
        jnp.concatenate(pieces, 0).astype(bf16)[None], (N, 16, 128)
    )

    stores = []

    def store(t, k):
        src = scr_out[t]
        src = (src.at[k], src.at[:, k], src.at[:, :, k])[AX.index(ORDERS[t][0])]
        stores.append(pltpu.make_async_copy(src, back[4 * t + k], sem_out.at[4 * t + k]))
        stores[-1].start()

    for kz in range(4):
        z = lax.rem(here[0] + kz, 4)

        def out(kx, _):
            x = lax.rem(here[1] + kx, 4)
            rows = pl.ds(pl.multiple_of((4 * z + x) * 4 * ROWS, 64), 4 * ROWS)
            for l in range(NL):
                part = jnp.dot(
                    x_ref[rows, 512 * l : 512 * (l + 1)], sk_ref[l], preferred_element_type=f32
                ).astype(bf16)
                for y in range(4):
                    ky = lax.rem(y + 4 - here[2], 4)
                    one = part[ROWS * y : ROWS * (y + 1)]
                    for t in range(3):
                        scr_out[t][kz, kx, ky, ROWS * l : ROWS * (l + 1), :] = one[:, 128 * t : 128 * (t + 1)]
                    last = one[:, 384:512]
                    if l == 0:
                        scr_out[0][kz, kx, ky, 160:208, :] = last[0:48]
                        scr_out[1][kz, kx, ky, 160:192, :] = last[48:80]
                    else:
                        scr_out[1][kz, kx, ky, 192:208, :] = last[0:16]
                        scr_out[2][kz, kx, ky, 160:224, :] = last[16:80]
            return 0

        lax.fori_loop(0, 4, out, 0)
        store(0, kz)
    for t in (1, 2):
        for k in range(4):
            store(t, k)
    for c in stores:
        c.wait()


def panel_products(pos, got, s, old, picker):
    outs = pl.pallas_call(
        panel_kernel,
        in_specs=[SMEM] + [HBM] * 13 + [INNER] * 2,
        out_specs=[HBM] * 12 + [INNER] * 2,
        out_shape=[jax.ShapeDtypeStruct((4, 4, n, 128), bf16) for n in BACK for _ in range(4)]
        + [jax.ShapeDtypeStruct((NL, KS, KS), bf16), jax.ShapeDtypeStruct((N, 16, KS + 128), bf16)],
        scratch_shapes=[pltpu.VMEM((4, 4, 4, n, 128), bf16) for n in PANEL]
        + [pltpu.VMEM((4, 4, 4, n, 128), bf16) for n in BACK]
        + [
            pltpu.VMEM((N * ROWS, NL * 512), bf16),
            pltpu.VMEM((N * ROWS, KS), bf16),
            pltpu.VMEM((KS, NL * 512), f32),
            pltpu.SemaphoreType.DMA((12,)),
            pltpu.SemaphoreType.DMA,
            pltpu.SemaphoreType.DMA((12,)),
        ],
        compiler_params=params(),
        cost_estimate=cost(26_000_000, 11_000_000_000),
    )(pos, *flat(got, 2), s, old, picker)
    return [list(outs[4 * t : 4 * t + 4]) for t in range(3)], outs[12], outs[13]


def owner_kernel(me_ref, got_ref, ranks_ref, mine_ref, scores_ref):
    total = jnp.sum(got_ref[...].astype(f32), axis=0)
    row = me_ref[0] * 8 + lax.broadcasted_iota(jnp.int32, (8, 128), 0)
    lane = lax.broadcasted_iota(jnp.int32, (8, 128), 1)
    my_rows = me_ref[0] * 8 + lax.broadcasted_iota(jnp.int32, (8, RANK), 0)
    owned, scores = [], 0.0
    for l in range(NL):
        diag = total[8 * l : 8 * l + 4, KS:] + total[8 * l + 4 : 8 * l + 8, KS:]
        scores = scores + diag
        trace = jnp.sum(jnp.sum(diag, axis=1, keepdims=True), axis=0, keepdims=True)
        mine = jnp.zeros((8, 128), f32)
        for c in range(4):
            mine = mine + jnp.where(lane + 128 * c == row, diag[c : c + 1, :], 0.0)
        my_diag = jnp.sum(mine, axis=1, keepdims=True)
        scale = 0.5 * KS / trace
        rms = jnp.sqrt(trace / (FF * KS))
        gram = total[8 * l : 8 * l + 8, 0:RANK]
        corrected = jnp.where(my_rows == ranks_ref[l : l + 1, :], 1.5 - scale * my_diag, -scale * gram)
        owned.append(jnp.concatenate([corrected / rms, total[8 * l : 8 * l + 8, RANK:KS]], 1))
    mine_ref[...] = jnp.broadcast_to(jnp.concatenate(owned, 0).astype(bf16)[None], (N, 16, KS))
    scores_ref[...] = scores / FF


def owner_rows(me, got, ranks):
    return pl.pallas_call(
        owner_kernel,
        in_specs=[SMEM, INNER, INNER],
        out_specs=[INNER, INNER],
        out_shape=[jax.ShapeDtypeStruct((N, 16, KS), bf16), jax.ShapeDtypeStruct((4, 128), f32)],
        compiler_params=params(),
        cost_estimate=cost(2_500_000),
    )(me, got, ranks)


def moments_kernel(rows_ref, sk_ref, one_ref, two_ref, basis_ref, first_ref, second_ref, factor_ref):
    rows = rows_ref[...].astype(f32)
    for l in range(NL):
        both = rows[:, 8 * l : 8 * l + 8, :].reshape(KS, KS).astype(bf16)
        factor, inner = both[:, :RANK], both[:, RANK:]
        factor_ref[l] = factor
        basis_ref[l] = jnp.dot(sk_ref[l, 0:COLS, :], factor, preferred_element_type=f32).astype(bf16)
        correlation = lax.dot_general(
            inner, factor, (((0,), (0,)), ((), ())), preferred_element_type=f32
        ) / math.sqrt(FF * RANK)
        first_ref[l] = jnp.dot(one_ref[l], correlation, precision=highest, preferred_element_type=f32)
        second_ref[l] = jnp.dot(
            two_ref[l], correlation * correlation, precision=highest, preferred_element_type=f32
        )


def moments(rows, sk, one, two):
    return pl.pallas_call(
        moments_kernel,
        in_specs=[INNER] * 4,
        out_specs=[INNER] * 4,
        out_shape=[
            jax.ShapeDtypeStruct((NL, COLS, RANK), bf16),
            jax.ShapeDtypeStruct((NL, ROWS, RANK), f32),
            jax.ShapeDtypeStruct((NL, ROWS, RANK), f32),
            jax.ShapeDtypeStruct((NL, KS, RANK), bf16),
        ],
        compiler_params=params(),
        cost_estimate=cost(4_000_000, 500_000_000),
    )(rows, sk, one, two)


def project_kernel(*refs):
    got = unflat(refs[:12], 2)
    factor_ref, out_ref = refs[12:]
    t0, t1, t2 = [sum(got[t][k][...].astype(f32) for k in range(4)) for t in range(3)]
    last = (jnp.concatenate([t0[160:208], t1[160:192]], 0), jnp.concatenate([t1[192:208], t2[160:224]], 0))
    for l in range(NL):
        rows = slice(ROWS * l, ROWS * (l + 1))
        t_rows = jnp.concatenate([t0[rows], t1[rows], t2[rows], last[l]], 1)
        out_ref[l] = (
            jnp.dot(t_rows, factor_ref[l].astype(f32), precision=highest, preferred_element_type=f32)
            / math.sqrt(FF)
        ).astype(bf16)


def project(got, factor):
    return pl.pallas_call(
        project_kernel,
        in_specs=[INNER] * 13,
        out_specs=INNER,
        out_shape=jax.ShapeDtypeStruct((NL, ROWS, RANK), bf16),
        compiler_params=params(),
        cost_estimate=cost(2_000_000, 100_000_000),
    )(*flat(got, 2), factor)


def reduce_kernel(stage, *refs):
    got = unflat(refs[:12], stage)
    outs = refs[12:]
    for t in range(3):
        axis = ORDERS[t][stage + 1]
        dim = rest_axes(t, stage + 1).index(axis)
        for k in range(4):
            out = outs[4 * t + k]
            if stage == 0:
                for i in range(4):
                    at = (k, i) if dim == 0 else (i, k)
                    out[i] = sum(got[t][j][at].astype(f32) for j in range(4)).astype(bf16)
            else:
                out[...] = sum(got[t][j][k].astype(f32) for j in range(4)).astype(bf16)


def reduce_stage(got, stage):
    lead = (4,) if stage == 0 else ()
    outs = pl.pallas_call(
        lambda *refs: reduce_kernel(stage, *refs),
        in_specs=[INNER] * 12,
        out_specs=[INNER] * 12,
        out_shape=[jax.ShapeDtypeStruct(lead + (n, 128), bf16) for n in BACK for _ in range(4)],
        compiler_params=params(),
        cost_estimate=cost(13_000_000 if stage == 0 else 3_300_000),
    )(*flat(got, stage))
    return [list(outs[4 * t : 4 * t + 4]) for t in range(3)]


def shift_back(bufs, stage):
    got = [[b[0], None, None, None] for b in bufs]
    for t, k in ISSUE:
        got[t][k] = shifted(bufs[t][4 - k], ORDERS[t][stage], k)
    return got


def shards(gradients, sketch, rank_lists, old_basis, first_moment, second_moment):
    full_sketch = lax.all_gather(sketch, AX, axis=0, tiled=True)
    pos = jnp.stack([lax.axis_index(a) for a in AX]).astype(jnp.int32)
    got1 = permute_stage(pack(pos, gradients), 0)
    got2 = permute_stage(second(pos, got1), 1)
    got3 = permute_stage(third(pos, got1, got2), 2)
    picker = (lax.broadcasted_iota(jnp.int32, (NL, KS, RANK), 1) == rank_lists[:, None, :]).astype(bf16)
    parts, sketched, send = panel_products(pos, got3, full_sketch, old_basis, picker)
    got = lax.all_to_all(send, AX, 0, 0, tiled=True)
    me = (16 * pos[0] + 4 * pos[1] + pos[2])[None]
    mine, scores = owner_rows(me, got, rank_lists)
    everyone = lax.all_to_all(mine, AX, 0, 0, tiled=True)
    basis, first, second_out, factor = moments(everyone, sketched, first_moment, second_moment)
    back = shift_back(parts, 0)
    back = shift_back(reduce_stage(back, 0), 1)
    back = shift_back(reduce_stage(back, 1), 2)
    projected = project(back, factor)
    return basis, projected, first, second_out, lax.psum(scores.reshape(KS), "layer")


def solution(mesh):
    cube = Mesh(mesh.devices.reshape(4, 4, 4, 2), AX + ("layer",))
    rows = P("layer", AX, None)
    return jax.shard_map(
        shards,
        mesh=cube,
        in_specs=(rows, P(AX, None), P("layer", None), rows, rows, rows),
        out_specs=(rows, rows, rows, rows, P()),
        check_vma=False,
    )
```

time: 849 us -> 341 us (0.40)
  Pallas kernels: 505 us -> 81.4 us
  waiting for transfers between devices: 194 us -> 131 us
    pallas_call x1, Pallas kernels: 257 us -> 7.97 us  [third(): pl.pallas_call(third_kernel, in_specs=[SMEM] + [HBM] * 21, out_specs=[HBM...]
    pallas_call x1, Pallas kernels: 193 us -> 6.62 us  [second(): pl.pallas_call(second_kernel, in_specs=[SMEM] + [HBM] * 12, out_specs=[HB...]
    ppermute x54, waiting for transfers between devices: 193 us -> 128 us  [shifted(): return lax.ppermute(x, axis, [(s, (s - k) % 4) for s in range(4)])]
    pallas_call x0 -> x3, Pallas kernels: none -> 9.09 us  [the longest x1 3.62 us: moments(): pl.pallas_call(moments_kernel, in_specs=[INNER] * 4, out_specs=[INNER] *...]
  transfers between devices with their start and end apart: 57 -> 57, of which waited for: 23 -> 29; matrix products, arithmetic and copies ran while one was open for 1% -> 0% of each run, Pallas kernels for 55% -> 12%
where the time goes in v2:
time: 341 us; the launch traced here: 339 us
  waiting for transfers between devices  131 us (38%)
  starting transfers between devices  102 us (30%)
  Pallas kernels  81.4 us (24%)
  between operations  14.5 us (4%)
  local copies, waits for them, and re-layouts  5.13 us (2%)
    ppermute x54, waiting for transfers between devices, shifted(): return lax.ppermute(x, axis, [(s, (s - k) % 4) for s in range(4)])  128 us
    ppermute x54, starting transfers between devices, shifted(): return lax.ppermute(x, axis, [(s, (s - k) % 4) for s in range(4)])  81 us
    pallas_call x1, Pallas kernels, panel_products(): pl.pallas_call(panel_kernel, in_specs=[SMEM] + [HBM] * 13 + [INNER] * 2,...  37.1 us
    all_to_all x1, starting transfers between devices, shards(): everyone = lax.all_to_all(mine, AX, 0, 0, tiled=True)  12.3 us
    pallas_call x1, Pallas kernels, pack(): pl.pallas_call(pack_kernel, grid=(8,), in_specs=[SMEM, pl.BlockSpec((NL,...  11.5 us
    pallas_call x2, Pallas kernels, reduce_stage(): pl.pallas_call(lambda *refs: reduce_kernel(stage, *refs), in_specs=[INNER...  9.07 us
    all_to_all x1, starting transfers between devices, shards(): got = lax.all_to_all(send, AX, 0, 0, tiled=True)  8.99 us
    pallas_call x1, Pallas kernels, third(): pl.pallas_call(third_kernel, in_specs=[SMEM] + [HBM] * 21, out_specs=[HBM...  7.97 us
  transfers between devices with their start and end apart: 57, of which 29 were waited for; matrix products, arithmetic and copies ran while one was open for 0% of the time, Pallas kernels for 12%

profile of v2, /device:TPU:0, one launch (start us, length us, event | category | flops | bytes accessed | tf_op | source)
XLA Modules:
  0.0 339.3 jit_solution(12896407011078456327)
XLA Ops:
  8.5 11.5 %shard_map.101 = (bf16[16,176,128]{2,1,0:T(8,128)(2,1)}, bf16[16,176,128]{2,1,0:T(8,128)(2,1)}, bf16[16,176,128]{2,1,0:T(8,128)(2,1)}, bf16[16,176,128]{2,1,0:T(...) custom-call(s32[3]{0:T(128)} %pad_add_fusion.pos_ref, ...), custom_call_target="tpu_custom_call" | custom-call | bytes 17000000 | tf_op jit(solution)/shard_map/pallas_call | solution.py:107
  20.0 4.0 %collective-permute-start = (bf16[4,4,176,128]{3,2,1,0:T(8,128)(2,1)}, bf16[4,4,176,128]{3,2,1,0:T(8,128)(2,1)S(1)}, u32[]{:S(2)}, u32[]{:S(2)}) collective-permute-start(bf16[4,4,176,128]{3,2,1,0:T(8,128)(2,1)} %bitcast.32), channel_id=1, source_target_pairs={{0,64},{32,96},{64,0},{96,32},{1,65},{33,97},{65,1},{97,33},{2,66}... | collective-permute-start | bytes 2162696 | tf_op jit(solution)/shard_map/ppermute | solution.py:38
  30.8 10.4 %collective-permute-done.refs_0_ = bf16[4,4,176,128]{3,2,1,0:T(8,128)(2,1)S(1)} collective-permute-done((bf16[4,4,176,128]{3,2,1,0:T(8,128)(2,1)}, bf16[4,4,176,128]{3,2,1,0:T(8,128)(2,1)S(1)}, u32[]{:S(2)}, u32[]{:S(2)}) %collective-permute-start) | collective-permute-done | bytes 720928 | tf_op jit(solution)/shard_map/ppermute | solution.py:38
  50.1 8.6 %collective-permute-done.4.refs_4_ = bf16[4,4,176,128]{3,2,1,0:T(8,128)(2,1)S(1)} collective-permute-done((bf16[4,4,176,128]{3,2,1,0:T(8,128)(2,1)}, bf16[4,4,176,128]{3,2,1,0:T(8,128)(2,1)S(1)}, u32[]{:S(2)}, u32[]{:S(2)}) %collective-permute-start.4) | collective-permute-done | bytes 720928 | tf_op jit(solution)/shard_map/ppermute | solution.py:38
  63.6 3.3 collective-permute-done.7.refs_7_
  66.9 3.7 %collective-permute-done.8.refs_8_ = bf16[4,4,176,128]{3,2,1,0:T(8,128)(2,1)S(1)} collective-permute-done((bf16[4,4,176,128]{3,2,1,0:T(8,128)(2,1)}, bf16[4,4,176,128]{3,2,1,0:T(8,128)(2,1)S(1)}, u32[]{:S(2)}, u32[]{:S(2)}) %collective-permute-start.8) | collective-permute-done | bytes 720928 | tf_op jit(solution)/shard_map/ppermute | solution.py:38
  71.4 6.6 %shard_map.102 = (bf16[4,4,176,128]{3,2,1,0:T(8,128)(2,1)}, bf16[4,4,176,128]{3,2,1,0:T(8,128)(2,1)}, bf16[4,4,176,128]{3,2,1,0:T(8,128)(2,1)}, bf16[4,4,176,128...) custom-call(s32[3]{0:T(128)} %pad_add_fusion.pos_ref, ...), custom_call_target="tpu_custom_call" | custom-call | bytes 13000000 | tf_op jit(solution)/shard_map/pallas_call | solution.py:156
  84.3 26.9 %collective-permute-done.9.refs_12_ = bf16[4,4,176,128]{3,2,1,0:T(8,128)(2,1)S(1)} collective-permute-done((bf16[4,4,176,128]{3,2,1,0:T(8,128)(2,1)}, bf16[4,4,176,128]{3,2,1,0:T(8,128)(2,1)S(1)}, u32[]{:S(2)}, u32[]{:S(2)}) %collective-permute-start.9) | collective-permute-done | bytes 720928 | tf_op jit(solution)/shard_map/ppermute | solution.py:38
  114.8 7.5 %collective-permute-done.13.refs_16_ = bf16[4,4,176,128]{3,2,1,0:T(8,128)(2,1)S(1)} collective-permute-done((bf16[4,4,176,128]{3,2,1,0:T(8,128)(2,1)}, bf16[4,4,176,128]{3,2,1,0:T(8,128)(2,1)S(1)}, u32[]{:S(2)}, u32[]{:S(2)}) %collective-permute-start.13) | collective-permute-done | bytes 720928 | tf_op jit(solution)/shard_map/ppermute | solution.py:38
  129.0 8.0 %shard_map.103 = (bf16[4,4,176,128]{3,2,1,0:T(8,128)(2,1)}, bf16[4,4,176,128]{3,2,1,0:T(8,128)(2,1)}, bf16[4,4,176,128]{3,2,1,0:T(8,128)(2,1)}, bf16[4,4,176,128...) custom-call(s32[3]{0:T(128)} %pad_add_fusion.pos_ref, ...), custom_call_target="tpu_custom_call" | custom-call | bytes 17000000 | tf_op jit(solution)/shard_map/pallas_call | solution.py:197
  144.3 10.6 %collective-permute-done.18.refs_0_ = bf16[4,4,176,128]{3,2,1,0:T(8,128)(2,1)S(1)} collective-permute-done((bf16[4,4,176,128]{3,2,1,0:T(8,128)(2,1)}, bf16[4,4,176,128]{3,2,1,0:T(8,128)(2,1)S(1)}, u32[]{:S(2)}, u32[]{:S(2)}) %collective-permute-start.18) | collective-permute-done | bytes 720928 | tf_op jit(solution)/shard_map/ppermute | solution.py:38
  154.9 3.5 %collective-permute-start.23 = (bf16[4,4,176,128]{3,2,1,0:T(8,128)(2,1)}, bf16[4,4,176,128]{3,2,1,0:T(8,128)(2,1)}, u32[]{:S(2)}, u32[]{:S(2)}) collective-permute-start(bf16[4,4,176,128]{3,2,1,0:T(8,128)(2,1)} %get-tuple-element.108), channel_id=1, source_target_pairs={{0,2},{2,4},{4,6},{6,0},{1,3},{3,5},{5,7},{7,1},{8,10},{10,12},{12... | collective-permute-start | bytes 2162696 | tf_op jit(solution)/shard_map/ppermute | solution.py:38
  160.4 4.6 %collective-permute-done.21.refs_3_ = bf16[4,4,176,128]{3,2,1,0:T(8,128)(2,1)S(1)} collective-permute-done((bf16[4,4,176,128]{3,2,1,0:T(8,128)(2,1)}, bf16[4,4,176,128]{3,2,1,0:T(8,128)(2,1)S(1)}, u32[]{:S(2)}, u32[]{:S(2)}) %collective-permute-start.21) | collective-permute-done | bytes 720928 | tf_op jit(solution)/shard_map/ppermute | solution.py:38
  171.5 6.6 %collective-permute-done.26.refs_8_ = bf16[4,4,176,128]{3,2,1,0:T(8,128)(2,1)} collective-permute-done((bf16[4,4,176,128]{3,2,1,0:T(8,128)(2,1)}, bf16[4,4,176,128]{3,2,1,0:T(8,128)(2,1)}, u32[]{:S(2)}, u32[]{:S(2)}) %collective-permute-start.26) | collective-permute-done | bytes 720928 | tf_op jit(solution)/shard_map/ppermute | solution.py:38
  178.1 37.1 %shard_map.104 = (bf16[4,4,224,128]{3,2,1,0:T(8,128)(2,1)}, bf16[4,4,224,128]{3,2,1,0:T(8,128)(2,1)}, bf16[4,4,224,128]{3,2,1,0:T(8,128)(2,1)}, bf16[4,4,224,128...) custom-call(s32[3]{0:T(128)} %pad_add_fusion.pos_ref, ...), custom_call_target="tpu_custom_call" | custom-call | flops 11000000512 | bytes 26000000 | tf_op jit(solution)/shard_map/pallas_call | solution.py:326
  218.4 9.0 %all-to-all-start = ((bf16[64,16,640]{2,1,0:T(8,128)(2,1)}), bf16[64,16,640]{2,1,0:T(8,128)(2,1)S(1)}, u32[]{:S(2)}, u32[]{:S(2)}) async-start(bf16[64,16,640]{2,1,0:T(8,128)(2,1)} %get-tuple-element.115), calls=%async_computation | async-start | bytes 2621440 | tf_op jit(solution)/shard_map/all_to_all | solution.py:483
  230.4 16.1 %collective-permute-done.27.refs_0_ = bf16[4,4,224,128]{3,2,1,0:T(8,128)(2,1)S(1)} collective-permute-done((bf16[4,4,224,128]{3,2,1,0:T(8,128)(2,1)}, bf16[4,4,224,128]{3,2,1,0:T(8,128)(2,1)S(1)}, u32[]{:S(2)}, u32[]{:S(2)}) %collective-permute-start.27) | collective-permute-done | bytes 917536 | tf_op jit(solution)/shard_map/ppermute | solution.py:38
  246.7 5.2 %collective-permute-start.34 = (bf16[4,4,224,128]{3,2,1,0:T(8,128)(2,1)}, bf16[4,4,224,128]{3,2,1,0:T(8,128)(2,1)}, u32[]{:S(2)}, u32[]{:S(2)}) collective-permute-start(bf16[4,4,224,128]{3,2,1,0:T(8,128)(2,1)} %get-tuple-element.126), channel_id=1, source_target_pairs={{0,8},{8,16},{16,24},{24,0},{1,9},{9,17},{17,25},{25,1},{2,10},{10... | collective-permute-start | bytes 2752520 | tf_op jit(solution)/shard_map/ppermute | solution.py:38
  258.3 12.3 %all-to-all-start.1 = ((bf16[64,16,512]{2,1,0:T(8,128)(2,1)}), bf16[64,16,512]{2,1,0:T(8,128)(2,1)S(1)}, u32[]{:S(2)}, u32[]{:S(2)}) async-start(bf16[64,16,512]{2,1,0:T(8,128)(2,1)} %get-tuple-element.116), calls=%async_computation.1 | async-start | bytes 2097152 | tf_op jit(solution)/shard_map/all_to_all | solution.py:486
  272.1 6.3 %shard_map.107 = (bf16[4,224,128]{2,1,0:T(8,128)(2,1)}, bf16[4,224,128]{2,1,0:T(8,128)(2,1)}, bf16[4,224,128]{2,1,0:T(8,128)(2,1)}, bf16[4,224,128]{2,1,0:T(8,12...) custom-call(bf16[4,4,224,128]{3,2,1,0:T(8,128)(2,1)} %copy-done.11, ...), custom_call_target="tpu_custom_call" | custom-call | bytes 13000000 | tf_op jit(solution)/shard_map/pallas_call | solution.py:457
  286.0 9.8 %collective-permute-start.40 = (bf16[4,224,128]{2,1,0:T(8,128)(2,1)}, bf16[4,224,128]{2,1,0:T(8,128)(2,1)S(1)}, u32[]{:S(2)}, u32[]{:S(2)}) collective-permute-start(bf16[4,224,128]{2,1,0:T(8,128)(2,1)} %get-tuple-element.135), channel_id=1, source_target_pairs={{0,24},{8,0},{16,8},{24,16},{1,25},{9,1},{17,9},{25,17},{2,26},{10... | collective-permute-start | bytes 688136 | tf_op jit(solution)/shard_map/ppermute | solution.py:38
  299.6 3.6 %collective-permute-done.41.refs_5_ = bf16[4,224,128]{2,1,0:T(8,128)(2,1)S(1)} collective-permute-done((bf16[4,224,128]{2,1,0:T(8,128)(2,1)}, bf16[4,224,128]{2,1,0:T(8,128)(2,1)S(1)}, u32[]{:S(2)}, u32[]{:S(2)}) %collective-permute-start.41) | collective-permute-done | bytes 229408 | tf_op jit(solution)/shard_map/ppermute | solution.py:38
  312.2 3.4 %collective-permute-start.47 = (bf16[224,128]{1,0:T(8,128)(2,1)}, bf16[224,128]{1,0:T(8,128)(2,1)S(1)}, u32[]{:S(2)}, u32[]{:S(2)}) collective-permute-start(bf16[224,128]{1,0:T(8,128)(2,1)} %get-tuple-element.145), channel_id=1, source_target_pairs={{0,24},{8,0},{16,8},{24,16},{1,25},{9,1},{17,9},{25,17},{2,26},{10... | collective-permute-start | bytes 172040 | tf_op jit(solution)/shard_map/ppermute | solution.py:38
  325.3 3.6 %shard_map.106 = (bf16[2,400,256]{2,1,0:T(8,128)(2,1)}, f32[2,80,256]{2,1,0:T(8,128)}, f32[2,80,256]{2,1,0:T(8,128)}, bf16[2,512,256]{2,1,0:T(8,128)(2,1)}) custom-call(bf16[64,16,512]{2,1,0:T(8,128)(2,1)} %copy-done.1, bf16[2,512,512]{2,1,0:T(8,128)(2,1)} %get-tuple-element.117.sk_ref, f32[2,80,256]{2,1,0:T(8,128)} %one_ref.1, f32[2,80,256]{2,1,0:T(8,128)} %two_ref.1), custom_call_target="tpu_custom_call" | custom-call | flops 500000000 | bytes 4000000 | tf_op jit(solution)/shard_map/pallas_call | solution.py:399
  (195 shorter events, 102.7 us)
Async XLA Ops:
  7.2 170.9 %all-gather.2.cloned.1.call-start = ((), (), s32[]{:S(2)}) async-start(), calls=%async_computation.2 | async-start | bytes 5324800 | tf_op jit(solution)/shard_map/all_gather | solution.py:476
  20.0 21.2 %collective-permute-start = (bf16[4,4,176,128]{3,2,1,0:T(8,128)(2,1)}, bf16[4,4,176,128]{3,2,1,0:T(8,128)(2,1)S(1)}, u32[]{:S(2)}, u32[]{:S(2)}) collective-permute-start(bf16[4,4,176,128]{3,2,1,0:T(8,128)(2,1)} %bitcast.32), channel_id=1, source_target_pairs={{0,64},{32,96},{64,0},{96,32},{1,65},{33,97},{65,1},{97,33},{2,66}... | collective-permute-start | bytes 2162696 | tf_op jit(solution)/shard_map/ppermute | solution.py:38
  24.1 20.2 %collective-permute-start.1 = (bf16[4,4,176,128]{3,2,1,0:T(8,128)(2,1)}, bf16[4,4,176,128]{3,2,1,0:T(8,128)(2,1)S(1)}, u32[]{:S(2)}, u32[]{:S(2)}) collective-permute-start(bf16[4,4,176,128]{3,2,1,0:T(8,128)(2,1)} %bitcast.31), channel_id=1, source_target_pairs={{0,16},{8,24},{16,0},{24,8},{1,17},{9,25},{17,1},{25,9},{2,18},{10... | collective-permute-start | bytes 2162696 | tf_op jit(solution)/shard_map/ppermute | solution.py:38
  30.1 28.5 %collective-permute-start.4 = (bf16[4,4,176,128]{3,2,1,0:T(8,128)(2,1)}, bf16[4,4,176,128]{3,2,1,0:T(8,128)(2,1)S(1)}, u32[]{:S(2)}, u32[]{:S(2)}) collective-permute-start(bf16[4,4,176,128]{3,2,1,0:T(8,128)(2,1)} %bitcast.28), channel_id=1, source_target_pairs={{0,96},{32,0},{64,32},{96,64},{1,97},{33,1},{65,33},{97,65},{2,98}... | collective-permute-start | bytes 2162696 | tf_op jit(solution)/shard_map/ppermute | solution.py:38
  46.8 20.1 %collective-permute-start.7 = (bf16[4,4,176,128]{3,2,1,0:T(8,128)(2,1)}, bf16[4,4,176,128]{3,2,1,0:T(8,128)(2,1)S(1)}, u32[]{:S(2)}, u32[]{:S(2)}) collective-permute-start(bf16[4,4,176,128]{3,2,1,0:T(8,128)(2,1)} %bitcast.25), channel_id=1, source_target_pairs={{0,8},{8,16},{16,24},{24,0},{1,9},{9,17},{17,25},{25,1},{2,10},{10... | collective-permute-start | bytes 2162696 | tf_op jit(solution)/shard_map/ppermute | solution.py:38
  49.0 21.6 %collective-permute-start.8 = (bf16[4,4,176,128]{3,2,1,0:T(8,128)(2,1)}, bf16[4,4,176,128]{3,2,1,0:T(8,128)(2,1)S(1)}, u32[]{:S(2)}, u32[]{:S(2)}) collective-permute-start(bf16[4,4,176,128]{3,2,1,0:T(8,128)(2,1)} %bitcast.24), channel_id=1, source_target_pairs={{0,4},{2,6},{4,0},{6,2},{1,5},{3,7},{5,1},{7,3},{8,12},{10,14},{12... | collective-permute-start | bytes 2162696 | tf_op jit(solution)/shard_map/ppermute | solution.py:38
  78.0 33.2 %collective-permute-start.9 = (bf16[4,4,176,128]{3,2,1,0:T(8,128)(2,1)}, bf16[4,4,176,128]{3,2,1,0:T(8,128)(2,1)S(1)}, u32[]{:S(2)}, u32[]{:S(2)}) collective-permute-start(bf16[4,4,176,128]{3,2,1,0:T(8,128)(2,1)} %get-tuple-element.94), channel_id=1, source_target_pairs={{0,16},{8,24},{16,0},{24,8},{1,17},{9,25},{17,1},{25,9},{2,18},{10... | collective-permute-start | bytes 2162696 | tf_op jit(solution)/shard_map/ppermute | solution.py:38
  78.5 32.7 %collective-permute-start.10 = (bf16[4,4,176,128]{3,2,1,0:T(8,128)(2,1)}, bf16[4,4,176,128]{3,2,1,0:T(8,128)(2,1)S(1)}, u32[]{:S(2)}, u32[]{:S(2)}) collective-permute-start(bf16[4,4,176,128]{3,2,1,0:T(8,128)(2,1)} %get-tuple-element.95), channel_id=1, source_target_pairs={{0,4},{2,6},{4,0},{6,2},{1,5},{3,7},{5,1},{7,3},{8,12},{10,14},{12... | collective-permute-start | bytes 2162696 | tf_op jit(solution)/shard_map/ppermute | solution.py:38
  81.2 30.7 %collective-permute-start.11 = (bf16[4,4,176,128]{3,2,1,0:T(8,128)(2,1)}, bf16[4,4,176,128]{3,2,1,0:T(8,128)(2,1)S(1)}, u32[]{:S(2)}, u32[]{:S(2)}) collective-permute-start(bf16[4,4,176,128]{3,2,1,0:T(8,128)(2,1)} %get-tuple-element.96), channel_id=1, source_target_pairs={{0,96},{32,0},{64,32},{96,64},{1,97},{33,1},{65,33},{97,65},{2,98}... | collective-permute-start | bytes 2162696 | tf_op jit(solution)/shard_map/ppermute | solution.py:38
  82.2 31.1 %collective-permute-start.12 = (bf16[4,4,176,128]{3,2,1,0:T(8,128)(2,1)}, bf16[4,4,176,128]{3,2,1,0:T(8,128)(2,1)S(1)}, u32[]{:S(2)}, u32[]{:S(2)}) collective-permute-start(bf16[4,4,176,128]{3,2,1,0:T(8,128)(2,1)} %get-tuple-element.97), channel_id=1, source_target_pairs={{0,32},{32,64},{64,96},{96,0},{1,33},{33,65},{65,97},{97,1},{2,34}... | collective-permute-start | bytes 2162696 | tf_op jit(solution)/shard_map/ppermute | solution.py:38
  83.3 39.0 %collective-permute-start.13 = (bf16[4,4,176,128]{3,2,1,0:T(8,128)(2,1)}, bf16[4,4,176,128]{3,2,1,0:T(8,128)(2,1)S(1)}, u32[]{:S(2)}, u32[]{:S(2)}) collective-permute-start(bf16[4,4,176,128]{3,2,1,0:T(8,128)(2,1)} %get-tuple-element.98), channel_id=1, source_target_pairs={{0,24},{8,0},{16,8},{24,16},{1,25},{9,1},{17,9},{25,17},{2,26},{10... | collective-permute-start | bytes 2162696 | tf_op jit(solution)/shard_map/ppermute | solution.py:38
  141.5 23.5 %collective-permute-start.21 = (bf16[4,4,176,128]{3,2,1,0:T(8,128)(2,1)}, bf16[4,4,176,128]{3,2,1,0:T(8,128)(2,1)S(1)}, u32[]{:S(2)}, u32[]{:S(2)}) collective-permute-start(bf16[4,4,176,128]{3,2,1,0:T(8,128)(2,1)} %get-tuple-element.106), channel_id=1, source_target_pairs={{0,8},{8,16},{16,24},{24,0},{1,9},{9,17},{17,25},{25,1},{2,10},{10... | collective-permute-start | bytes 2162696 | tf_op jit(solution)/shard_map/ppermute | solution.py:38
  141.5 25.0 %collective-permute-start.22 = (bf16[4,4,176,128]{3,2,1,0:T(8,128)(2,1)}, bf16[4,4,176,128]{3,2,1,0:T(8,128)(2,1)}, u32[]{:S(2)}, u32[]{:S(2)}) collective-permute-start(bf16[4,4,176,128]{3,2,1,0:T(8,128)(2,1)} %get-tuple-element.107), channel_id=1, source_target_pairs={{0,6},{2,0},{4,2},{6,4},{1,7},{3,1},{5,3},{7,5},{8,14},{10,8},{12,... | collective-permute-start | bytes 2162696 | tf_op jit(solution)/shard_map/ppermute | solution.py:38
  215.2 31.3 %collective-permute-start.27 = (bf16[4,4,224,128]{3,2,1,0:T(8,128)(2,1)}, bf16[4,4,224,128]{3,2,1,0:T(8,128)(2,1)S(1)}, u32[]{:S(2)}, u32[]{:S(2)}) collective-permute-start(bf16[4,4,224,128]{3,2,1,0:T(8,128)(2,1)} %get-tuple-element.119), channel_id=1, source_target_pairs={{0,64},{32,96},{64,0},{96,32},{1,65},{33,97},{65,1},{97,33},{2,66}... | collective-permute-start | bytes 2752520 | tf_op jit(solution)/shard_map/ppermute | solution.py:38
  215.3 31.2 %collective-permute-start.28 = (bf16[4,4,224,128]{3,2,1,0:T(8,128)(2,1)}, bf16[4,4,224,128]{3,2,1,0:T(8,128)(2,1)S(1)}, u32[]{:S(2)}, u32[]{:S(2)}) collective-permute-start(bf16[4,4,224,128]{3,2,1,0:T(8,128)(2,1)} %get-tuple-element.120), channel_id=1, source_target_pairs={{0,16},{8,24},{16,0},{24,8},{1,17},{9,25},{17,1},{25,9},{2,18},{10... | collective-permute-start | bytes 2752520 | tf_op jit(solution)/shard_map/ppermute | solution.py:38
  215.4 31.2 %collective-permute-start.29 = (bf16[4,4,224,128]{3,2,1,0:T(8,128)(2,1)}, bf16[4,4,224,128]{3,2,1,0:T(8,128)(2,1)}, u32[]{:S(2)}, u32[]{:S(2)}) collective-permute-start(bf16[4,4,224,128]{3,2,1,0:T(8,128)(2,1)} %get-tuple-element.121), channel_id=1, source_target_pairs={{0,6},{2,0},{4,2},{6,4},{1,7},{3,1},{5,3},{7,5},{8,14},{10,8},{12,... | collective-permute-start | bytes 2752520 | tf_op jit(solution)/shard_map/ppermute | solution.py:38
  218.4 33.5 %collective-permute-start.30 = (bf16[4,4,224,128]{3,2,1,0:T(8,128)(2,1)}, bf16[4,4,224,128]{3,2,1,0:T(8,128)(2,1)}, u32[]{:S(2)}, u32[]{:S(2)}) collective-permute-start(bf16[4,4,224,128]{3,2,1,0:T(8,128)(2,1)} %get-tuple-element.122), channel_id=1, source_target_pairs={{0,2},{2,4},{4,6},{6,0},{1,3},{3,5},{5,7},{7,1},{8,10},{10,12},{12... | collective-permute-start | bytes 2752520 | tf_op jit(solution)/shard_map/ppermute | solution.py:38
  218.4 36.1 %all-to-all-start = ((bf16[64,16,640]{2,1,0:T(8,128)(2,1)}), bf16[64,16,640]{2,1,0:T(8,128)(2,1)S(1)}, u32[]{:S(2)}, u32[]{:S(2)}) async-start(bf16[64,16,640]{2,1,0:T(8,128)(2,1)} %get-tuple-element.115), calls=%async_computation | async-start | bytes 2621440 | tf_op jit(solution)/shard_map/all_to_all | solution.py:483
  227.4 43.2 %collective-permute-start.31 = (bf16[4,4,224,128]{3,2,1,0:T(8,128)(2,1)}, bf16[4,4,224,128]{3,2,1,0:T(8,128)(2,1)}, u32[]{:S(2)}, u32[]{:S(2)}) collective-permute-start(bf16[4,4,224,128]{3,2,1,0:T(8,128)(2,1)} %get-tuple-element.123), channel_id=1, source_target_pairs={{0,96},{32,0},{64,32},{96,64},{1,97},{33,1},{65,33},{97,65},{2,98}... | collective-permute-start | bytes 2752520 | tf_op jit(solution)/shard_map/ppermute | solution.py:38
  246.6 24.1 %collective-permute-start.32 = (bf16[4,4,224,128]{3,2,1,0:T(8,128)(2,1)}, bf16[4,4,224,128]{3,2,1,0:T(8,128)(2,1)}, u32[]{:S(2)}, u32[]{:S(2)}) collective-permute-start(bf16[4,4,224,128]{3,2,1,0:T(8,128)(2,1)} %get-tuple-element.124), channel_id=1, source_target_pairs={{0,32},{32,64},{64,96},{96,0},{1,33},{33,65},{65,97},{97,1},{2,34}... | collective-permute-start | bytes 2752520 | tf_op jit(solution)/shard_map/ppermute | solution.py:38
  246.6 24.1 %collective-permute-start.33 = (bf16[4,4,224,128]{3,2,1,0:T(8,128)(2,1)}, bf16[4,4,224,128]{3,2,1,0:T(8,128)(2,1)}, u32[]{:S(2)}, u32[]{:S(2)}) collective-permute-start(bf16[4,4,224,128]{3,2,1,0:T(8,128)(2,1)} %get-tuple-element.125), channel_id=1, source_target_pairs={{0,24},{8,0},{16,8},{24,16},{1,25},{9,1},{17,9},{25,17},{2,26},{10... | collective-permute-start | bytes 2752520 | tf_op jit(solution)/shard_map/ppermute | solution.py:38
  246.7 24.0 %collective-permute-start.34 = (bf16[4,4,224,128]{3,2,1,0:T(8,128)(2,1)}, bf16[4,4,224,128]{3,2,1,0:T(8,128)(2,1)}, u32[]{:S(2)}, u32[]{:S(2)}) collective-permute-start(bf16[4,4,224,128]{3,2,1,0:T(8,128)(2,1)} %get-tuple-element.126), channel_id=1, source_target_pairs={{0,8},{8,16},{16,24},{24,0},{1,9},{9,17},{17,25},{25,1},{2,10},{10... | collective-permute-start | bytes 2752520 | tf_op jit(solution)/shard_map/ppermute | solution.py:38
  251.8 20.2 %collective-permute-start.35 = (bf16[4,4,224,128]{3,2,1,0:T(8,128)(2,1)}, bf16[4,4,224,128]{3,2,1,0:T(8,128)(2,1)}, u32[]{:S(2)}, u32[]{:S(2)}) collective-permute-start(bf16[4,4,224,128]{3,2,1,0:T(8,128)(2,1)} %get-tuple-element.127), channel_id=1, source_target_pairs={{0,4},{2,6},{4,0},{6,2},{1,5},{3,7},{5,1},{7,3},{8,12},{10,14},{12... | collective-permute-start | bytes 2752520 | tf_op jit(solution)/shard_map/ppermute | solution.py:38
  258.3 66.1 %all-to-all-start.1 = ((bf16[64,16,512]{2,1,0:T(8,128)(2,1)}), bf16[64,16,512]{2,1,0:T(8,128)(2,1)S(1)}, u32[]{:S(2)}, u32[]{:S(2)}) async-start(bf16[64,16,512]{2,1,0:T(8,128)(2,1)} %get-tuple-element.116), calls=%async_computation.1 | async-start | bytes 2097152 | tf_op jit(solution)/shard_map/all_to_all | solution.py:486
  (79 other events, 963.8 us)
Sparse Core Ops, SparseCore 0:
  10.9 107.4 all-gather.1

commit v3 on v0

v3 whole, which is shorter than its diff:
```python
import math

import jax
import jax.numpy as jnp
from jax import lax
from jax.experimental import pallas as pl
from jax.experimental.pallas import tpu as pltpu
from jax.sharding import Mesh, PartitionSpec as P

FF = 25600
KS = 512
RANK = 256
ROWS = 80
COLS = 400
NL = 2
N = 64
WIDE = 4 * COLS
LANES = 1664

bf16 = jnp.bfloat16
f32 = jnp.float32
highest = lax.Precision.HIGHEST
AX = ("z", "x", "y")
VMEM = 56 * 1024 * 1024

ORDERS = (("z", "x", "y"), ("y", "z", "x"))
ISSUE = ((1, 1), (1, 3), (0, 1), (0, 3), (0, 2), (1, 2))
HBM = pl.BlockSpec(memory_space=pl.ANY)
SMEM = pl.BlockSpec(memory_space=pltpu.SMEM)
INNER = pl.BlockSpec(memory_space=pltpu.VMEM)


def shifted(x, axis, k):
    return lax.ppermute(x, axis, [(s, (s - k) % 4) for s in range(4)])


def params():
    return pltpu.CompilerParams(vmem_limit_bytes=VMEM)


def cost(nbytes, flops=0):
    return pl.CostEstimate(flops=flops, bytes_accessed=nbytes, transcendentals=0)


def pack_kernel(pos_ref, g_ref, *refs):
    outs, scr, sem = refs[:8], refs[8:10], refs[10]
    z = pl.program_id(0)
    kz = lax.rem(pos_ref[0] - z + 4, 4)

    def put(block, strips):
        wide = jnp.concatenate(strips + [jnp.zeros((ROWS, LANES - WIDE), bf16)], axis=1)
        block[...] = wide

    for i in range(4):
        put(scr[0].at[kz, i], [g_ref[0, :, WIDE * i : WIDE * (i + 1)]])
        ky = lax.rem(pos_ref[2] - i + 4, 4)
        put(
            scr[1].at[ky, z],
            [g_ref[1, :, WIDE * x + COLS * i : WIDE * x + COLS * (i + 1)] for x in range(4)],
        )
    for k in range(4):

        @pl.when(kz == k)
        def _():
            pltpu.make_async_copy(scr[0].at[k], outs[k], sem.at[k]).start()

        pltpu.make_async_copy(scr[1].at[k, z], outs[4 + k].at[z], sem.at[4 + k]).start()

    @pl.when(z == 3)
    def _():
        for l in range(NL):
            for k in range(4):
                pltpu.make_async_copy(scr[l].at[k], outs[4 * l + k], sem.at[4 * l + k]).wait()


def pack(pos, g):
    outs = pl.pallas_call(
        pack_kernel,
        grid=(4,),
        in_specs=[SMEM, pl.BlockSpec((NL, ROWS, 4 * WIDE), lambda i: (0, 0, i))],
        out_specs=[HBM] * 8,
        out_shape=[jax.ShapeDtypeStruct((4, ROWS, LANES), bf16)] * 8,
        scratch_shapes=[pltpu.VMEM((4, 4, ROWS, LANES), bf16)] * 2 + [pltpu.SemaphoreType.DMA((8,))],
        compiler_params=params(),
        cost_estimate=cost(17_000_000),
    )(pos, g)
    return [list(outs[:4]), list(outs[4:])]


def permute_stage(bufs, stage):
    got = [[b[0], None, None, None] for b in bufs]
    for l, k in ISSUE:
        got[l][k] = shifted(bufs[l][k], ORDERS[l][stage], k)
    return got


def moved(got):
    return [got[l][k] for l, k in ISSUE]


def flat(got):
    return moved(got) + [got[l][0] for l in range(NL)]


def unflat(refs):
    got = [[None] * 4 for _ in range(NL)]
    for (l, k), r in zip(ISSUE, refs):
        got[l][k] = r
    for l, r in enumerate(refs[6:]):
        got[l][0] = r
    return got


def second_kernel(pos_ref, *refs):
    first = unflat(refs[:8])
    outs, scr, sem, sem_out = refs[8:14], refs[14:20], refs[20], refs[21]
    loads = [[] for _ in outs]
    for at, (l, k) in enumerate(ISSUE):
        place = lax.rem(pos_ref[AX.index(ORDERS[l][1])] + 4 - k, 4)
        for k1 in range(4):
            loads[at].append(
                pltpu.make_async_copy(first[l][k1].at[place], scr[at].at[k1], sem.at[4 * at + k1])
            )
    for group in loads:
        for c in group:
            c.start()
    stores = []
    for at, group in enumerate(loads):
        for c in group:
            c.wait()
        stores.append(pltpu.make_async_copy(scr[at], outs[at], sem_out.at[at]))
        stores[-1].start()
    for c in stores:
        c.wait()


def second(pos, got):
    outs = pl.pallas_call(
        second_kernel,
        in_specs=[SMEM] + [HBM] * 8,
        out_specs=[HBM] * 6,
        out_shape=[jax.ShapeDtypeStruct((4, ROWS, LANES), bf16)] * 6,
        scratch_shapes=[pltpu.VMEM((4, ROWS, LANES), bf16)] * 6
        + [pltpu.SemaphoreType.DMA((24,)), pltpu.SemaphoreType.DMA((6,))],
        compiler_params=params(),
        cost_estimate=cost(13_000_000),
    )(pos, *flat(got))
    bufs = [[None] * 4 for _ in range(NL)]
    for (l, k), o in zip(ISSUE, outs):
        bufs[l][k] = o
    return bufs


def panel_loads(pos_ref, first, got, x_ref, sem):
    loads = []
    for l in range(NL):
        own = pos_ref[AX.index(ORDERS[l][1])]
        copies = []
        for k in range(4):
            dst = x_ref.at[l, k, 0] if l == 0 else x_ref.at[l, 0, k]
            copies.append(pltpu.make_async_copy(first[l][k].at[own], dst, sem.at[8 * l + k]))
            if k:
                dst = x_ref.at[l, :, k] if l == 0 else x_ref.at[l, k]
                copies.append(pltpu.make_async_copy(got[l][k], dst, sem.at[8 * l + 4 + k]))
        for c in copies:
            c.start()
        loads.append(copies)
    return loads


def panel_kernel(pos_ref, *refs):
    first, got = unflat(refs[:8]), unflat(refs[8:14])
    s_ref = refs[14:16]
    outs = refs[16:24]
    x_ref, s_vmem, acc_ref, u_ref, sem, sem_s, sem_out = refs[24:]
    load_s = []
    for l in range(NL):
        for kz in range(4):
            for k in range(4):
                z, other = lax.rem(pos_ref[0] + kz, 4), lax.rem(pos_ref[1 + l] + k, 4)
                at = 16 * l + 4 * kz + k
                load_s.append(
                    pltpu.make_async_copy(s_ref[l].at[4 * z + other], s_vmem.at[l, kz, k], sem_s.at[at])
                )
                load_s[-1].start()
    loads = panel_loads(pos_ref, first, got, x_ref, sem)
    for c in load_s:
        c.wait()
    stores = []
    for l in range(NL):
        for c in loads[l]:
            c.wait()
        for i in range(2):
            part = lax.dot_general(
                s_vmem[l, 2 * i : 2 * i + 2].reshape(8 * ROWS, KS),
                x_ref[l, 2 * i : 2 * i + 2].reshape(8 * ROWS, LANES),
                (((0,), (0,)), ((), ())),
                preferred_element_type=f32,
            )
            acc_ref[...] = part if i == 0 else acc_ref[...] + part
        u_ref[l] = jnp.transpose(acc_ref[...], (1, 0)).astype(bf16)
        stores += [
            pltpu.make_async_copy(u_ref.at[l, rows], outs[4 * l + k], sem_out.at[4 * l + k])
            for k, rows in strips(pos_ref, l)
        ]
        for c in stores[-4:]:
            c.start()
    for c in stores:
        c.wait()


def strips(pos_ref, l):
    me = pos_ref[AX.index(ORDERS[l][2])]
    return [(k, pl.ds(pl.multiple_of(lax.rem(me + k, 4) * COLS, 16), COLS)) for k in range(4)]


def panel_products(pos, got1, got2, s):
    outs = pl.pallas_call(
        panel_kernel,
        in_specs=[SMEM] + [HBM] * 16,
        out_specs=[HBM] * 8,
        out_shape=[jax.ShapeDtypeStruct((COLS, KS), bf16)] * 8,
        scratch_shapes=[
            pltpu.VMEM((NL, 4, 4, ROWS, LANES), bf16),
            pltpu.VMEM((NL, 4, 4, ROWS, KS), bf16),
            pltpu.VMEM((KS, LANES), f32),
            pltpu.VMEM((NL, LANES, KS), bf16),
            pltpu.SemaphoreType.DMA((16,)),
            pltpu.SemaphoreType.DMA((32,)),
            pltpu.SemaphoreType.DMA((8,)),
        ],
        compiler_params=params(),
        cost_estimate=cost(15_000_000, 4_400_000_000),
    )(pos, *flat(got1), *moved(got2), *s)
    return [list(outs[:4]), list(outs[4:])]


def gram_kernel(*refs):
    got = unflat(refs[:8])
    old_ref, pick_ref = refs[8:10]
    sk_refs, send_ref = refs[10:12], refs[12]
    sums, pieces = [], []
    for l in range(NL):
        parts = [r[...].astype(f32) for r in got[l]]
        sk = (parts[0] + parts[1] + parts[2] + parts[3]).astype(bf16)
        sk_refs[l][...] = sk
        wide = sk.astype(f32)
        diag = jnp.sum(wide * wide, axis=0, keepdims=True)
        high = diag.astype(bf16).astype(f32)
        for d in (high, diag - high):
            pieces += [d[:, 128 * i : 128 * (i + 1)] for i in range(4)]
        chosen = jnp.dot(sk, pick_ref[l], preferred_element_type=f32).astype(bf16)
        right = jnp.concatenate([chosen, old_ref[l]], 1)
        both = lax.dot_general(sk, right, (((0,), (0,)), ((), ())), preferred_element_type=f32)
        sums.append(both.reshape(N, 8, KS))
    send_ref[:, :, 0:KS] = jnp.concatenate(sums, 1).astype(bf16)
    send_ref[:, :, KS : KS + 128] = jnp.broadcast_to(
        jnp.concatenate(pieces, 0).astype(bf16)[None], (N, 16, 128)
    )


def gram_products(got, old, picker):
    outs = pl.pallas_call(
        gram_kernel,
        in_specs=[INNER] * 10,
        out_specs=[INNER] * 3,
        out_shape=[jax.ShapeDtypeStruct((COLS, KS), bf16)] * 2
        + [jax.ShapeDtypeStruct((N, 16, KS + 128), bf16)],
        compiler_params=params(),
        cost_estimate=cost(7_000_000, 1_000_000_000),
    )(*flat(got), old, picker)
    return list(outs[:2]), outs[2]


def back_kernel(pos_ref, *refs):
    first, got = unflat(refs[:8]), unflat(refs[8:14])
    sk_in = unflat(refs[14:22])
    outs = refs[22:30]
    x_ref, sk_ref, t_ref, sem, sem_s, sem_out = refs[30:]
    load_s = []
    for l in range(NL):
        for k, rows in strips(pos_ref, l):
            load_s.append(pltpu.make_async_copy(sk_in[l][k], sk_ref.at[l, rows], sem_s.at[4 * l + k]))
            load_s[-1].start()
    loads = panel_loads(pos_ref, first, got, x_ref, sem)
    for l in range(NL):
        sk_ref[l, WIDE:LANES, :] = jnp.zeros((LANES - WIDE, KS), bf16)
    for c in load_s:
        c.wait()
    stores = []
    for l in range(NL):
        for c in loads[l]:
            c.wait()
        for kz in range(4):
            t_ref[l, kz] = (
                jnp.dot(x_ref[l, kz].reshape(4 * ROWS, LANES), sk_ref[l], preferred_element_type=f32)
                .astype(bf16)
                .reshape(4, ROWS, KS)
            )
            if l == 0:
                stores.append(pltpu.make_async_copy(t_ref.at[0, kz], outs[kz], sem_out.at[kz]))
                stores[-1].start()
                continue
            for k in range(4):
                stores.append(
                    pltpu.make_async_copy(t_ref.at[1, kz, k], outs[4 + k].at[kz], sem_out.at[4 + 4 * kz + k])
                )
                stores[-1].start()
    for c in stores:
        c.wait()


def back_products(pos, got1, got2, sks):
    outs = pl.pallas_call(
        back_kernel,
        in_specs=[SMEM] + [HBM] * 22,
        out_specs=[HBM] * 8,
        out_shape=[jax.ShapeDtypeStruct((4, ROWS, KS), bf16)] * 8,
        scratch_shapes=[
            pltpu.VMEM((NL, 4, 4, ROWS, LANES), bf16),
            pltpu.VMEM((NL, LANES, KS), bf16),
            pltpu.VMEM((NL, 4, 4, ROWS, KS), bf16),
            pltpu.SemaphoreType.DMA((16,)),
            pltpu.SemaphoreType.DMA((8,)),
            pltpu.SemaphoreType.DMA((20,)),
        ],
        compiler_params=params(),
        cost_estimate=cost(16_000_000, 4_400_000_000),
    )(pos, *flat(got1), *moved(got2), *flat(sks))
    return [list(outs[:4]), list(outs[4:])]


def owner_kernel(me_ref, got_ref, ranks_ref, mine_ref, scores_ref):
    total = jnp.sum(got_ref[...].astype(f32), axis=0)
    row = me_ref[0] * 8 + lax.broadcasted_iota(jnp.int32, (8, 128), 0)
    lane = lax.broadcasted_iota(jnp.int32, (8, 128), 1)
    my_rows = me_ref[0] * 8 + lax.broadcasted_iota(jnp.int32, (8, RANK), 0)
    owned, scores = [], 0.0
    for l in range(NL):
        diag = total[8 * l : 8 * l + 4, KS:] + total[8 * l + 4 : 8 * l + 8, KS:]
        scores = scores + diag
        trace = jnp.sum(jnp.sum(diag, axis=1, keepdims=True), axis=0, keepdims=True)
        mine = jnp.zeros((8, 128), f32)
        for c in range(4):
            mine = mine + jnp.where(lane + 128 * c == row, diag[c : c + 1, :], 0.0)
        my_diag = jnp.sum(mine, axis=1, keepdims=True)
        scale = 0.5 * KS / trace
        rms = jnp.sqrt(trace / (FF * KS))
        gram = total[8 * l : 8 * l + 8, 0:RANK]
        corrected = jnp.where(my_rows == ranks_ref[l : l + 1, :], 1.5 - scale * my_diag, -scale * gram)
        owned.append(jnp.concatenate([corrected / rms, total[8 * l : 8 * l + 8, RANK:KS]], 1))
    mine_ref[...] = jnp.concatenate(owned, 0).astype(bf16)
    scores_ref[...] = scores / FF


def owner_rows(me, got, ranks):
    return pl.pallas_call(
        owner_kernel,
        in_specs=[SMEM, INNER, INNER],
        out_specs=[INNER, INNER],
        out_shape=[jax.ShapeDtypeStruct((16, KS), bf16), jax.ShapeDtypeStruct((4, 128), f32)],
        compiler_params=params(),
        cost_estimate=cost(2_500_000),
    )(me, got, ranks)


def moments_kernel(rows_ref, sk0_ref, sk1_ref, one_ref, two_ref, basis_ref, first_ref, second_ref, factor_ref):
    rows = rows_ref[...].astype(f32)
    for l in range(NL):
        both = rows[:, 8 * l : 8 * l + 8, :].reshape(KS, KS).astype(bf16)
        factor, inner = both[:, :RANK], both[:, RANK:]
        factor_ref[l] = factor
        sk = (sk0_ref, sk1_ref)[l][...]
        basis_ref[l] = jnp.dot(sk, factor, preferred_element_type=f32).astype(bf16)
        correlation = lax.dot_general(
            inner, factor, (((0,), (0,)), ((), ())), preferred_element_type=f32
        ) / math.sqrt(FF * RANK)
        first_ref[l] = jnp.dot(one_ref[l], correlation, precision=highest, preferred_element_type=f32)
        second_ref[l] = jnp.dot(
            two_ref[l], correlation * correlation, precision=highest, preferred_element_type=f32
        )


def moments(rows, sk, one, two):
    return pl.pallas_call(
        moments_kernel,
        in_specs=[INNER] * 5,
        out_specs=[INNER] * 4,
        out_shape=[
            jax.ShapeDtypeStruct((NL, COLS, RANK), bf16),
            jax.ShapeDtypeStruct((NL, ROWS, RANK), f32),
            jax.ShapeDtypeStruct((NL, ROWS, RANK), f32),
            jax.ShapeDtypeStruct((NL, KS, RANK), bf16),
        ],
        compiler_params=params(),
        cost_estimate=cost(4_000_000, 500_000_000),
    )(rows, *sk, one, two)


def project_kernel(*refs):
    got = unflat(refs[:8])
    factor_ref, out_ref = refs[8:]
    for l in range(NL):
        t_rows = sum(got[l][k][...].astype(f32) for k in range(4))
        out_ref[l] = (
            jnp.dot(t_rows, factor_ref[l].astype(f32), precision=highest, preferred_element_type=f32)
            / math.sqrt(FF)
        ).astype(bf16)


def project(got, factor):
    return pl.pallas_call(
        project_kernel,
        in_specs=[INNER] * 9,
        out_specs=INNER,
        out_shape=jax.ShapeDtypeStruct((NL, ROWS, RANK), bf16),
        compiler_params=params(),
        cost_estimate=cost(2_000_000, 100_000_000),
    )(*flat(got), factor)


def reduce_kernel(*refs):
    got = unflat(refs[:8])
    outs = refs[8:]
    for l in range(NL):
        for k in range(4):
            outs[4 * l + k][...] = sum(got[l][j][k].astype(f32) for j in range(4)).astype(bf16)


def reduce_stage(got):
    outs = pl.pallas_call(
        reduce_kernel,
        in_specs=[INNER] * 8,
        out_specs=[INNER] * 8,
        out_shape=[jax.ShapeDtypeStruct((ROWS, KS), bf16)] * 8,
        compiler_params=params(),
        cost_estimate=cost(3_300_000),
    )(*flat(got))
    return [list(outs[:4]), list(outs[4:])]


def shift_back(bufs, stage):
    got = [[b[0], None, None, None] for b in bufs]
    for l, k in ISSUE:
        got[l][k] = shifted(bufs[l][4 - k], ORDERS[l][stage], k)
    return got


def shards(gradients, sketch, rank_lists, old_basis, first_moment, second_moment):
    s_rows = [lax.all_gather(sketch, axes, axis=0) for axes in (("z", "x"), ("z", "y"))]
    pos = jnp.stack([lax.axis_index(a) for a in AX]).astype(jnp.int32)
    got1 = permute_stage(pack(pos, gradients), 0)
    got2 = permute_stage(second(pos, got1), 1)
    picker = (lax.broadcasted_iota(jnp.int32, (NL, KS, RANK), 1) == rank_lists[:, None, :]).astype(bf16)
    parts = shift_back(panel_products(pos, got1, got2, s_rows), 2)
    sketched, send = gram_products(parts, old_basis, picker)
    got = lax.all_to_all(send, AX, 0, 0, tiled=True)
    sks = permute_stage([[sk] * 4 for sk in sketched], 2)
    me = (16 * pos[0] + 4 * pos[1] + pos[2])[None]
    mine, scores = owner_rows(me, got, rank_lists)
    everyone = lax.all_gather(mine, AX, axis=0)
    basis, first, second_out, factor = moments(everyone, sketched, first_moment, second_moment)
    back = shift_back(back_products(pos, got1, got2, sks), 0)
    back = shift_back(reduce_stage(back), 1)
    projected = project(back, factor)
    scores = scores + lax.ppermute(scores, "layer", [(0, 1), (1, 0)])
    return basis, projected, first, second_out, scores.reshape(KS)


def solution(mesh):
    cube = Mesh(mesh.devices.reshape(4, 4, 4, 2), AX + ("layer",))
    rows = P("layer", AX, None)
    return jax.shard_map(
        shards,
        mesh=cube,
        in_specs=(rows, P(AX, None), P("layer", None), rows, rows, rows),
        out_specs=(rows, rows, rows, rows, P()),
        check_vma=False,
    )
```

time: 1280 us -> 298 us (0.23)
  waiting for transfers between devices: 939 us -> 159 us
  blocking collectives: 179 us -> 0 us
  local copies, waits for them, and re-layouts: 101 us -> 5.2 us
  starting transfers between devices: 0.38 us -> 63.9 us
  Pallas kernels: 0 us -> 53.2 us
  matrix products: 35.8 us -> 0 us
    unnamed x7 -> x3, waiting for transfers between devices: 712 us -> 0.71 us
    psum x2 -> x0, waiting for transfers between devices: 227 us -> none  [the longest x1 131 us: refresh_panel(): gram = lax.psum(gram_part, 'fsdp')]
    all_to_all x1 -> x0, blocking collectives: 176 us -> none  [shards(): lax.all_to_all(gradients, 'fsdp', split_axis=2, concat_axis=1, tiled=True)]
    ppermute x0 -> x37, waiting for transfers between devices: none -> 136 us  [the longest x36 136 us: shifted(): return lax.ppermute(x, axis, [(s, (s - k) % 4) for s in range(4)])]
    ppermute x0 -> x37, starting transfers between devices: none -> 57.9 us  [the longest x36 57.9 us: shifted(): return lax.ppermute(x, axis, [(s, (s - k) % 4) for s in range(4)])]
    pallas_call x0 -> x9, Pallas kernels: none -> 53.2 us  [the longest x1 12.5 us: panel_products(): pl.pallas_call(panel_kernel, in_specs=[SMEM] + [HBM] * 16, out_specs=[HBM...]
    unnamed x20 -> x70, local copies, waits for them, and re-layouts: 41.6 us -> 5.2 us
    dot_general x16 -> x0, matrix products: 35.8 us -> none  [the longest x2 12.9 us: refresh_panel(): jnp.dot(panel_cols, basis_new, preferred_element_type=jnp.float32)]
  transfers between devices with their start and end apart: 5 -> 41, of which waited for: 4 -> 19; matrix products, arithmetic and copies ran while one was open for 8% -> 1% of each run, Pallas kernels for 0% -> 11%
where the time goes in v3:
time: 298 us
  waiting for transfers between devices  159 us (53%)
  starting transfers between devices  63.9 us (21%)
  Pallas kernels  53.2 us (18%)
  between operations  14.1 us (5%)
  local copies, waits for them, and re-layouts  5.2 us (2%)
    ppermute x36, waiting for transfers between devices, shifted(): return lax.ppermute(x, axis, [(s, (s - k) % 4) for s in range(4)])  136 us
    ppermute x36, starting transfers between devices, shifted(): return lax.ppermute(x, axis, [(s, (s - k) % 4) for s in range(4)])  57.9 us
    all_to_all x1, waiting for transfers between devices, shards(): got = lax.all_to_all(send, AX, 0, 0, tiled=True)  17 us
    pallas_call x1, Pallas kernels, panel_products(): pl.pallas_call(panel_kernel, in_specs=[SMEM] + [HBM] * 16, out_specs=[HBM...  12.5 us
    pallas_call x1, Pallas kernels, back_products(): pl.pallas_call(back_kernel, in_specs=[SMEM] + [HBM] * 22, out_specs=[HBM]...  10.9 us
    pallas_call x1, Pallas kernels, pack(): pl.pallas_call(pack_kernel, grid=(4,), in_specs=[SMEM, pl.BlockSpec((NL,...  7.76 us
    pallas_call x1, Pallas kernels, second(): pl.pallas_call(second_kernel, in_specs=[SMEM] + [HBM] * 8, out_specs=[HBM...  6.25 us
  transfers between devices with their start and end apart: 41, of which 19 were waited for; matrix products, arithmetic and copies ran while one was open for 1% of the time, Pallas kernels for 11%

profile of v3, /device:TPU:0, one launch (start us, length us, event | category | flops | bytes accessed | tf_op | source)
XLA Modules:
  0.0 298.1 jit_solution(4447919556999452862)
XLA Ops:
  8.6 7.8 %shard_map.101 = (bf16[4,80,1664]{2,1,0:T(8,128)(2,1)}, bf16[4,80,1664]{2,1,0:T(8,128)(2,1)}, bf16[4,80,1664]{2,1,0:T(8,128)(2,1)}, bf16[4,80,1664]{2,1,0:T(8,12...) custom-call(s32[3]{0:T(128)} %pad_add_fusion.pos_ref, ...), custom_call_target="tpu_custom_call" | custom-call | bytes 17000000 | tf_op jit(solution)/shard_map/pallas_call | solution.py:77
  19.5 4.2 %collective-permute-start.2 = (bf16[4,80,1664]{2,1,0:T(8,128)(2,1)}, bf16[4,80,1664]{2,1,0:T(8,128)(2,1)S(1)}, u32[]{:S(2)}, u32[]{:S(2)}) collective-permute-start(bf16[4,80,1664]{2,1,0:T(8,128)(2,1)} %get-tuple-element.54), channel_id=1, source_target_pairs={{0,96},{32,0},{64,32},{96,64},{1,97},{33,1},{65,33},{97,65},{2,98}... | collective-permute-start | bytes 3194888 | tf_op jit(solution)/shard_map/ppermute | solution.py:34
  25.4 17.2 %collective-permute-done.refs_0_ = bf16[4,80,1664]{2,1,0:T(8,128)(2,1)S(1)} collective-permute-done((bf16[4,80,1664]{2,1,0:T(8,128)(2,1)}, bf16[4,80,1664]{2,1,0:T(8,128)(2,1)S(1)}, u32[]{:S(2)}, u32[]{:S(2)}) %collective-permute-start) | collective-permute-done | bytes 1064992 | tf_op jit(solution)/shard_map/ppermute | solution.py:34
  45.9 29.4 %collective-permute-done.2.refs_2_ = bf16[4,80,1664]{2,1,0:T(8,128)(2,1)S(1)} collective-permute-done((bf16[4,80,1664]{2,1,0:T(8,128)(2,1)}, bf16[4,80,1664]{2,1,0:T(8,128)(2,1)S(1)}, u32[]{:S(2)}, u32[]{:S(2)}) %collective-permute-start.2) | collective-permute-done | bytes 1064992 | tf_op jit(solution)/shard_map/ppermute | solution.py:34
  75.3 3.8 %collective-permute-done.3.refs_3_ = bf16[4,80,1664]{2,1,0:T(8,128)(2,1)} collective-permute-done((bf16[4,80,1664]{2,1,0:T(8,128)(2,1)}, bf16[4,80,1664]{2,1,0:T(8,128)(2,1)}, u32[]{:S(2)}, u32[]{:S(2)}) %collective-permute-start.3) | collective-permute-done | bytes 1064992 | tf_op jit(solution)/shard_map/ppermute | solution.py:34
  79.1 6.2 %shard_map.102 = (bf16[4,80,1664]{2,1,0:T(8,128)(2,1)}, bf16[4,80,1664]{2,1,0:T(8,128)(2,1)}, bf16[4,80,1664]{2,1,0:T(8,128)(2,1)}, bf16[4,80,1664]{2,1,0:T(8,12...) custom-call(s32[3]{0:T(128)} %pad_add_fusion.pos_ref, bf16[4,80,1664]{2,1,0:T(8,128)(2,1)} %copy-done, ...), custom_call_target="tpu_custom_call" | custom-call | bytes 13000000 | tf_op jit(solution)/shard_map/pallas_call | solution.py:138
  92.2 17.8 %collective-permute-done.10.refs_12_ = bf16[4,80,1664]{2,1,0:T(8,128)(2,1)S(1)} collective-permute-done((bf16[4,80,1664]{2,1,0:T(8,128)(2,1)}, bf16[4,80,1664]{2,1,0:T(8,128)(2,1)S(1)}, u32[]{:S(2)}, u32[]{:S(2)}) %collective-permute-start.10) | collective-permute-done | bytes 1064992 | tf_op jit(solution)/shard_map/ppermute | solution.py:34
  110.0 4.8 %collective-permute-start.9 = (bf16[4,80,1664]{2,1,0:T(8,128)(2,1)}, bf16[4,80,1664]{2,1,0:T(8,128)(2,1)}, u32[]{:S(2)}, u32[]{:S(2)}) collective-permute-start(bf16[4,80,1664]{2,1,0:T(8,128)(2,1)} %get-tuple-element.63), channel_id=1, source_target_pairs={{0,8},{8,16},{16,24},{24,0},{1,9},{9,17},{17,25},{25,1},{2,10},{10... | collective-permute-start | bytes 3194888 | tf_op jit(solution)/shard_map/ppermute | solution.py:34
  117.7 21.4 %collective-permute-done.6.refs_8_ = bf16[4,80,1664]{2,1,0:T(8,128)(2,1)S(1)} collective-permute-done((bf16[4,80,1664]{2,1,0:T(8,128)(2,1)}, bf16[4,80,1664]{2,1,0:T(8,128)(2,1)S(1)}, u32[]{:S(2)}, u32[]{:S(2)}) %collective-permute-start.6) | collective-permute-done | bytes 1064992 | tf_op jit(solution)/shard_map/ppermute | solution.py:34
  139.1 3.3 %collective-permute-done.7.refs_9_ = bf16[4,80,1664]{2,1,0:T(8,128)(2,1)} collective-permute-done((bf16[4,80,1664]{2,1,0:T(8,128)(2,1)}, bf16[4,80,1664]{2,1,0:T(8,128)(2,1)}, u32[]{:S(2)}, u32[]{:S(2)}) %collective-permute-start.7) | collective-permute-done | bytes 1064992 | tf_op jit(solution)/shard_map/ppermute | solution.py:34
  142.4 12.5 %shard_map.103 = (bf16[400,512]{1,0:T(8,128)(2,1)}, bf16[400,512]{1,0:T(8,128)(2,1)}, bf16[400,512]{1,0:T(8,128)(2,1)}, bf16[400,512]{1,0:T(8,128)(2,1)}, bf16[4...) custom-call(s32[3]{0:T(128)} %pad_add_fusion.pos_ref, ...), custom_call_target="tpu_custom_call" | custom-call | flops 4400000000 | bytes 15000000 | tf_op jit(solution)/shard_map/pallas_call | solution.py:218
  161.4 5.2 %collective-permute-done.12.refs_0_ = bf16[400,512]{1,0:T(8,128)(2,1)S(1)} collective-permute-done((bf16[400,512]{1,0:T(8,128)(2,1)}, bf16[400,512]{1,0:T(8,128)(2,1)S(1)}, u32[]{:S(2)}, u32[]{:S(2)}) %collective-permute-start.12) | collective-permute-done | bytes 409632 | tf_op jit(solution)/shard_map/ppermute | solution.py:34
  168.7 8.7 %collective-permute-done.14.refs_2_ = bf16[400,512]{1,0:T(8,128)(2,1)S(1)} collective-permute-done((bf16[400,512]{1,0:T(8,128)(2,1)}, bf16[400,512]{1,0:T(8,128)(2,1)S(1)}, u32[]{:S(2)}, u32[]{:S(2)}) %collective-permute-start.14) | collective-permute-done | bytes 409632 | tf_op jit(solution)/shard_map/ppermute | solution.py:34
  177.4 3.3 %collective-permute-done.15.refs_3_ = bf16[400,512]{1,0:T(8,128)(2,1)S(1)} collective-permute-done((bf16[400,512]{1,0:T(8,128)(2,1)}, bf16[400,512]{1,0:T(8,128)(2,1)S(1)}, u32[]{:S(2)}, u32[]{:S(2)}) %collective-permute-start.15) | collective-permute-done | bytes 409632 | tf_op jit(solution)/shard_map/ppermute | solution.py:34
  181.8 4.6 %shard_map.104 = (bf16[400,512]{1,0:T(8,128)(2,1)}, bf16[400,512]{1,0:T(8,128)(2,1)}, bf16[64,16,640]{2,1,0:T(8,128)(2,1)}) custom-call(bf16[400,512]{1,0:T(8,128)(2,1)} %copy-done.9, bf16[400,512]{1,0:T(8,128)(2,1)} %copy-done.10, bf16[400,512]{1,0:T(8,128)(2,1)} %copy-done.11, bf16[400,512]{1,0:T(8,128)(2,1)} %copy-done.12, bf16[400,512]{1,0:T(8,128)(2,1)} %copy-done.13, ...), custom_call_target="tpu_custom_call" | custom-call | flops 1000000000 | bytes 7000000 | tf_op jit(solution)/shard_map/pallas_call | solution.py:263
  186.4 5.9 %all-to-all-start = ((bf16[64,16,640]{2,1,0:T(8,128)(2,1)}), bf16[64,16,640]{2,1,0:T(8,128)(2,1)S(1)}, u32[]{:S(2)}, u32[]{:S(2)}) async-start(bf16[64,16,640]{2,1,0:T(8,128)(2,1)} %get-tuple-element.74), calls=%async_computation | async-start | bytes 2621440 | tf_op jit(solution)/shard_map/all_to_all | solution.py:457
  195.2 17.0 %all-to-all-done.got_ref = bf16[64,16,640]{2,1,0:T(8,128)(2,1)S(1)} async-done(((bf16[64,16,640]{2,1,0:T(8,128)(2,1)}), bf16[64,16,640]{2,1,0:T(8,128)(2,1)S(1)}, u32[]{:S(2)}, u32[]{:S(2)}) %all-to-all-start) | async-done | bytes 1310752 | tf_op jit(solution)/shard_map/all_to_all | solution.py:457
  222.7 11.1 %collective-permute-done.19.refs_15_ = bf16[400,512]{1,0:T(8,128)(2,1)S(1)} collective-permute-done((bf16[400,512]{1,0:T(8,128)(2,1)S(1)}, bf16[400,512]{1,0:T(8,128)(2,1)S(1)}, u32[]{:S(2)}, u32[]{:S(2)}) %collective-permute-start.19) | collective-permute-done | bytes 409632 | tf_op jit(solution)/shard_map/ppermute | solution.py:34
  235.8 10.9 %shard_map.107 = (bf16[4,80,512]{2,1,0:T(8,128)(2,1)}, bf16[4,80,512]{2,1,0:T(8,128)(2,1)}, bf16[4,80,512]{2,1,0:T(8,128)(2,1)}, bf16[4,80,512]{2,1,0:T(8,128)(2...) custom-call(s32[3]{0:T(128)} %pad_add_fusion.pos_ref, ...), custom_call_target="tpu_custom_call" | custom-call | flops 4400000000 | bytes 16000000 | tf_op jit(solution)/shard_map/pallas_call | solution.py:314
  252.4 4.4 %collective-permute-done.24.refs_0_ = bf16[4,80,512]{2,1,0:T(8,128)(2,1)S(1)} collective-permute-done((bf16[4,80,512]{2,1,0:T(8,128)(2,1)}, bf16[4,80,512]{2,1,0:T(8,128)(2,1)S(1)}, u32[]{:S(2)}, u32[]{:S(2)}) %collective-permute-start.24) | collective-permute-done | bytes 327712 | tf_op jit(solution)/shard_map/ppermute | solution.py:34
  259.1 3.4 %collective-permute-done.27.refs_3_ = bf16[4,80,512]{2,1,0:T(8,128)(2,1)S(1)} collective-permute-done((bf16[4,80,512]{2,1,0:T(8,128)(2,1)}, bf16[4,80,512]{2,1,0:T(8,128)(2,1)S(1)}, u32[]{:S(2)}, u32[]{:S(2)}) %collective-permute-start.27) | collective-permute-done | bytes 327712 | tf_op jit(solution)/shard_map/ppermute | solution.py:34
  271.0 3.7 %collective-permute-start.32 = (bf16[80,512]{1,0:T(8,128)(2,1)}, bf16[80,512]{1,0:T(8,128)(2,1)S(1)}, u32[]{:S(2)}, u32[]{:S(2)}) collective-permute-start(bf16[80,512]{1,0:T(8,128)(2,1)} %get-tuple-element.89), channel_id=1, source_target_pairs={{0,24},{8,0},{16,8},{24,16},{1,25},{9,1},{17,9},{25,17},{2,26},{10... | collective-permute-start | bytes 245768 | tf_op jit(solution)/shard_map/ppermute | solution.py:34
  278.9 5.5 %all-gather.11.cloned.1.call-done = bf16[1024,512]{1,0:T(8,128)(2,1)} async-done(((bf16[16,512]{1,0:T(8,128)(2,1)}), bf16[1024,512]{1,0:T(8,128)(2,1)}) %all-gather.11.cloned.1.call-update) | async-done | bytes 1048592 | tf_op jit(solution)/shard_map/all_gather | solution.py:461
  284.4 3.6 %shard_map.106 = (bf16[2,400,256]{2,1,0:T(8,128)(2,1)}, f32[2,80,256]{2,1,0:T(8,128)}, f32[2,80,256]{2,1,0:T(8,128)}, bf16[2,512,256]{2,1,0:T(8,128)(2,1)}) custom-call(bf16[64,16,512]{2,1,0:T(8,128)(2,1)} %bitcast.11, bf16[400,512]{1,0:T(8,128)(2,1)} %get-tuple-element.76.sk0_ref.refs_20_, bf16[400,512]{1,0:T(8,128)(2,1)} %get-tuple-element.77.sk1_ref.refs_21_, ...), custom_call_target="tpu_custom_call" | custom-call | flops 500000000 | bytes 4000000 | tf_op jit(solution)/shard_map/pallas_call | solution.py:385
  (143 shorter events, 68.4 us)
Async XLA Ops:
  7.2 135.2 %all-gather.7.cloned.1.call-start = ((), (), s32[]{:S(2)}) async-start(), calls=%async_computation.1 | async-start | bytes 1392640 | tf_op jit(solution)/shard_map/all_gather | solution.py:450
  7.9 134.5 %all-gather.9.cloned.1.call-start = ((), (), s32[]{:S(2)}) async-start(), calls=%async_computation.2 | async-start | bytes 1392640 | tf_op jit(solution)/shard_map/all_gather | solution.py:450
  16.4 26.3 %collective-permute-start = (bf16[4,80,1664]{2,1,0:T(8,128)(2,1)}, bf16[4,80,1664]{2,1,0:T(8,128)(2,1)S(1)}, u32[]{:S(2)}, u32[]{:S(2)}) collective-permute-start(bf16[4,80,1664]{2,1,0:T(8,128)(2,1)} %get-tuple-element.52), channel_id=1, source_target_pairs={{0,6},{2,0},{4,2},{6,4},{1,7},{3,1},{5,3},{7,5},{8,14},{10,8},{12,... | collective-permute-start | bytes 3194888 | tf_op jit(solution)/shard_map/ppermute | solution.py:34
  19.5 26.4 %collective-permute-start.1 = (bf16[4,80,1664]{2,1,0:T(8,128)(2,1)}, bf16[4,80,1664]{2,1,0:T(8,128)(2,1)S(1)}, u32[]{:S(2)}, u32[]{:S(2)}) collective-permute-start(bf16[4,80,1664]{2,1,0:T(8,128)(2,1)} %get-tuple-element.53), channel_id=1, source_target_pairs={{0,2},{2,4},{4,6},{6,0},{1,3},{3,5},{5,7},{7,1},{8,10},{10,12},{12... | collective-permute-start | bytes 3194888 | tf_op jit(solution)/shard_map/ppermute | solution.py:34
  19.5 55.8 %collective-permute-start.2 = (bf16[4,80,1664]{2,1,0:T(8,128)(2,1)}, bf16[4,80,1664]{2,1,0:T(8,128)(2,1)S(1)}, u32[]{:S(2)}, u32[]{:S(2)}) collective-permute-start(bf16[4,80,1664]{2,1,0:T(8,128)(2,1)} %get-tuple-element.54), channel_id=1, source_target_pairs={{0,96},{32,0},{64,32},{96,64},{1,97},{33,1},{65,33},{97,65},{2,98}... | collective-permute-start | bytes 3194888 | tf_op jit(solution)/shard_map/ppermute | solution.py:34
  23.7 55.4 %collective-permute-start.3 = (bf16[4,80,1664]{2,1,0:T(8,128)(2,1)}, bf16[4,80,1664]{2,1,0:T(8,128)(2,1)}, u32[]{:S(2)}, u32[]{:S(2)}) collective-permute-start(bf16[4,80,1664]{2,1,0:T(8,128)(2,1)} %get-tuple-element.55), channel_id=1, source_target_pairs={{0,32},{32,64},{64,96},{96,0},{1,33},{33,65},{65,97},{97,1},{2,34}... | collective-permute-start | bytes 3194888 | tf_op jit(solution)/shard_map/ppermute | solution.py:34
  23.7 55.4 %collective-permute-start.4 = (bf16[4,80,1664]{2,1,0:T(8,128)(2,1)}, bf16[4,80,1664]{2,1,0:T(8,128)(2,1)}, u32[]{:S(2)}, u32[]{:S(2)}) collective-permute-start(bf16[4,80,1664]{2,1,0:T(8,128)(2,1)} %get-tuple-element.56), channel_id=1, source_target_pairs={{0,64},{32,96},{64,0},{96,32},{1,65},{33,97},{65,1},{97,33},{2,66}... | collective-permute-start | bytes 3194888 | tf_op jit(solution)/shard_map/ppermute | solution.py:34
  42.6 36.5 %collective-permute-start.5 = (bf16[4,80,1664]{2,1,0:T(8,128)(2,1)}, bf16[4,80,1664]{2,1,0:T(8,128)(2,1)}, u32[]{:S(2)}, u32[]{:S(2)}) collective-permute-start(bf16[4,80,1664]{2,1,0:T(8,128)(2,1)} %get-tuple-element.57), channel_id=1, source_target_pairs={{0,4},{2,6},{4,0},{6,2},{1,5},{3,7},{5,1},{7,3},{8,12},{10,14},{12... | collective-permute-start | bytes 3194888 | tf_op jit(solution)/shard_map/ppermute | solution.py:34
  85.4 24.6 %collective-permute-start.10 = (bf16[4,80,1664]{2,1,0:T(8,128)(2,1)}, bf16[4,80,1664]{2,1,0:T(8,128)(2,1)S(1)}, u32[]{:S(2)}, u32[]{:S(2)}) collective-permute-start(bf16[4,80,1664]{2,1,0:T(8,128)(2,1)} %get-tuple-element.64), channel_id=1, source_target_pairs={{0,16},{8,24},{16,0},{24,8},{1,17},{9,25},{17,1},{25,9},{2,18},{10... | collective-permute-start | bytes 3194888 | tf_op jit(solution)/shard_map/ppermute | solution.py:34
  88.2 29.5 %collective-permute-start.11 = (bf16[4,80,1664]{2,1,0:T(8,128)(2,1)}, bf16[4,80,1664]{2,1,0:T(8,128)(2,1)S(1)}, u32[]{:S(2)}, u32[]{:S(2)}) collective-permute-start(bf16[4,80,1664]{2,1,0:T(8,128)(2,1)} %get-tuple-element.65), channel_id=1, source_target_pairs={{0,64},{32,96},{64,0},{96,32},{1,65},{33,97},{65,1},{97,33},{2,66}... | collective-permute-start | bytes 3194888 | tf_op jit(solution)/shard_map/ppermute | solution.py:34
  89.1 50.0 %collective-permute-start.6 = (bf16[4,80,1664]{2,1,0:T(8,128)(2,1)}, bf16[4,80,1664]{2,1,0:T(8,128)(2,1)S(1)}, u32[]{:S(2)}, u32[]{:S(2)}) collective-permute-start(bf16[4,80,1664]{2,1,0:T(8,128)(2,1)} %get-tuple-element.60), channel_id=1, source_target_pairs={{0,96},{32,0},{64,32},{96,64},{1,97},{33,1},{65,33},{97,65},{2,98}... | collective-permute-start | bytes 3194888 | tf_op jit(solution)/shard_map/ppermute | solution.py:34
  89.5 52.8 %collective-permute-start.7 = (bf16[4,80,1664]{2,1,0:T(8,128)(2,1)}, bf16[4,80,1664]{2,1,0:T(8,128)(2,1)}, u32[]{:S(2)}, u32[]{:S(2)}) collective-permute-start(bf16[4,80,1664]{2,1,0:T(8,128)(2,1)} %get-tuple-element.61), channel_id=1, source_target_pairs={{0,32},{32,64},{64,96},{96,0},{1,33},{33,65},{65,97},{97,1},{2,34}... | collective-permute-start | bytes 3194888 | tf_op jit(solution)/shard_map/ppermute | solution.py:34
  91.1 51.2 %collective-permute-start.8 = (bf16[4,80,1664]{2,1,0:T(8,128)(2,1)}, bf16[4,80,1664]{2,1,0:T(8,128)(2,1)}, u32[]{:S(2)}, u32[]{:S(2)}) collective-permute-start(bf16[4,80,1664]{2,1,0:T(8,128)(2,1)} %get-tuple-element.62), channel_id=1, source_target_pairs={{0,24},{8,0},{16,8},{24,16},{1,25},{9,1},{17,9},{25,17},{2,26},{10... | collective-permute-start | bytes 3194888 | tf_op jit(solution)/shard_map/ppermute | solution.py:34
  110.0 32.3 %collective-permute-start.9 = (bf16[4,80,1664]{2,1,0:T(8,128)(2,1)}, bf16[4,80,1664]{2,1,0:T(8,128)(2,1)}, u32[]{:S(2)}, u32[]{:S(2)}) collective-permute-start(bf16[4,80,1664]{2,1,0:T(8,128)(2,1)} %get-tuple-element.63), channel_id=1, source_target_pairs={{0,8},{8,16},{16,24},{24,0},{1,9},{9,17},{17,25},{25,1},{2,10},{10... | collective-permute-start | bytes 3194888 | tf_op jit(solution)/shard_map/ppermute | solution.py:34
  157.0 20.4 %collective-permute-start.14 = (bf16[400,512]{1,0:T(8,128)(2,1)}, bf16[400,512]{1,0:T(8,128)(2,1)S(1)}, u32[]{:S(2)}, u32[]{:S(2)}) collective-permute-start(bf16[400,512]{1,0:T(8,128)(2,1)} %get-tuple-element.68), channel_id=1, source_target_pairs={{0,6},{2,0},{4,2},{6,4},{1,7},{3,1},{5,3},{7,5},{8,14},{10,8},{12,... | collective-permute-start | bytes 1228808 | tf_op jit(solution)/shard_map/ppermute | solution.py:34
  160.0 20.7 %collective-permute-start.15 = (bf16[400,512]{1,0:T(8,128)(2,1)}, bf16[400,512]{1,0:T(8,128)(2,1)S(1)}, u32[]{:S(2)}, u32[]{:S(2)}) collective-permute-start(bf16[400,512]{1,0:T(8,128)(2,1)} %get-tuple-element.69), channel_id=1, source_target_pairs={{0,2},{2,4},{4,6},{6,0},{1,3},{3,5},{5,7},{7,1},{8,10},{10,12},{12... | collective-permute-start | bytes 1228808 | tf_op jit(solution)/shard_map/ppermute | solution.py:34
  160.0 20.7 %collective-permute-start.16 = (bf16[400,512]{1,0:T(8,128)(2,1)}, bf16[400,512]{1,0:T(8,128)(2,1)S(1)}, u32[]{:S(2)}, u32[]{:S(2)}) collective-permute-start(bf16[400,512]{1,0:T(8,128)(2,1)} %get-tuple-element.70), channel_id=1, source_target_pairs={{0,4},{2,6},{4,0},{6,2},{1,5},{3,7},{5,1},{7,3},{8,12},{10,14},{12... | collective-permute-start | bytes 1228808 | tf_op jit(solution)/shard_map/ppermute | solution.py:34
  186.4 25.8 %all-to-all-start = ((bf16[64,16,640]{2,1,0:T(8,128)(2,1)}), bf16[64,16,640]{2,1,0:T(8,128)(2,1)S(1)}, u32[]{:S(2)}, u32[]{:S(2)}) async-start(bf16[64,16,640]{2,1,0:T(8,128)(2,1)} %get-tuple-element.74), calls=%async_computation | async-start | bytes 2621440 | tf_op jit(solution)/shard_map/all_to_all | solution.py:457
  192.3 92.2 %all-gather.11.cloned.1.call-start = ((), (), s32[]{:S(2)}) async-start(), calls=%async_computation.3 | async-start | bytes 1064960 | tf_op jit(solution)/shard_map/all_gather | solution.py:461
  192.3 29.0 %collective-permute-start.18 = (bf16[400,512]{1,0:T(8,128)(2,1)S(1)}, bf16[400,512]{1,0:T(8,128)(2,1)S(1)}, u32[]{:S(2)}, u32[]{:S(2)}) collective-permute-start(bf16[400,512]{1,0:T(8,128)(2,1)S(1)} %copy-done.8), channel_id=1, source_target_pairs={{0,24},{8,0},{16,8},{24,16},{1,25},{9,1},{17,9},{25,17},{2,26},{10... | collective-permute-start | bytes 1228808 | tf_op jit(solution)/shard_map/ppermute | solution.py:34
  215.4 18.4 %collective-permute-start.19 = (bf16[400,512]{1,0:T(8,128)(2,1)S(1)}, bf16[400,512]{1,0:T(8,128)(2,1)S(1)}, u32[]{:S(2)}, u32[]{:S(2)}) collective-permute-start(bf16[400,512]{1,0:T(8,128)(2,1)S(1)} %copy-done.8), channel_id=1, source_target_pairs={{0,8},{8,16},{16,24},{24,0},{1,9},{9,17},{17,25},{25,1},{2,10},{10... | collective-permute-start | bytes 1228808 | tf_op jit(solution)/shard_map/ppermute | solution.py:34
  218.7 15.5 %collective-permute-start.21 = (bf16[400,512]{1,0:T(8,128)(2,1)S(1)}, bf16[400,512]{1,0:T(8,128)(2,1)S(1)}, u32[]{:S(2)}, u32[]{:S(2)}) collective-permute-start(bf16[400,512]{1,0:T(8,128)(2,1)S(1)} %copy-done.7), channel_id=1, source_target_pairs={{0,2},{2,4},{4,6},{6,0},{1,3},{3,5},{5,7},{7,1},{8,10},{10,12},{12... | collective-permute-start | bytes 1228808 | tf_op jit(solution)/shard_map/ppermute | solution.py:34
  269.6 18.4 %collective-permute-start.31 = (bf16[80,512]{1,0:T(8,128)(2,1)}, bf16[80,512]{1,0:T(8,128)(2,1)S(1)}, u32[]{:S(2)}, u32[]{:S(2)}) collective-permute-start(bf16[80,512]{1,0:T(8,128)(2,1)} %get-tuple-element.88), channel_id=1, source_target_pairs={{0,32},{32,64},{64,96},{96,0},{1,33},{33,65},{65,97},{97,1},{2,34}... | collective-permute-start | bytes 245768 | tf_op jit(solution)/shard_map/ppermute | solution.py:34
  271.0 17.0 %collective-permute-start.32 = (bf16[80,512]{1,0:T(8,128)(2,1)}, bf16[80,512]{1,0:T(8,128)(2,1)S(1)}, u32[]{:S(2)}, u32[]{:S(2)}) collective-permute-start(bf16[80,512]{1,0:T(8,128)(2,1)} %get-tuple-element.89), channel_id=1, source_target_pairs={{0,24},{8,0},{16,8},{24,16},{1,25},{9,1},{17,9},{25,17},{2,26},{10... | collective-permute-start | bytes 245768 | tf_op jit(solution)/shard_map/ppermute | solution.py:34
  (52 other events, 485.5 us)
Sparse Core Ops, SparseCore 0:
  10.1 69.2 all-gather.6
  81.6 58.0 all-gather.8
  215.5 68.8 all-gather.10

commit v4 on v3

--- a/solution.py
+++ b/solution.py
@@ -330,7 +330,7 @@
     return [list(outs[:4]), list(outs[4:])]
 
 
-def owner_kernel(me_ref, got_ref, ranks_ref, mine_ref, scores_ref):
+def owner_kernel(me_ref, got_ref, ranks_ref, _, mine_ref, scores_ref):
     total = jnp.sum(got_ref[...].astype(f32), axis=0)
     row = me_ref[0] * 8 + lax.broadcasted_iota(jnp.int32, (8, 128), 0)
     lane = lax.broadcasted_iota(jnp.int32, (8, 128), 1)
@@ -349,19 +349,19 @@
         gram = total[8 * l : 8 * l + 8, 0:RANK]
         corrected = jnp.where(my_rows == ranks_ref[l : l + 1, :], 1.5 - scale * my_diag, -scale * gram)
         owned.append(jnp.concatenate([corrected / rms, total[8 * l : 8 * l + 8, RANK:KS]], 1))
-    mine_ref[...] = jnp.concatenate(owned, 0).astype(bf16)
+    mine_ref[...] = jnp.broadcast_to(jnp.concatenate(owned, 0).astype(bf16)[None], (N, 16, KS))
     scores_ref[...] = scores / FF
 
 
-def owner_rows(me, got, ranks):
+def owner_rows(me, got, ranks, earlier):
     return pl.pallas_call(
         owner_kernel,
-        in_specs=[SMEM, INNER, INNER],
+        in_specs=[SMEM, INNER, INNER, HBM],
         out_specs=[INNER, INNER],
-        out_shape=[jax.ShapeDtypeStruct((16, KS), bf16), jax.ShapeDtypeStruct((4, 128), f32)],
+        out_shape=[jax.ShapeDtypeStruct((N, 16, KS), bf16), jax.ShapeDtypeStruct((4, 128), f32)],
         compiler_params=params(),
         cost_estimate=cost(2_500_000),
-    )(me, got, ranks)
+    )(me, got, ranks, earlier)
 
 
 def moments_kernel(rows_ref, sk0_ref, sk1_ref, one_ref, two_ref, basis_ref, first_ref, second_ref, factor_ref):
@@ -457,8 +457,8 @@
     got = lax.all_to_all(send, AX, 0, 0, tiled=True)
     sks = permute_stage([[sk] * 4 for sk in sketched], 2)
     me = (16 * pos[0] + 4 * pos[1] + pos[2])[None]
-    mine, scores = owner_rows(me, got, rank_lists)
-    everyone = lax.all_gather(mine, AX, axis=0)
+    mine, scores = owner_rows(me, got, rank_lists, sks[1][1])
+    everyone = lax.all_to_all(mine, AX, 0, 0, tiled=True)
     basis, first, second_out, factor = moments(everyone, sketched, first_moment, second_moment)
     back = shift_back(back_products(pos, got1, got2, sks), 0)
     back = shift_back(reduce_stage(back), 1)

time: 298 us -> 290 us (0.973)
  waiting for transfers between devices: 159 us -> 139 us
  starting transfers between devices: 63.9 us -> 75.7 us
    all_to_all x1, waiting for transfers between devices: 17 us -> 0.01 us  [shards(): got = lax.all_to_all(send, AX, 0, 0, tiled=True)]
    all_to_all x0 -> x1, starting transfers between devices: none -> 8.72 us  [shards(): everyone = lax.all_to_all(mine, AX, 0, 0, tiled=True)]
    all_gather x1 -> x0, waiting for transfers between devices: 5.51 us -> none  [shards(): everyone = lax.all_gather(mine, AX, axis=0)]
  transfers between devices with their start and end apart: 41 -> 41, of which waited for: 19 -> 16; matrix products, arithmetic and copies ran while one was open for 1% -> 1% of each run, Pallas kernels for 11% -> 12%
where the time goes in v4:
time: 290 us
  waiting for transfers between devices  139 us (48%)
  starting transfers between devices  75.7 us (26%)
  Pallas kernels  53.8 us (19%)
  between operations  14.4 us (5%)
  local copies, waits for them, and re-layouts  4.64 us (2%)
    ppermute x36, waiting for transfers between devices, shifted(): return lax.ppermute(x, axis, [(s, (s - k) % 4) for s in range(4)])  138 us
    ppermute x36, starting transfers between devices, shifted(): return lax.ppermute(x, axis, [(s, (s - k) % 4) for s in range(4)])  60.8 us
    pallas_call x1, Pallas kernels, panel_products(): pl.pallas_call(panel_kernel, in_specs=[SMEM] + [HBM] * 16, out_specs=[HBM...  12.5 us
    pallas_call x1, Pallas kernels, back_products(): pl.pallas_call(back_kernel, in_specs=[SMEM] + [HBM] * 22, out_specs=[HBM]...  11 us
    all_to_all x1, starting transfers between devices, shards(): everyone = lax.all_to_all(mine, AX, 0, 0, tiled=True)  8.72 us
    pallas_call x1, Pallas kernels, pack(): pl.pallas_call(pack_kernel, grid=(4,), in_specs=[SMEM, pl.BlockSpec((NL,...  7.84 us
    pallas_call x1, Pallas kernels, second(): pl.pallas_call(second_kernel, in_specs=[SMEM] + [HBM] * 8, out_specs=[HBM...  6.27 us
    all_to_all x1, starting transfers between devices, shards(): got = lax.all_to_all(send, AX, 0, 0, tiled=True)  6.11 us
  transfers between devices with their start and end apart: 41, of which 16 were waited for; matrix products, arithmetic and copies ran while one was open for 1% of the time, Pallas kernels for 12%

profile of v4, /device:TPU:0, one launch (start us, length us, event | category | flops | bytes accessed | tf_op | source)
XLA Modules:
  0.0 289.8 jit_solution(2866018787815569267)
XLA Ops:
  8.5 7.8 %shard_map.101 = (bf16[4,80,1664]{2,1,0:T(8,128)(2,1)}, bf16[4,80,1664]{2,1,0:T(8,128)(2,1)}, bf16[4,80,1664]{2,1,0:T(8,128)(2,1)}, bf16[4,80,1664]{2,1,0:T(8,12...) custom-call(s32[3]{0:T(128)} %pad_add_fusion.pos_ref, ...), custom_call_target="tpu_custom_call" | custom-call | bytes 17000000 | tf_op jit(solution)/shard_map/pallas_call | solution.py:77
  16.4 3.2 %collective-permute-start = (bf16[4,80,1664]{2,1,0:T(8,128)(2,1)}, bf16[4,80,1664]{2,1,0:T(8,128)(2,1)S(1)}, u32[]{:S(2)}, u32[]{:S(2)}) collective-permute-start(bf16[4,80,1664]{2,1,0:T(8,128)(2,1)} %get-tuple-element.52), channel_id=1, source_target_pairs={{0,6},{2,0},{4,2},{6,4},{1,7},{3,1},{5,3},{7,5},{8,14},{10,8},{12,... | collective-permute-start | bytes 3194888 | tf_op jit(solution)/shard_map/ppermute | solution.py:34
  19.6 4.0 %collective-permute-start.2 = (bf16[4,80,1664]{2,1,0:T(8,128)(2,1)}, bf16[4,80,1664]{2,1,0:T(8,128)(2,1)S(1)}, u32[]{:S(2)}, u32[]{:S(2)}) collective-permute-start(bf16[4,80,1664]{2,1,0:T(8,128)(2,1)} %get-tuple-element.54), channel_id=1, source_target_pairs={{0,96},{32,0},{64,32},{96,64},{1,97},{33,1},{65,33},{97,65},{2,98}... | collective-permute-start | bytes 3194888 | tf_op jit(solution)/shard_map/ppermute | solution.py:34
  25.4 17.3 %collective-permute-done.refs_0_ = bf16[4,80,1664]{2,1,0:T(8,128)(2,1)S(1)} collective-permute-done((bf16[4,80,1664]{2,1,0:T(8,128)(2,1)}, bf16[4,80,1664]{2,1,0:T(8,128)(2,1)S(1)}, u32[]{:S(2)}, u32[]{:S(2)}) %collective-permute-start) | collective-permute-done | bytes 1064992 | tf_op jit(solution)/shard_map/ppermute | solution.py:34
  46.0 29.3 %collective-permute-done.2.refs_2_ = bf16[4,80,1664]{2,1,0:T(8,128)(2,1)S(1)} collective-permute-done((bf16[4,80,1664]{2,1,0:T(8,128)(2,1)}, bf16[4,80,1664]{2,1,0:T(8,128)(2,1)S(1)}, u32[]{:S(2)}, u32[]{:S(2)}) %collective-permute-start.2) | collective-permute-done | bytes 1064992 | tf_op jit(solution)/shard_map/ppermute | solution.py:34
  75.2 3.8 %collective-permute-done.3.refs_3_ = bf16[4,80,1664]{2,1,0:T(8,128)(2,1)} collective-permute-done((bf16[4,80,1664]{2,1,0:T(8,128)(2,1)}, bf16[4,80,1664]{2,1,0:T(8,128)(2,1)}, u32[]{:S(2)}, u32[]{:S(2)}) %collective-permute-start.3) | collective-permute-done | bytes 1064992 | tf_op jit(solution)/shard_map/ppermute | solution.py:34
  79.1 6.3 %shard_map.102 = (bf16[4,80,1664]{2,1,0:T(8,128)(2,1)}, bf16[4,80,1664]{2,1,0:T(8,128)(2,1)}, bf16[4,80,1664]{2,1,0:T(8,128)(2,1)}, bf16[4,80,1664]{2,1,0:T(8,12...) custom-call(s32[3]{0:T(128)} %pad_add_fusion.pos_ref, bf16[4,80,1664]{2,1,0:T(8,128)(2,1)} %copy-done, ...), custom_call_target="tpu_custom_call" | custom-call | bytes 13000000 | tf_op jit(solution)/shard_map/pallas_call | solution.py:138
  92.2 17.7 %collective-permute-done.10.refs_12_ = bf16[4,80,1664]{2,1,0:T(8,128)(2,1)S(1)} collective-permute-done((bf16[4,80,1664]{2,1,0:T(8,128)(2,1)}, bf16[4,80,1664]{2,1,0:T(8,128)(2,1)S(1)}, u32[]{:S(2)}, u32[]{:S(2)}) %collective-permute-start.10) | collective-permute-done | bytes 1064992 | tf_op jit(solution)/shard_map/ppermute | solution.py:34
  109.9 4.8 %collective-permute-start.9 = (bf16[4,80,1664]{2,1,0:T(8,128)(2,1)}, bf16[4,80,1664]{2,1,0:T(8,128)(2,1)}, u32[]{:S(2)}, u32[]{:S(2)}) collective-permute-start(bf16[4,80,1664]{2,1,0:T(8,128)(2,1)} %get-tuple-element.63), channel_id=1, source_target_pairs={{0,8},{8,16},{16,24},{24,0},{1,9},{9,17},{17,25},{25,1},{2,10},{10... | collective-permute-start | bytes 3194888 | tf_op jit(solution)/shard_map/ppermute | solution.py:34
  117.6 21.3 %collective-permute-done.6.refs_8_ = bf16[4,80,1664]{2,1,0:T(8,128)(2,1)S(1)} collective-permute-done((bf16[4,80,1664]{2,1,0:T(8,128)(2,1)}, bf16[4,80,1664]{2,1,0:T(8,128)(2,1)S(1)}, u32[]{:S(2)}, u32[]{:S(2)}) %collective-permute-start.6) | collective-permute-done | bytes 1064992 | tf_op jit(solution)/shard_map/ppermute | solution.py:34
  138.9 3.4 %collective-permute-done.7.refs_9_ = bf16[4,80,1664]{2,1,0:T(8,128)(2,1)} collective-permute-done((bf16[4,80,1664]{2,1,0:T(8,128)(2,1)}, bf16[4,80,1664]{2,1,0:T(8,128)(2,1)}, u32[]{:S(2)}, u32[]{:S(2)}) %collective-permute-start.7) | collective-permute-done | bytes 1064992 | tf_op jit(solution)/shard_map/ppermute | solution.py:34
  142.3 12.5 %shard_map.103 = (bf16[400,512]{1,0:T(8,128)(2,1)}, bf16[400,512]{1,0:T(8,128)(2,1)}, bf16[400,512]{1,0:T(8,128)(2,1)}, bf16[400,512]{1,0:T(8,128)(2,1)}, bf16[4...) custom-call(s32[3]{0:T(128)} %pad_add_fusion.pos_ref, ...), custom_call_target="tpu_custom_call" | custom-call | flops 4400000000 | bytes 15000000 | tf_op jit(solution)/shard_map/pallas_call | solution.py:218
  161.3 5.2 %collective-permute-done.12.refs_0_ = bf16[400,512]{1,0:T(8,128)(2,1)S(1)} collective-permute-done((bf16[400,512]{1,0:T(8,128)(2,1)}, bf16[400,512]{1,0:T(8,128)(2,1)S(1)}, u32[]{:S(2)}, u32[]{:S(2)}) %collective-permute-start.12) | collective-permute-done | bytes 409632 | tf_op jit(solution)/shard_map/ppermute | solution.py:34
  168.5 8.7 %collective-permute-done.14.refs_2_ = bf16[400,512]{1,0:T(8,128)(2,1)S(1)} collective-permute-done((bf16[400,512]{1,0:T(8,128)(2,1)}, bf16[400,512]{1,0:T(8,128)(2,1)S(1)}, u32[]{:S(2)}, u32[]{:S(2)}) %collective-permute-start.14) | collective-permute-done | bytes 409632 | tf_op jit(solution)/shard_map/ppermute | solution.py:34
  177.2 3.3 %collective-permute-done.15.refs_3_ = bf16[400,512]{1,0:T(8,128)(2,1)S(1)} collective-permute-done((bf16[400,512]{1,0:T(8,128)(2,1)}, bf16[400,512]{1,0:T(8,128)(2,1)S(1)}, u32[]{:S(2)}, u32[]{:S(2)}) %collective-permute-start.15) | collective-permute-done | bytes 409632 | tf_op jit(solution)/shard_map/ppermute | solution.py:34
  181.6 4.6 %shard_map.104 = (bf16[400,512]{1,0:T(8,128)(2,1)}, bf16[400,512]{1,0:T(8,128)(2,1)}, bf16[64,16,640]{2,1,0:T(8,128)(2,1)}) custom-call(bf16[400,512]{1,0:T(8,128)(2,1)} %copy-done.11, bf16[400,512]{1,0:T(8,128)(2,1)} %copy-done.12, bf16[400,512]{1,0:T(8,128)(2,1)} %copy-done.13, bf16[400,512]{1,0:T(8,128)(2,1)} %copy-done.14, bf16[400,512]{1,0:T(8,128)(2,1)} %copy-done.15, ...), custom_call_target="tpu_custom_call" | custom-call | flops 1000000000 | bytes 7000000 | tf_op jit(solution)/shard_map/pallas_call | solution.py:263
  186.2 6.1 %all-to-all-start = ((bf16[64,16,640]{2,1,0:T(8,128)(2,1)}), bf16[64,16,640]{2,1,0:T(8,128)(2,1)S(1)}, u32[]{:S(2)}, u32[]{:S(2)}) async-start(bf16[64,16,640]{2,1,0:T(8,128)(2,1)} %get-tuple-element.74), calls=%async_computation | async-start | bytes 2621440 | tf_op jit(solution)/shard_map/all_to_all | solution.py:457
  200.1 14.9 %collective-permute-done.18._.refs_14_ = bf16[400,512]{1,0:T(8,128)(2,1)S(1)} collective-permute-done((bf16[400,512]{1,0:T(8,128)(2,1)S(1)}, bf16[400,512]{1,0:T(8,128)(2,1)S(1)}, u32[]{:S(2)}, u32[]{:S(2)}) %collective-permute-start.18) | collective-permute-done | bytes 409632 | tf_op jit(solution)/shard_map/ppermute | solution.py:34
  221.4 8.7 %all-to-all-start.1 = ((bf16[64,16,512]{2,1,0:T(8,128)(2,1)}), bf16[64,16,512]{2,1,0:T(8,128)(2,1)S(1)}, u32[]{:S(2)}, u32[]{:S(2)}) async-start(bf16[64,16,512]{2,1,0:T(8,128)(2,1)} %get-tuple-element.76), calls=%async_computation.1 | async-start | bytes 2097152 | tf_op jit(solution)/shard_map/all_to_all | solution.py:461
  230.2 11.0 %shard_map.107 = (bf16[4,80,512]{2,1,0:T(8,128)(2,1)}, bf16[4,80,512]{2,1,0:T(8,128)(2,1)}, bf16[4,80,512]{2,1,0:T(8,128)(2,1)}, bf16[4,80,512]{2,1,0:T(8,128)(2...) custom-call(s32[3]{0:T(128)} %pad_add_fusion.pos_ref, ...), custom_call_target="tpu_custom_call" | custom-call | flops 4400000000 | bytes 16000000 | tf_op jit(solution)/shard_map/pallas_call | solution.py:314
  244.0 2.9 %collective-permute-start.26 = (bf16[4,80,512]{2,1,0:T(8,128)(2,1)}, bf16[4,80,512]{2,1,0:T(8,128)(2,1)S(1)}, u32[]{:S(2)}, u32[]{:S(2)}) collective-permute-start(bf16[4,80,512]{2,1,0:T(8,128)(2,1)} %get-tuple-element.81), channel_id=1, source_target_pairs={{0,96},{32,0},{64,32},{96,64},{1,97},{33,1},{65,33},{97,65},{2,98}... | collective-permute-start | bytes 983048 | tf_op jit(solution)/shard_map/ppermute | solution.py:34
  249.5 2.9 %collective-permute-start.29 = (bf16[4,80,512]{2,1,0:T(8,128)(2,1)}, bf16[4,80,512]{2,1,0:T(8,128)(2,1)S(1)}, u32[]{:S(2)}, u32[]{:S(2)}) collective-permute-start(bf16[4,80,512]{2,1,0:T(8,128)(2,1)} %get-tuple-element.84), channel_id=1, source_target_pairs={{0,4},{2,6},{4,0},{6,2},{1,5},{3,7},{5,1},{7,3},{8,12},{10,14},{12... | collective-permute-start | bytes 983048 | tf_op jit(solution)/shard_map/ppermute | solution.py:34
  252.4 7.1 %collective-permute-done.25.refs_1_ = bf16[4,80,512]{2,1,0:T(8,128)(2,1)S(1)} collective-permute-done((bf16[4,80,512]{2,1,0:T(8,128)(2,1)}, bf16[4,80,512]{2,1,0:T(8,128)(2,1)S(1)}, u32[]{:S(2)}, u32[]{:S(2)}) %collective-permute-start.25) | collective-permute-done | bytes 327712 | tf_op jit(solution)/shard_map/ppermute | solution.py:34
  275.8 3.6 %shard_map.106 = (bf16[2,400,256]{2,1,0:T(8,128)(2,1)}, f32[2,80,256]{2,1,0:T(8,128)}, f32[2,80,256]{2,1,0:T(8,128)}, bf16[2,512,256]{2,1,0:T(8,128)(2,1)}) custom-call(bf16[64,16,512]{2,1,0:T(8,128)(2,1)} %copy-done.7, bf16[400,512]{1,0:T(8,128)(2,1)} %get-tuple-element.77.sk0_ref.refs_20_, bf16[400,512]{1,0:T(8,128)(2,1)} %get-tuple-element.75.sk1_ref.refs_21_, ...), custom_call_target="tpu_custom_call" | custom-call | flops 500000000 | bytes 4000000 | tf_op jit(solution)/shard_map/pallas_call | solution.py:385
  (134 shorter events, 65.0 us)
Async XLA Ops:
  7.2 135.1 %all-gather.5.cloned.1.call-start = ((), (), s32[]{:S(2)}) async-start(), calls=%async_computation.2 | async-start | bytes 1392640 | tf_op jit(solution)/shard_map/all_gather | solution.py:450
  7.9 134.4 %all-gather.7.cloned.1.call-start = ((), (), s32[]{:S(2)}) async-start(), calls=%async_computation.3 | async-start | bytes 1392640 | tf_op jit(solution)/shard_map/all_gather | solution.py:450
  16.4 26.3 %collective-permute-start = (bf16[4,80,1664]{2,1,0:T(8,128)(2,1)}, bf16[4,80,1664]{2,1,0:T(8,128)(2,1)S(1)}, u32[]{:S(2)}, u32[]{:S(2)}) collective-permute-start(bf16[4,80,1664]{2,1,0:T(8,128)(2,1)} %get-tuple-element.52), channel_id=1, source_target_pairs={{0,6},{2,0},{4,2},{6,4},{1,7},{3,1},{5,3},{7,5},{8,14},{10,8},{12,... | collective-permute-start | bytes 3194888 | tf_op jit(solution)/shard_map/ppermute | solution.py:34
  19.6 26.4 %collective-permute-start.1 = (bf16[4,80,1664]{2,1,0:T(8,128)(2,1)}, bf16[4,80,1664]{2,1,0:T(8,128)(2,1)S(1)}, u32[]{:S(2)}, u32[]{:S(2)}) collective-permute-start(bf16[4,80,1664]{2,1,0:T(8,128)(2,1)} %get-tuple-element.53), channel_id=1, source_target_pairs={{0,2},{2,4},{4,6},{6,0},{1,3},{3,5},{5,7},{7,1},{8,10},{10,12},{12... | collective-permute-start | bytes 3194888 | tf_op jit(solution)/shard_map/ppermute | solution.py:34
  19.6 55.7 %collective-permute-start.2 = (bf16[4,80,1664]{2,1,0:T(8,128)(2,1)}, bf16[4,80,1664]{2,1,0:T(8,128)(2,1)S(1)}, u32[]{:S(2)}, u32[]{:S(2)}) collective-permute-start(bf16[4,80,1664]{2,1,0:T(8,128)(2,1)} %get-tuple-element.54), channel_id=1, source_target_pairs={{0,96},{32,0},{64,32},{96,64},{1,97},{33,1},{65,33},{97,65},{2,98}... | collective-permute-start | bytes 3194888 | tf_op jit(solution)/shard_map/ppermute | solution.py:34
  23.6 55.5 %collective-permute-start.3 = (bf16[4,80,1664]{2,1,0:T(8,128)(2,1)}, bf16[4,80,1664]{2,1,0:T(8,128)(2,1)}, u32[]{:S(2)}, u32[]{:S(2)}) collective-permute-start(bf16[4,80,1664]{2,1,0:T(8,128)(2,1)} %get-tuple-element.55), channel_id=1, source_target_pairs={{0,32},{32,64},{64,96},{96,0},{1,33},{33,65},{65,97},{97,1},{2,34}... | collective-permute-start | bytes 3194888 | tf_op jit(solution)/shard_map/ppermute | solution.py:34
  23.6 55.5 %collective-permute-start.4 = (bf16[4,80,1664]{2,1,0:T(8,128)(2,1)}, bf16[4,80,1664]{2,1,0:T(8,128)(2,1)}, u32[]{:S(2)}, u32[]{:S(2)}) collective-permute-start(bf16[4,80,1664]{2,1,0:T(8,128)(2,1)} %get-tuple-element.56), channel_id=1, source_target_pairs={{0,64},{32,96},{64,0},{96,32},{1,65},{33,97},{65,1},{97,33},{2,66}... | collective-permute-start | bytes 3194888 | tf_op jit(solution)/shard_map/ppermute | solution.py:34
  42.6 36.4 %collective-permute-start.5 = (bf16[4,80,1664]{2,1,0:T(8,128)(2,1)}, bf16[4,80,1664]{2,1,0:T(8,128)(2,1)}, u32[]{:S(2)}, u32[]{:S(2)}) collective-permute-start(bf16[4,80,1664]{2,1,0:T(8,128)(2,1)} %get-tuple-element.57), channel_id=1, source_target_pairs={{0,4},{2,6},{4,0},{6,2},{1,5},{3,7},{5,1},{7,3},{8,12},{10,14},{12... | collective-permute-start | bytes 3194888 | tf_op jit(solution)/shard_map/ppermute | solution.py:34
  85.4 24.5 %collective-permute-start.10 = (bf16[4,80,1664]{2,1,0:T(8,128)(2,1)}, bf16[4,80,1664]{2,1,0:T(8,128)(2,1)S(1)}, u32[]{:S(2)}, u32[]{:S(2)}) collective-permute-start(bf16[4,80,1664]{2,1,0:T(8,128)(2,1)} %get-tuple-element.64), channel_id=1, source_target_pairs={{0,16},{8,24},{16,0},{24,8},{1,17},{9,25},{17,1},{25,9},{2,18},{10... | collective-permute-start | bytes 3194888 | tf_op jit(solution)/shard_map/ppermute | solution.py:34
  88.1 29.5 %collective-permute-start.11 = (bf16[4,80,1664]{2,1,0:T(8,128)(2,1)}, bf16[4,80,1664]{2,1,0:T(8,128)(2,1)S(1)}, u32[]{:S(2)}, u32[]{:S(2)}) collective-permute-start(bf16[4,80,1664]{2,1,0:T(8,128)(2,1)} %get-tuple-element.65), channel_id=1, source_target_pairs={{0,64},{32,96},{64,0},{96,32},{1,65},{33,97},{65,1},{97,33},{2,66}... | collective-permute-start | bytes 3194888 | tf_op jit(solution)/shard_map/ppermute | solution.py:34
  89.0 49.8 %collective-permute-start.6 = (bf16[4,80,1664]{2,1,0:T(8,128)(2,1)}, bf16[4,80,1664]{2,1,0:T(8,128)(2,1)S(1)}, u32[]{:S(2)}, u32[]{:S(2)}) collective-permute-start(bf16[4,80,1664]{2,1,0:T(8,128)(2,1)} %get-tuple-element.60), channel_id=1, source_target_pairs={{0,96},{32,0},{64,32},{96,64},{1,97},{33,1},{65,33},{97,65},{2,98}... | collective-permute-start | bytes 3194888 | tf_op jit(solution)/shard_map/ppermute | solution.py:34
  89.5 52.7 %collective-permute-start.7 = (bf16[4,80,1664]{2,1,0:T(8,128)(2,1)}, bf16[4,80,1664]{2,1,0:T(8,128)(2,1)}, u32[]{:S(2)}, u32[]{:S(2)}) collective-permute-start(bf16[4,80,1664]{2,1,0:T(8,128)(2,1)} %get-tuple-element.61), channel_id=1, source_target_pairs={{0,32},{32,64},{64,96},{96,0},{1,33},{33,65},{65,97},{97,1},{2,34}... | collective-permute-start | bytes 3194888 | tf_op jit(solution)/shard_map/ppermute | solution.py:34
  91.0 51.2 %collective-permute-start.8 = (bf16[4,80,1664]{2,1,0:T(8,128)(2,1)}, bf16[4,80,1664]{2,1,0:T(8,128)(2,1)}, u32[]{:S(2)}, u32[]{:S(2)}) collective-permute-start(bf16[4,80,1664]{2,1,0:T(8,128)(2,1)} %get-tuple-element.62), channel_id=1, source_target_pairs={{0,24},{8,0},{16,8},{24,16},{1,25},{9,1},{17,9},{25,17},{2,26},{10... | collective-permute-start | bytes 3194888 | tf_op jit(solution)/shard_map/ppermute | solution.py:34
  109.9 32.3 %collective-permute-start.9 = (bf16[4,80,1664]{2,1,0:T(8,128)(2,1)}, bf16[4,80,1664]{2,1,0:T(8,128)(2,1)}, u32[]{:S(2)}, u32[]{:S(2)}) collective-permute-start(bf16[4,80,1664]{2,1,0:T(8,128)(2,1)} %get-tuple-element.63), channel_id=1, source_target_pairs={{0,8},{8,16},{16,24},{24,0},{1,9},{9,17},{17,25},{25,1},{2,10},{10... | collective-permute-start | bytes 3194888 | tf_op jit(solution)/shard_map/ppermute | solution.py:34
  156.9 20.3 %collective-permute-start.14 = (bf16[400,512]{1,0:T(8,128)(2,1)}, bf16[400,512]{1,0:T(8,128)(2,1)S(1)}, u32[]{:S(2)}, u32[]{:S(2)}) collective-permute-start(bf16[400,512]{1,0:T(8,128)(2,1)} %get-tuple-element.68), channel_id=1, source_target_pairs={{0,6},{2,0},{4,2},{6,4},{1,7},{3,1},{5,3},{7,5},{8,14},{10,8},{12,... | collective-permute-start | bytes 1228808 | tf_op jit(solution)/shard_map/ppermute | solution.py:34
  159.8 20.7 %collective-permute-start.15 = (bf16[400,512]{1,0:T(8,128)(2,1)}, bf16[400,512]{1,0:T(8,128)(2,1)S(1)}, u32[]{:S(2)}, u32[]{:S(2)}) collective-permute-start(bf16[400,512]{1,0:T(8,128)(2,1)} %get-tuple-element.69), channel_id=1, source_target_pairs={{0,2},{2,4},{4,6},{6,0},{1,3},{3,5},{5,7},{7,1},{8,10},{10,12},{12... | collective-permute-start | bytes 1228808 | tf_op jit(solution)/shard_map/ppermute | solution.py:34
  159.8 20.7 %collective-permute-start.16 = (bf16[400,512]{1,0:T(8,128)(2,1)}, bf16[400,512]{1,0:T(8,128)(2,1)S(1)}, u32[]{:S(2)}, u32[]{:S(2)}) collective-permute-start(bf16[400,512]{1,0:T(8,128)(2,1)} %get-tuple-element.70), channel_id=1, source_target_pairs={{0,4},{2,6},{4,0},{6,2},{1,5},{3,7},{5,1},{7,3},{8,12},{10,14},{12... | collective-permute-start | bytes 1228808 | tf_op jit(solution)/shard_map/ppermute | solution.py:34
  186.2 31.6 %all-to-all-start = ((bf16[64,16,640]{2,1,0:T(8,128)(2,1)}), bf16[64,16,640]{2,1,0:T(8,128)(2,1)S(1)}, u32[]{:S(2)}, u32[]{:S(2)}) async-start(bf16[64,16,640]{2,1,0:T(8,128)(2,1)} %get-tuple-element.74), calls=%async_computation | async-start | bytes 2621440 | tf_op jit(solution)/shard_map/all_to_all | solution.py:457
  192.3 22.8 %collective-permute-start.18 = (bf16[400,512]{1,0:T(8,128)(2,1)S(1)}, bf16[400,512]{1,0:T(8,128)(2,1)S(1)}, u32[]{:S(2)}, u32[]{:S(2)}) collective-permute-start(bf16[400,512]{1,0:T(8,128)(2,1)S(1)} %copy-done.10), channel_id=1, source_target_pairs={{0,24},{8,0},{16,8},{24,16},{1,25},{9,1},{17,9},{25,17},{2,26},{10... | collective-permute-start | bytes 1228808 | tf_op jit(solution)/shard_map/ppermute | solution.py:34
  195.1 35.0 %collective-permute-start.19 = (bf16[400,512]{1,0:T(8,128)(2,1)S(1)}, bf16[400,512]{1,0:T(8,128)(2,1)}, u32[]{:S(2)}, u32[]{:S(2)}) collective-permute-start(bf16[400,512]{1,0:T(8,128)(2,1)S(1)} %copy-done.10), channel_id=1, source_target_pairs={{0,8},{8,16},{16,24},{24,0},{1,9},{9,17},{17,25},{25,1},{2,10},{10... | collective-permute-start | bytes 1228808 | tf_op jit(solution)/shard_map/ppermute | solution.py:34
  195.1 35.0 %collective-permute-start.20 = (bf16[400,512]{1,0:T(8,128)(2,1)S(1)}, bf16[400,512]{1,0:T(8,128)(2,1)}, u32[]{:S(2)}, u32[]{:S(2)}) collective-permute-start(bf16[400,512]{1,0:T(8,128)(2,1)S(1)} %copy-done.9), channel_id=1, source_target_pairs={{0,6},{2,0},{4,2},{6,4},{1,7},{3,1},{5,3},{7,5},{8,14},{10,8},{12,... | collective-permute-start | bytes 1228808 | tf_op jit(solution)/shard_map/ppermute | solution.py:34
  197.8 32.3 %collective-permute-start.21 = (bf16[400,512]{1,0:T(8,128)(2,1)S(1)}, bf16[400,512]{1,0:T(8,128)(2,1)}, u32[]{:S(2)}, u32[]{:S(2)}) collective-permute-start(bf16[400,512]{1,0:T(8,128)(2,1)S(1)} %copy-done.9), channel_id=1, source_target_pairs={{0,2},{2,4},{4,6},{6,0},{1,3},{3,5},{5,7},{7,1},{8,10},{10,12},{12... | collective-permute-start | bytes 1228808 | tf_op jit(solution)/shard_map/ppermute | solution.py:34
  197.8 32.3 %collective-permute-start.22 = (bf16[400,512]{1,0:T(8,128)(2,1)S(1)}, bf16[400,512]{1,0:T(8,128)(2,1)}, u32[]{:S(2)}, u32[]{:S(2)}) collective-permute-start(bf16[400,512]{1,0:T(8,128)(2,1)S(1)} %copy-done.9), channel_id=1, source_target_pairs={{0,4},{2,6},{4,0},{6,2},{1,5},{3,7},{5,1},{7,3},{8,12},{10,14},{12... | collective-permute-start | bytes 1228808 | tf_op jit(solution)/shard_map/ppermute | solution.py:34
  221.4 53.5 %all-to-all-start.1 = ((bf16[64,16,512]{2,1,0:T(8,128)(2,1)}), bf16[64,16,512]{2,1,0:T(8,128)(2,1)S(1)}, u32[]{:S(2)}, u32[]{:S(2)}) async-start(bf16[64,16,512]{2,1,0:T(8,128)(2,1)} %get-tuple-element.76), calls=%async_computation.1 | async-start | bytes 2097152 | tf_op jit(solution)/shard_map/all_to_all | solution.py:461
  (48 other events, 442.4 us)
Sparse Core Ops, SparseCore 0:
  10.1 69.2 all-gather.4
  81.5 57.8 all-gather.6

commit v5 on v4

--- a/solution.py
+++ b/solution.py
@@ -25,6 +25,7 @@
 
 ORDERS = (("z", "x", "y"), ("y", "z", "x"))
 ISSUE = ((1, 1), (1, 3), (0, 1), (0, 3), (0, 2), (1, 2))
+FIRST = ((0, 1), (0, 3), (1, 1), (1, 3), (1, 2), (0, 2))
 HBM = pl.BlockSpec(memory_space=pl.ANY)
 SMEM = pl.BlockSpec(memory_space=pltpu.SMEM)
 INNER = pl.BlockSpec(memory_space=pltpu.VMEM)
@@ -87,24 +88,24 @@
     return [list(outs[:4]), list(outs[4:])]
 
 
-def permute_stage(bufs, stage):
+def permute_stage(bufs, stage, order=ISSUE):
     got = [[b[0], None, None, None] for b in bufs]
-    for l, k in ISSUE:
+    for l, k in order:
         got[l][k] = shifted(bufs[l][k], ORDERS[l][stage], k)
     return got
 
 
-def moved(got):
-    return [got[l][k] for l, k in ISSUE]
-
-
-def flat(got):
-    return moved(got) + [got[l][0] for l in range(NL)]
-
-
-def unflat(refs):
+def moved(got, order=ISSUE):
+    return [got[l][k] for l, k in order]
+
+
+def flat(got, order=ISSUE):
+    return moved(got, order) + [got[l][0] for l in range(NL)]
+
+
+def unflat(refs, order=ISSUE):
     got = [[None] * 4 for _ in range(NL)]
-    for (l, k), r in zip(ISSUE, refs):
+    for (l, k), r in zip(order, refs):
         got[l][k] = r
     for l, r in enumerate(refs[6:]):
         got[l][0] = r
@@ -112,7 +113,7 @@
 
 
 def second_kernel(pos_ref, *refs):
-    first = unflat(refs[:8])
+    first = unflat(refs[:8], FIRST)
     outs, scr, sem, sem_out = refs[8:14], refs[14:20], refs[20], refs[21]
     loads = [[] for _ in outs]
     for at, (l, k) in enumerate(ISSUE):
@@ -144,7 +145,7 @@
         + [pltpu.SemaphoreType.DMA((24,)), pltpu.SemaphoreType.DMA((6,))],
         compiler_params=params(),
         cost_estimate=cost(13_000_000),
-    )(pos, *flat(got))
+    )(pos, *flat(got, FIRST))
     bufs = [[None] * 4 for _ in range(NL)]
     for (l, k), o in zip(ISSUE, outs):
         bufs[l][k] = o
@@ -169,7 +170,7 @@
 
 
 def panel_kernel(pos_ref, *refs):
-    first, got = unflat(refs[:8]), unflat(refs[8:14])
+    first, got = unflat(refs[:8], FIRST), unflat(refs[8:14])
     s_ref = refs[14:16]
     outs = refs[16:24]
     x_ref, s_vmem, acc_ref, u_ref, sem, sem_s, sem_out = refs[24:]
@@ -231,7 +232,7 @@
         ],
         compiler_params=params(),
         cost_estimate=cost(15_000_000, 4_400_000_000),
-    )(pos, *flat(got1), *moved(got2), *s)
+    )(pos, *flat(got1, FIRST), *moved(got2), *s)
     return [list(outs[:4]), list(outs[4:])]
 
 
@@ -273,7 +274,7 @@
 
 
 def back_kernel(pos_ref, *refs):
-    first, got = unflat(refs[:8]), unflat(refs[8:14])
+    first, got = unflat(refs[:8], FIRST), unflat(refs[8:14])
     sk_in = unflat(refs[14:22])
     outs = refs[22:30]
     x_ref, sk_ref, t_ref, sem, sem_s, sem_out = refs[30:]
@@ -326,7 +327,7 @@
         ],
         compiler_params=params(),
         cost_estimate=cost(16_000_000, 4_400_000_000),
-    )(pos, *flat(got1), *moved(got2), *flat(sks))
+    )(pos, *flat(got1, FIRST), *moved(got2), *flat(sks))
     return [list(outs[:4]), list(outs[4:])]
 
 
@@ -449,7 +450,7 @@
 def shards(gradients, sketch, rank_lists, old_basis, first_moment, second_moment):
     s_rows = [lax.all_gather(sketch, axes, axis=0) for axes in (("z", "x"), ("z", "y"))]
     pos = jnp.stack([lax.axis_index(a) for a in AX]).astype(jnp.int32)
-    got1 = permute_stage(pack(pos, gradients), 0)
+    got1 = permute_stage(pack(pos, gradients), 0, FIRST)
     got2 = permute_stage(second(pos, got1), 1)
     picker = (lax.broadcasted_iota(jnp.int32, (NL, KS, RANK), 1) == rank_lists[:, None, :]).astype(bf16)
     parts = shift_back(panel_products(pos, got1, got2, s_rows), 2)

time: 290 us -> 289 us (level)
  waiting for transfers between devices: 139 us -> 136 us
where the time goes in v5:
time: 289 us; the launch traced here: 288 us
  waiting for transfers between devices  136 us (47%)
  starting transfers between devices  77.1 us (27%)
  Pallas kernels  53.8 us (19%)
  between operations  14.4 us (5%)
  local copies, waits for them, and re-layouts  4.64 us (2%)
    ppermute x36, waiting for transfers between devices, shifted(): return lax.ppermute(x, axis, [(s, (s - k) % 4) for s in range(4)])  136 us
    ppermute x36, starting transfers between devices, shifted(): return lax.ppermute(x, axis, [(s, (s - k) % 4) for s in range(4)])  61.4 us
    pallas_call x1, Pallas kernels, panel_products(): pl.pallas_call(panel_kernel, in_specs=[SMEM] + [HBM] * 16, out_specs=[HBM...  12.5 us
    pallas_call x1, Pallas kernels, back_products(): pl.pallas_call(back_kernel, in_specs=[SMEM] + [HBM] * 22, out_specs=[HBM]...  11 us
    all_to_all x1, starting transfers between devices, shards(): everyone = lax.all_to_all(mine, AX, 0, 0, tiled=True)  8.72 us
    pallas_call x1, Pallas kernels, pack(): pl.pallas_call(pack_kernel, grid=(4,), in_specs=[SMEM, pl.BlockSpec((NL,...  7.81 us
    all_to_all x1, starting transfers between devices, shards(): got = lax.all_to_all(send, AX, 0, 0, tiled=True)  6.87 us
    pallas_call x1, Pallas kernels, second(): pl.pallas_call(second_kernel, in_specs=[SMEM] + [HBM] * 8, out_specs=[HBM...  6.27 us
  transfers between devices with their start and end apart: 41, of which 16 were waited for; matrix products, arithmetic and copies ran while one was open for 1% of the time, Pallas kernels for 12%

profile of v5, /device:TPU:0, one launch (start us, length us, event | category | flops | bytes accessed | tf_op | source)
XLA Modules:
  0.0 288.4 jit_solution(13834248115851368662)
XLA Ops:
  8.5 7.8 %shard_map.101 = (bf16[4,80,1664]{2,1,0:T(8,128)(2,1)}, bf16[4,80,1664]{2,1,0:T(8,128)(2,1)}, bf16[4,80,1664]{2,1,0:T(8,128)(2,1)}, bf16[4,80,1664]{2,1,0:T(8,12...) custom-call(s32[3]{0:T(128)} %pad_add_fusion.pos_ref, ...), custom_call_target="tpu_custom_call" | custom-call | bytes 17000000 | tf_op jit(solution)/shard_map/pallas_call | solution.py:78
  16.4 4.2 %collective-permute-start = (bf16[4,80,1664]{2,1,0:T(8,128)(2,1)}, bf16[4,80,1664]{2,1,0:T(8,128)(2,1)S(1)}, u32[]{:S(2)}, u32[]{:S(2)}) collective-permute-start(bf16[4,80,1664]{2,1,0:T(8,128)(2,1)} %get-tuple-element.52), channel_id=1, source_target_pairs={{0,96},{32,0},{64,32},{96,64},{1,97},{33,1},{65,33},{97,65},{2,98}... | collective-permute-start | bytes 3194888 | tf_op jit(solution)/shard_map/ppermute | solution.py:35
  20.6 3.0 %collective-permute-start.2 = (bf16[4,80,1664]{2,1,0:T(8,128)(2,1)}, bf16[4,80,1664]{2,1,0:T(8,128)(2,1)S(1)}, u32[]{:S(2)}, u32[]{:S(2)}) collective-permute-start(bf16[4,80,1664]{2,1,0:T(8,128)(2,1)} %get-tuple-element.54), channel_id=1, source_target_pairs={{0,6},{2,0},{4,2},{6,4},{1,7},{3,1},{5,3},{7,5},{8,14},{10,8},{12,... | collective-permute-start | bytes 3194888 | tf_op jit(solution)/shard_map/ppermute | solution.py:35
  25.8 20.9 %collective-permute-done.refs_0_ = bf16[4,80,1664]{2,1,0:T(8,128)(2,1)S(1)} collective-permute-done((bf16[4,80,1664]{2,1,0:T(8,128)(2,1)}, bf16[4,80,1664]{2,1,0:T(8,128)(2,1)S(1)}, u32[]{:S(2)}, u32[]{:S(2)}) %collective-permute-start) | collective-permute-done | bytes 1064992 | tf_op jit(solution)/shard_map/ppermute | solution.py:35
  47.1 8.8 %collective-permute-done.1.refs_1_ = bf16[4,80,1664]{2,1,0:T(8,128)(2,1)S(1)} collective-permute-done((bf16[4,80,1664]{2,1,0:T(8,128)(2,1)}, bf16[4,80,1664]{2,1,0:T(8,128)(2,1)S(1)}, u32[]{:S(2)}, u32[]{:S(2)}) %collective-permute-start.1) | collective-permute-done | bytes 1064992 | tf_op jit(solution)/shard_map/ppermute | solution.py:35
  56.0 13.3 %collective-permute-done.2.refs_2_ = bf16[4,80,1664]{2,1,0:T(8,128)(2,1)S(1)} collective-permute-done((bf16[4,80,1664]{2,1,0:T(8,128)(2,1)}, bf16[4,80,1664]{2,1,0:T(8,128)(2,1)S(1)}, u32[]{:S(2)}, u32[]{:S(2)}) %collective-permute-start.2) | collective-permute-done | bytes 1064992 | tf_op jit(solution)/shard_map/ppermute | solution.py:35
  69.2 3.4 %collective-permute-done.3.refs_3_ = bf16[4,80,1664]{2,1,0:T(8,128)(2,1)} collective-permute-done((bf16[4,80,1664]{2,1,0:T(8,128)(2,1)}, bf16[4,80,1664]{2,1,0:T(8,128)(2,1)}, u32[]{:S(2)}, u32[]{:S(2)}) %collective-permute-start.3) | collective-permute-done | bytes 1064992 | tf_op jit(solution)/shard_map/ppermute | solution.py:35
  75.3 6.3 %shard_map.102 = (bf16[4,80,1664]{2,1,0:T(8,128)(2,1)}, bf16[4,80,1664]{2,1,0:T(8,128)(2,1)}, bf16[4,80,1664]{2,1,0:T(8,128)(2,1)}, bf16[4,80,1664]{2,1,0:T(8,12...) custom-call(s32[3]{0:T(128)} %pad_add_fusion.pos_ref, bf16[4,80,1664]{2,1,0:T(8,128)(2,1)} %copy-done, ...), custom_call_target="tpu_custom_call" | custom-call | bytes 13000000 | tf_op jit(solution)/shard_map/pallas_call | solution.py:139
  81.6 3.0 %collective-permute-start.10 = (bf16[4,80,1664]{2,1,0:T(8,128)(2,1)}, bf16[4,80,1664]{2,1,0:T(8,128)(2,1)S(1)}, u32[]{:S(2)}, u32[]{:S(2)}) collective-permute-start(bf16[4,80,1664]{2,1,0:T(8,128)(2,1)} %get-tuple-element.64), channel_id=1, source_target_pairs={{0,16},{8,24},{16,0},{24,8},{1,17},{9,25},{17,1},{25,9},{2,18},{10... | collective-permute-start | bytes 3194888 | tf_op jit(solution)/shard_map/ppermute | solution.py:35
  89.7 17.5 %collective-permute-done.10.refs_12_ = bf16[4,80,1664]{2,1,0:T(8,128)(2,1)S(1)} collective-permute-done((bf16[4,80,1664]{2,1,0:T(8,128)(2,1)}, bf16[4,80,1664]{2,1,0:T(8,128)(2,1)S(1)}, u32[]{:S(2)}, u32[]{:S(2)}) %collective-permute-start.10) | collective-permute-done | bytes 1064992 | tf_op jit(solution)/shard_map/ppermute | solution.py:35
  107.2 4.1 %collective-permute-start.9 = (bf16[4,80,1664]{2,1,0:T(8,128)(2,1)}, bf16[4,80,1664]{2,1,0:T(8,128)(2,1)}, u32[]{:S(2)}, u32[]{:S(2)}) collective-permute-start(bf16[4,80,1664]{2,1,0:T(8,128)(2,1)} %get-tuple-element.63), channel_id=1, source_target_pairs={{0,8},{8,16},{16,24},{24,0},{1,9},{9,17},{17,25},{25,1},{2,10},{10... | collective-permute-start | bytes 3194888 | tf_op jit(solution)/shard_map/ppermute | solution.py:35
  114.1 24.4 %collective-permute-done.6.refs_8_ = bf16[4,80,1664]{2,1,0:T(8,128)(2,1)S(1)} collective-permute-done((bf16[4,80,1664]{2,1,0:T(8,128)(2,1)}, bf16[4,80,1664]{2,1,0:T(8,128)(2,1)S(1)}, u32[]{:S(2)}, u32[]{:S(2)}) %collective-permute-start.6) | collective-permute-done | bytes 1064992 | tf_op jit(solution)/shard_map/ppermute | solution.py:35
  139.7 12.5 %shard_map.103 = (bf16[400,512]{1,0:T(8,128)(2,1)}, bf16[400,512]{1,0:T(8,128)(2,1)}, bf16[400,512]{1,0:T(8,128)(2,1)}, bf16[400,512]{1,0:T(8,128)(2,1)}, bf16[4...) custom-call(s32[3]{0:T(128)} %pad_add_fusion.pos_ref, ...), custom_call_target="tpu_custom_call" | custom-call | flops 4400000000 | bytes 15000000 | tf_op jit(solution)/shard_map/pallas_call | solution.py:219
  154.3 3.3 %collective-permute-start.14 = (bf16[400,512]{1,0:T(8,128)(2,1)}, bf16[400,512]{1,0:T(8,128)(2,1)S(1)}, u32[]{:S(2)}, u32[]{:S(2)}) collective-permute-start(bf16[400,512]{1,0:T(8,128)(2,1)} %get-tuple-element.68), channel_id=1, source_target_pairs={{0,6},{2,0},{4,2},{6,4},{1,7},{3,1},{5,3},{7,5},{8,14},{10,8},{12,... | collective-permute-start | bytes 1228808 | tf_op jit(solution)/shard_map/ppermute | solution.py:35
  160.0 3.9 %collective-permute-done.12.refs_0_ = bf16[400,512]{1,0:T(8,128)(2,1)S(1)} collective-permute-done((bf16[400,512]{1,0:T(8,128)(2,1)}, bf16[400,512]{1,0:T(8,128)(2,1)S(1)}, u32[]{:S(2)}, u32[]{:S(2)}) %collective-permute-start.12) | collective-permute-done | bytes 409632 | tf_op jit(solution)/shard_map/ppermute | solution.py:35
  166.2 8.9 %collective-permute-done.14.refs_2_ = bf16[400,512]{1,0:T(8,128)(2,1)S(1)} collective-permute-done((bf16[400,512]{1,0:T(8,128)(2,1)}, bf16[400,512]{1,0:T(8,128)(2,1)S(1)}, u32[]{:S(2)}, u32[]{:S(2)}) %collective-permute-start.14) | collective-permute-done | bytes 409632 | tf_op jit(solution)/shard_map/ppermute | solution.py:35
  175.1 3.3 %collective-permute-done.15.refs_3_ = bf16[400,512]{1,0:T(8,128)(2,1)S(1)} collective-permute-done((bf16[400,512]{1,0:T(8,128)(2,1)}, bf16[400,512]{1,0:T(8,128)(2,1)S(1)}, u32[]{:S(2)}, u32[]{:S(2)}) %collective-permute-start.15) | collective-permute-done | bytes 409632 | tf_op jit(solution)/shard_map/ppermute | solution.py:35
  179.4 4.6 %shard_map.104 = (bf16[400,512]{1,0:T(8,128)(2,1)}, bf16[400,512]{1,0:T(8,128)(2,1)}, bf16[64,16,640]{2,1,0:T(8,128)(2,1)}) custom-call(bf16[400,512]{1,0:T(8,128)(2,1)} %copy-done.11, bf16[400,512]{1,0:T(8,128)(2,1)} %copy-done.12, bf16[400,512]{1,0:T(8,128)(2,1)} %copy-done.13, bf16[400,512]{1,0:T(8,128)(2,1)} %copy-done.14, bf16[400,512]{1,0:T(8,128)(2,1)} %copy-done.15, ...), custom_call_target="tpu_custom_call" | custom-call | flops 1000000000 | bytes 7000000 | tf_op jit(solution)/shard_map/pallas_call | solution.py:264
  184.0 6.9 %all-to-all-start = ((bf16[64,16,640]{2,1,0:T(8,128)(2,1)}), bf16[64,16,640]{2,1,0:T(8,128)(2,1)S(1)}, u32[]{:S(2)}, u32[]{:S(2)}) async-start(bf16[64,16,640]{2,1,0:T(8,128)(2,1)} %get-tuple-element.74), calls=%async_computation | async-start | bytes 2621440 | tf_op jit(solution)/shard_map/all_to_all | solution.py:458
  198.8 14.9 %collective-permute-done.18._.refs_14_ = bf16[400,512]{1,0:T(8,128)(2,1)S(1)} collective-permute-done((bf16[400,512]{1,0:T(8,128)(2,1)S(1)}, bf16[400,512]{1,0:T(8,128)(2,1)S(1)}, u32[]{:S(2)}, u32[]{:S(2)}) %collective-permute-start.18) | collective-permute-done | bytes 409632 | tf_op jit(solution)/shard_map/ppermute | solution.py:35
  220.0 8.7 %all-to-all-start.1 = ((bf16[64,16,512]{2,1,0:T(8,128)(2,1)}), bf16[64,16,512]{2,1,0:T(8,128)(2,1)S(1)}, u32[]{:S(2)}, u32[]{:S(2)}) async-start(bf16[64,16,512]{2,1,0:T(8,128)(2,1)} %get-tuple-element.76), calls=%async_computation.1 | async-start | bytes 2097152 | tf_op jit(solution)/shard_map/all_to_all | solution.py:462
  228.8 11.0 %shard_map.107 = (bf16[4,80,512]{2,1,0:T(8,128)(2,1)}, bf16[4,80,512]{2,1,0:T(8,128)(2,1)}, bf16[4,80,512]{2,1,0:T(8,128)(2,1)}, bf16[4,80,512]{2,1,0:T(8,128)(2...) custom-call(s32[3]{0:T(128)} %pad_add_fusion.pos_ref, ...), custom_call_target="tpu_custom_call" | custom-call | flops 4400000000 | bytes 16000000 | tf_op jit(solution)/shard_map/pallas_call | solution.py:315
  251.0 7.1 %collective-permute-done.25.refs_1_ = bf16[4,80,512]{2,1,0:T(8,128)(2,1)S(1)} collective-permute-done((bf16[4,80,512]{2,1,0:T(8,128)(2,1)}, bf16[4,80,512]{2,1,0:T(8,128)(2,1)S(1)}, u32[]{:S(2)}, u32[]{:S(2)}) %collective-permute-start.25) | collective-permute-done | bytes 327712 | tf_op jit(solution)/shard_map/ppermute | solution.py:35
  274.5 3.6 %shard_map.106 = (bf16[2,400,256]{2,1,0:T(8,128)(2,1)}, f32[2,80,256]{2,1,0:T(8,128)}, f32[2,80,256]{2,1,0:T(8,128)}, bf16[2,512,256]{2,1,0:T(8,128)(2,1)}) custom-call(bf16[64,16,512]{2,1,0:T(8,128)(2,1)} %copy-done.7, bf16[400,512]{1,0:T(8,128)(2,1)} %get-tuple-element.77.sk0_ref.refs_20_, bf16[400,512]{1,0:T(8,128)(2,1)} %get-tuple-element.75.sk1_ref.refs_21_, ...), custom_call_target="tpu_custom_call" | custom-call | flops 500000000 | bytes 4000000 | tf_op jit(solution)/shard_map/pallas_call | solution.py:386
  (134 shorter events, 68.7 us)
Async XLA Ops:
  7.2 132.5 %all-gather.5.cloned.1.call-start = ((), (), s32[]{:S(2)}) async-start(), calls=%async_computation.2 | async-start | bytes 1392640 | tf_op jit(solution)/shard_map/all_gather | solution.py:451
  7.9 131.8 %all-gather.7.cloned.1.call-start = ((), (), s32[]{:S(2)}) async-start(), calls=%async_computation.3 | async-start | bytes 1392640 | tf_op jit(solution)/shard_map/all_gather | solution.py:451
  16.4 30.4 %collective-permute-start = (bf16[4,80,1664]{2,1,0:T(8,128)(2,1)}, bf16[4,80,1664]{2,1,0:T(8,128)(2,1)S(1)}, u32[]{:S(2)}, u32[]{:S(2)}) collective-permute-start(bf16[4,80,1664]{2,1,0:T(8,128)(2,1)} %get-tuple-element.52), channel_id=1, source_target_pairs={{0,96},{32,0},{64,32},{96,64},{1,97},{33,1},{65,33},{97,65},{2,98}... | collective-permute-start | bytes 3194888 | tf_op jit(solution)/shard_map/ppermute | solution.py:35
  20.6 35.4 %collective-permute-start.1 = (bf16[4,80,1664]{2,1,0:T(8,128)(2,1)}, bf16[4,80,1664]{2,1,0:T(8,128)(2,1)S(1)}, u32[]{:S(2)}, u32[]{:S(2)}) collective-permute-start(bf16[4,80,1664]{2,1,0:T(8,128)(2,1)} %get-tuple-element.53), channel_id=1, source_target_pairs={{0,32},{32,64},{64,96},{96,0},{1,33},{33,65},{65,97},{97,1},{2,34}... | collective-permute-start | bytes 3194888 | tf_op jit(solution)/shard_map/ppermute | solution.py:35
  20.6 48.6 %collective-permute-start.2 = (bf16[4,80,1664]{2,1,0:T(8,128)(2,1)}, bf16[4,80,1664]{2,1,0:T(8,128)(2,1)S(1)}, u32[]{:S(2)}, u32[]{:S(2)}) collective-permute-start(bf16[4,80,1664]{2,1,0:T(8,128)(2,1)} %get-tuple-element.54), channel_id=1, source_target_pairs={{0,6},{2,0},{4,2},{6,4},{1,7},{3,1},{5,3},{7,5},{8,14},{10,8},{12,... | collective-permute-start | bytes 3194888 | tf_op jit(solution)/shard_map/ppermute | solution.py:35
  23.6 49.0 %collective-permute-start.3 = (bf16[4,80,1664]{2,1,0:T(8,128)(2,1)}, bf16[4,80,1664]{2,1,0:T(8,128)(2,1)}, u32[]{:S(2)}, u32[]{:S(2)}) collective-permute-start(bf16[4,80,1664]{2,1,0:T(8,128)(2,1)} %get-tuple-element.55), channel_id=1, source_target_pairs={{0,2},{2,4},{4,6},{6,0},{1,3},{3,5},{5,7},{7,1},{8,10},{10,12},{12... | collective-permute-start | bytes 3194888 | tf_op jit(solution)/shard_map/ppermute | solution.py:35
  23.6 49.0 %collective-permute-start.4 = (bf16[4,80,1664]{2,1,0:T(8,128)(2,1)}, bf16[4,80,1664]{2,1,0:T(8,128)(2,1)}, u32[]{:S(2)}, u32[]{:S(2)}) collective-permute-start(bf16[4,80,1664]{2,1,0:T(8,128)(2,1)} %get-tuple-element.56), channel_id=1, source_target_pairs={{0,4},{2,6},{4,0},{6,2},{1,5},{3,7},{5,1},{7,3},{8,12},{10,14},{12... | collective-permute-start | bytes 3194888 | tf_op jit(solution)/shard_map/ppermute | solution.py:35
  46.7 28.6 %collective-permute-start.5 = (bf16[4,80,1664]{2,1,0:T(8,128)(2,1)}, bf16[4,80,1664]{2,1,0:T(8,128)(2,1)}, u32[]{:S(2)}, u32[]{:S(2)}) collective-permute-start(bf16[4,80,1664]{2,1,0:T(8,128)(2,1)} %get-tuple-element.57), channel_id=1, source_target_pairs={{0,64},{32,96},{64,0},{96,32},{1,65},{33,97},{65,1},{97,33},{2,66}... | collective-permute-start | bytes 3194888 | tf_op jit(solution)/shard_map/ppermute | solution.py:35
  81.6 25.6 %collective-permute-start.10 = (bf16[4,80,1664]{2,1,0:T(8,128)(2,1)}, bf16[4,80,1664]{2,1,0:T(8,128)(2,1)S(1)}, u32[]{:S(2)}, u32[]{:S(2)}) collective-permute-start(bf16[4,80,1664]{2,1,0:T(8,128)(2,1)} %get-tuple-element.64), channel_id=1, source_target_pairs={{0,16},{8,24},{16,0},{24,8},{1,17},{9,25},{17,1},{25,9},{2,18},{10... | collective-permute-start | bytes 3194888 | tf_op jit(solution)/shard_map/ppermute | solution.py:35
  84.6 29.5 %collective-permute-start.11 = (bf16[4,80,1664]{2,1,0:T(8,128)(2,1)}, bf16[4,80,1664]{2,1,0:T(8,128)(2,1)S(1)}, u32[]{:S(2)}, u32[]{:S(2)}) collective-permute-start(bf16[4,80,1664]{2,1,0:T(8,128)(2,1)} %get-tuple-element.65), channel_id=1, source_target_pairs={{0,64},{32,96},{64,0},{96,32},{1,65},{33,97},{65,1},{97,33},{2,66}... | collective-permute-start | bytes 3194888 | tf_op jit(solution)/shard_map/ppermute | solution.py:35
  86.5 52.0 %collective-permute-start.6 = (bf16[4,80,1664]{2,1,0:T(8,128)(2,1)}, bf16[4,80,1664]{2,1,0:T(8,128)(2,1)S(1)}, u32[]{:S(2)}, u32[]{:S(2)}) collective-permute-start(bf16[4,80,1664]{2,1,0:T(8,128)(2,1)} %get-tuple-element.60), channel_id=1, source_target_pairs={{0,96},{32,0},{64,32},{96,64},{1,97},{33,1},{65,33},{97,65},{2,98}... | collective-permute-start | bytes 3194888 | tf_op jit(solution)/shard_map/ppermute | solution.py:35
  88.5 51.1 %collective-permute-start.7 = (bf16[4,80,1664]{2,1,0:T(8,128)(2,1)}, bf16[4,80,1664]{2,1,0:T(8,128)(2,1)}, u32[]{:S(2)}, u32[]{:S(2)}) collective-permute-start(bf16[4,80,1664]{2,1,0:T(8,128)(2,1)} %get-tuple-element.61), channel_id=1, source_target_pairs={{0,32},{32,64},{64,96},{96,0},{1,33},{33,65},{65,97},{97,1},{2,34}... | collective-permute-start | bytes 3194888 | tf_op jit(solution)/shard_map/ppermute | solution.py:35
  88.5 51.1 %collective-permute-start.8 = (bf16[4,80,1664]{2,1,0:T(8,128)(2,1)}, bf16[4,80,1664]{2,1,0:T(8,128)(2,1)}, u32[]{:S(2)}, u32[]{:S(2)}) collective-permute-start(bf16[4,80,1664]{2,1,0:T(8,128)(2,1)} %get-tuple-element.62), channel_id=1, source_target_pairs={{0,24},{8,0},{16,8},{24,16},{1,25},{9,1},{17,9},{25,17},{2,26},{10... | collective-permute-start | bytes 3194888 | tf_op jit(solution)/shard_map/ppermute | solution.py:35
  107.2 32.5 %collective-permute-start.9 = (bf16[4,80,1664]{2,1,0:T(8,128)(2,1)}, bf16[4,80,1664]{2,1,0:T(8,128)(2,1)}, u32[]{:S(2)}, u32[]{:S(2)}) collective-permute-start(bf16[4,80,1664]{2,1,0:T(8,128)(2,1)} %get-tuple-element.63), channel_id=1, source_target_pairs={{0,8},{8,16},{16,24},{24,0},{1,9},{9,17},{17,25},{25,1},{2,10},{10... | collective-permute-start | bytes 3194888 | tf_op jit(solution)/shard_map/ppermute | solution.py:35
  154.3 20.8 %collective-permute-start.14 = (bf16[400,512]{1,0:T(8,128)(2,1)}, bf16[400,512]{1,0:T(8,128)(2,1)S(1)}, u32[]{:S(2)}, u32[]{:S(2)}) collective-permute-start(bf16[400,512]{1,0:T(8,128)(2,1)} %get-tuple-element.68), channel_id=1, source_target_pairs={{0,6},{2,0},{4,2},{6,4},{1,7},{3,1},{5,3},{7,5},{8,14},{10,8},{12,... | collective-permute-start | bytes 1228808 | tf_op jit(solution)/shard_map/ppermute | solution.py:35
  157.7 20.7 %collective-permute-start.15 = (bf16[400,512]{1,0:T(8,128)(2,1)}, bf16[400,512]{1,0:T(8,128)(2,1)S(1)}, u32[]{:S(2)}, u32[]{:S(2)}) collective-permute-start(bf16[400,512]{1,0:T(8,128)(2,1)} %get-tuple-element.69), channel_id=1, source_target_pairs={{0,2},{2,4},{4,6},{6,0},{1,3},{3,5},{5,7},{7,1},{8,10},{10,12},{12... | collective-permute-start | bytes 1228808 | tf_op jit(solution)/shard_map/ppermute | solution.py:35
  157.7 20.7 %collective-permute-start.16 = (bf16[400,512]{1,0:T(8,128)(2,1)}, bf16[400,512]{1,0:T(8,128)(2,1)S(1)}, u32[]{:S(2)}, u32[]{:S(2)}) collective-permute-start(bf16[400,512]{1,0:T(8,128)(2,1)} %get-tuple-element.70), channel_id=1, source_target_pairs={{0,4},{2,6},{4,0},{6,2},{1,5},{3,7},{5,1},{7,3},{8,12},{10,14},{12... | collective-permute-start | bytes 1228808 | tf_op jit(solution)/shard_map/ppermute | solution.py:35
  184.0 32.3 %all-to-all-start = ((bf16[64,16,640]{2,1,0:T(8,128)(2,1)}), bf16[64,16,640]{2,1,0:T(8,128)(2,1)S(1)}, u32[]{:S(2)}, u32[]{:S(2)}) async-start(bf16[64,16,640]{2,1,0:T(8,128)(2,1)} %get-tuple-element.74), calls=%async_computation | async-start | bytes 2621440 | tf_op jit(solution)/shard_map/all_to_all | solution.py:458
  190.9 22.8 %collective-permute-start.18 = (bf16[400,512]{1,0:T(8,128)(2,1)S(1)}, bf16[400,512]{1,0:T(8,128)(2,1)S(1)}, u32[]{:S(2)}, u32[]{:S(2)}) collective-permute-start(bf16[400,512]{1,0:T(8,128)(2,1)S(1)} %copy-done.10), channel_id=1, source_target_pairs={{0,24},{8,0},{16,8},{24,16},{1,25},{9,1},{17,9},{25,17},{2,26},{10... | collective-permute-start | bytes 1228808 | tf_op jit(solution)/shard_map/ppermute | solution.py:35
  193.8 35.0 %collective-permute-start.19 = (bf16[400,512]{1,0:T(8,128)(2,1)S(1)}, bf16[400,512]{1,0:T(8,128)(2,1)}, u32[]{:S(2)}, u32[]{:S(2)}) collective-permute-start(bf16[400,512]{1,0:T(8,128)(2,1)S(1)} %copy-done.10), channel_id=1, source_target_pairs={{0,8},{8,16},{16,24},{24,0},{1,9},{9,17},{17,25},{25,1},{2,10},{10... | collective-permute-start | bytes 1228808 | tf_op jit(solution)/shard_map/ppermute | solution.py:35
  193.8 35.0 %collective-permute-start.20 = (bf16[400,512]{1,0:T(8,128)(2,1)S(1)}, bf16[400,512]{1,0:T(8,128)(2,1)}, u32[]{:S(2)}, u32[]{:S(2)}) collective-permute-start(bf16[400,512]{1,0:T(8,128)(2,1)S(1)} %copy-done.9), channel_id=1, source_target_pairs={{0,6},{2,0},{4,2},{6,4},{1,7},{3,1},{5,3},{7,5},{8,14},{10,8},{12,... | collective-permute-start | bytes 1228808 | tf_op jit(solution)/shard_map/ppermute | solution.py:35
  196.4 32.3 %collective-permute-start.21 = (bf16[400,512]{1,0:T(8,128)(2,1)S(1)}, bf16[400,512]{1,0:T(8,128)(2,1)}, u32[]{:S(2)}, u32[]{:S(2)}) collective-permute-start(bf16[400,512]{1,0:T(8,128)(2,1)S(1)} %copy-done.9), channel_id=1, source_target_pairs={{0,2},{2,4},{4,6},{6,0},{1,3},{3,5},{5,7},{7,1},{8,10},{10,12},{12... | collective-permute-start | bytes 1228808 | tf_op jit(solution)/shard_map/ppermute | solution.py:35
  196.4 32.3 %collective-permute-start.22 = (bf16[400,512]{1,0:T(8,128)(2,1)S(1)}, bf16[400,512]{1,0:T(8,128)(2,1)}, u32[]{:S(2)}, u32[]{:S(2)}) collective-permute-start(bf16[400,512]{1,0:T(8,128)(2,1)S(1)} %copy-done.9), channel_id=1, source_target_pairs={{0,4},{2,6},{4,0},{6,2},{1,5},{3,7},{5,1},{7,3},{8,12},{10,14},{12... | collective-permute-start | bytes 1228808 | tf_op jit(solution)/shard_map/ppermute | solution.py:35
  220.0 53.5 %all-to-all-start.1 = ((bf16[64,16,512]{2,1,0:T(8,128)(2,1)}), bf16[64,16,512]{2,1,0:T(8,128)(2,1)S(1)}, u32[]{:S(2)}, u32[]{:S(2)}) async-start(bf16[64,16,512]{2,1,0:T(8,128)(2,1)} %get-tuple-element.76), calls=%async_computation.1 | async-start | bytes 2097152 | tf_op jit(solution)/shard_map/all_to_all | solution.py:462
  (48 other events, 424.4 us)
Sparse Core Ops, SparseCore 0:
  10.1 66.7 all-gather.4
  79.0 59.7 all-gather.6

commit v6 on v5

--- a/solution.py
+++ b/solution.py
@@ -52,22 +52,28 @@
         wide = jnp.concatenate(strips + [jnp.zeros((ROWS, LANES - WIDE), bf16)], axis=1)
         block[...] = wide
 
-    for i in range(4):
-        put(scr[0].at[kz, i], [g_ref[0, :, WIDE * i : WIDE * (i + 1)]])
-        ky = lax.rem(pos_ref[2] - i + 4, 4)
-        put(
-            scr[1].at[ky, z],
-            [g_ref[1, :, WIDE * x + COLS * i : WIDE * x + COLS * (i + 1)] for x in range(4)],
-        )
-    for k in range(4):
-
-        @pl.when(kz == k)
-        def _():
-            pltpu.make_async_copy(scr[0].at[k], outs[k], sem.at[k]).start()
-
-        pltpu.make_async_copy(scr[1].at[k, z], outs[4 + k].at[z], sem.at[4 + k]).start()
-
-    @pl.when(z == 3)
+    @pl.when(pl.program_id(1) == 0)
+    def _():
+        for i in range(4):
+            put(scr[0].at[kz, i], [g_ref[0, :, WIDE * i : WIDE * (i + 1)]])
+        for k in range(4):
+
+            @pl.when(kz == k)
+            def _():
+                pltpu.make_async_copy(scr[0].at[k], outs[k], sem.at[k]).start()
+
+    @pl.when(pl.program_id(1) == 1)
+    def _():
+        for i in range(4):
+            ky = lax.rem(pos_ref[2] - i + 4, 4)
+            put(
+                scr[1].at[ky, z],
+                [g_ref[0, :, WIDE * x + COLS * i : WIDE * x + COLS * (i + 1)] for x in range(4)],
+            )
+        for k in range(4):
+            pltpu.make_async_copy(scr[1].at[k, z], outs[4 + k].at[z], sem.at[4 + k]).start()
+
+    @pl.when((z == 3) & (pl.program_id(1) == 1))
     def _():
         for l in range(NL):
             for k in range(4):
@@ -77,8 +83,8 @@
 def pack(pos, g):
     outs = pl.pallas_call(
         pack_kernel,
-        grid=(4,),
-        in_specs=[SMEM, pl.BlockSpec((NL, ROWS, 4 * WIDE), lambda i: (0, 0, i))],
+        grid=(4, NL),
+        in_specs=[SMEM, pl.BlockSpec((1, ROWS, 4 * WIDE), lambda i, l: (l, 0, i))],
         out_specs=[HBM] * 8,
         out_shape=[jax.ShapeDtypeStruct((4, ROWS, LANES), bf16)] * 8,
         scratch_shapes=[pltpu.VMEM((4, 4, ROWS, LANES), bf16)] * 2 + [pltpu.SemaphoreType.DMA((8,))],
@@ -174,6 +180,7 @@
     s_ref = refs[14:16]
     outs = refs[16:24]
     x_ref, s_vmem, acc_ref, u_ref, sem, sem_s, sem_out = refs[24:]
+    loads = panel_loads(pos_ref, first, got, x_ref, sem)
     load_s = []
     for l in range(NL):
         for kz in range(4):
@@ -184,12 +191,9 @@
                     pltpu.make_async_copy(s_ref[l].at[4 * z + other], s_vmem.at[l, kz, k], sem_s.at[at])
                 )
                 load_s[-1].start()
-    loads = panel_loads(pos_ref, first, got, x_ref, sem)
-    for c in load_s:
-        c.wait()
     stores = []
     for l in range(NL):
-        for c in loads[l]:
+        for c in loads[l] + load_s[16 * l : 16 * l + 16]:
             c.wait()
         for i in range(2):
             part = lax.dot_general(

time: 289 us -> 291 us (level)
  transfers between devices with their start and end apart: 41 -> 41, of which waited for: 16 -> 15; matrix products, arithmetic and copies ran while one was open for 1% -> 1% of each run, Pallas kernels for 12% -> 12%
where the time goes in v6:
time: 291 us; the launch traced here: 290 us
  waiting for transfers between devices  134 us (46%)
  starting transfers between devices  80 us (27%)
  Pallas kernels  54.8 us (19%)
  between operations  14.4 us (5%)
  local copies, waits for them, and re-layouts  5.51 us (2%)
    ppermute x36, waiting for transfers between devices, shifted(): return lax.ppermute(x, axis, [(s, (s - k) % 4) for s in range(4)])  133 us
    ppermute x36, starting transfers between devices, shifted(): return lax.ppermute(x, axis, [(s, (s - k) % 4) for s in range(4)])  63.5 us
    pallas_call x1, Pallas kernels, panel_products(): pl.pallas_call(panel_kernel, in_specs=[SMEM] + [HBM] * 16, out_specs=[HBM...  11.6 us
    pallas_call x1, Pallas kernels, back_products(): pl.pallas_call(back_kernel, in_specs=[SMEM] + [HBM] * 22, out_specs=[HBM]...  11 us
    pallas_call x1, Pallas kernels, pack(): pl.pallas_call(pack_kernel, grid=(4, NL), in_specs=[SMEM, pl.BlockSpec((1...  9.69 us
    all_to_all x1, starting transfers between devices, shards(): everyone = lax.all_to_all(mine, AX, 0, 0, tiled=True)  8.72 us
    all_to_all x1, starting transfers between devices, shards(): got = lax.all_to_all(send, AX, 0, 0, tiled=True)  7.67 us
    pallas_call x1, Pallas kernels, second(): pl.pallas_call(second_kernel, in_specs=[SMEM] + [HBM] * 8, out_specs=[HBM...  6.27 us
  transfers between devices with their start and end apart: 41, of which 15 were waited for; matrix products, arithmetic and copies ran while one was open for 1% of the time, Pallas kernels for 12%

profile of v6, /device:TPU:0, one launch (start us, length us, event | category | flops | bytes accessed | tf_op | source)
XLA Modules:
  0.0 290.4 jit_solution(14379499543090609042)
XLA Ops:
  8.5 9.7 %shard_map.101 = (bf16[4,80,1664]{2,1,0:T(8,128)(2,1)}, bf16[4,80,1664]{2,1,0:T(8,128)(2,1)}, bf16[4,80,1664]{2,1,0:T(8,128)(2,1)}, bf16[4,80,1664]{2,1,0:T(8,12...) custom-call(s32[3]{0:T(128)} %pad_add_fusion.pos_ref, ...), custom_call_target="tpu_custom_call" | custom-call | bytes 17000000 | tf_op jit(solution)/shard_map/pallas_call | solution.py:84
  18.2 4.2 %collective-permute-start = (bf16[4,80,1664]{2,1,0:T(8,128)(2,1)}, bf16[4,80,1664]{2,1,0:T(8,128)(2,1)S(1)}, u32[]{:S(2)}, u32[]{:S(2)}) collective-permute-start(bf16[4,80,1664]{2,1,0:T(8,128)(2,1)} %get-tuple-element.52), channel_id=1, source_target_pairs={{0,96},{32,0},{64,32},{96,64},{1,97},{33,1},{65,33},{97,65},{2,98}... | collective-permute-start | bytes 3194888 | tf_op jit(solution)/shard_map/ppermute | solution.py:35
  22.4 3.0 %collective-permute-start.2 = (bf16[4,80,1664]{2,1,0:T(8,128)(2,1)}, bf16[4,80,1664]{2,1,0:T(8,128)(2,1)S(1)}, u32[]{:S(2)}, u32[]{:S(2)}) collective-permute-start(bf16[4,80,1664]{2,1,0:T(8,128)(2,1)} %get-tuple-element.54), channel_id=1, source_target_pairs={{0,6},{2,0},{4,2},{6,4},{1,7},{3,1},{5,3},{7,5},{8,14},{10,8},{12,... | collective-permute-start | bytes 3194888 | tf_op jit(solution)/shard_map/ppermute | solution.py:35
  27.7 21.0 %collective-permute-done.refs_0_ = bf16[4,80,1664]{2,1,0:T(8,128)(2,1)S(1)} collective-permute-done((bf16[4,80,1664]{2,1,0:T(8,128)(2,1)}, bf16[4,80,1664]{2,1,0:T(8,128)(2,1)S(1)}, u32[]{:S(2)}, u32[]{:S(2)}) %collective-permute-start) | collective-permute-done | bytes 1064992 | tf_op jit(solution)/shard_map/ppermute | solution.py:35
  50.8 6.0 %collective-permute-done.1.refs_1_ = bf16[4,80,1664]{2,1,0:T(8,128)(2,1)S(1)} collective-permute-done((bf16[4,80,1664]{2,1,0:T(8,128)(2,1)}, bf16[4,80,1664]{2,1,0:T(8,128)(2,1)S(1)}, u32[]{:S(2)}, u32[]{:S(2)}) %collective-permute-start.1) | collective-permute-done | bytes 1064992 | tf_op jit(solution)/shard_map/ppermute | solution.py:35
  56.8 14.3 %collective-permute-done.2.refs_2_ = bf16[4,80,1664]{2,1,0:T(8,128)(2,1)S(1)} collective-permute-done((bf16[4,80,1664]{2,1,0:T(8,128)(2,1)}, bf16[4,80,1664]{2,1,0:T(8,128)(2,1)S(1)}, u32[]{:S(2)}, u32[]{:S(2)}) %collective-permute-start.2) | collective-permute-done | bytes 1064992 | tf_op jit(solution)/shard_map/ppermute | solution.py:35
  71.1 3.4 %collective-permute-done.3.refs_3_ = bf16[4,80,1664]{2,1,0:T(8,128)(2,1)} collective-permute-done((bf16[4,80,1664]{2,1,0:T(8,128)(2,1)}, bf16[4,80,1664]{2,1,0:T(8,128)(2,1)}, u32[]{:S(2)}, u32[]{:S(2)}) %collective-permute-start.3) | collective-permute-done | bytes 1064992 | tf_op jit(solution)/shard_map/ppermute | solution.py:35
  74.5 3.0 %collective-permute-done.5.refs_5_ = bf16[4,80,1664]{2,1,0:T(8,128)(2,1)} collective-permute-done((bf16[4,80,1664]{2,1,0:T(8,128)(2,1)}, bf16[4,80,1664]{2,1,0:T(8,128)(2,1)}, u32[]{:S(2)}, u32[]{:S(2)}) %collective-permute-start.5) | collective-permute-done | bytes 1064992 | tf_op jit(solution)/shard_map/ppermute | solution.py:35
  77.5 6.3 %shard_map.102 = (bf16[4,80,1664]{2,1,0:T(8,128)(2,1)}, bf16[4,80,1664]{2,1,0:T(8,128)(2,1)}, bf16[4,80,1664]{2,1,0:T(8,128)(2,1)}, bf16[4,80,1664]{2,1,0:T(8,12...) custom-call(s32[3]{0:T(128)} %pad_add_fusion.pos_ref, bf16[4,80,1664]{2,1,0:T(8,128)(2,1)} %copy-done, ...), custom_call_target="tpu_custom_call" | custom-call | bytes 13000000 | tf_op jit(solution)/shard_map/pallas_call | solution.py:145
  83.8 4.3 %collective-permute-start.10 = (bf16[4,80,1664]{2,1,0:T(8,128)(2,1)}, bf16[4,80,1664]{2,1,0:T(8,128)(2,1)S(1)}, u32[]{:S(2)}, u32[]{:S(2)}) collective-permute-start(bf16[4,80,1664]{2,1,0:T(8,128)(2,1)} %get-tuple-element.64), channel_id=1, source_target_pairs={{0,16},{8,24},{16,0},{24,8},{1,17},{9,25},{17,1},{25,9},{2,18},{10... | collective-permute-start | bytes 3194888 | tf_op jit(solution)/shard_map/ppermute | solution.py:35
  91.8 18.5 %collective-permute-done.10.refs_12_ = bf16[4,80,1664]{2,1,0:T(8,128)(2,1)S(1)} collective-permute-done((bf16[4,80,1664]{2,1,0:T(8,128)(2,1)}, bf16[4,80,1664]{2,1,0:T(8,128)(2,1)S(1)}, u32[]{:S(2)}, u32[]{:S(2)}) %collective-permute-start.10) | collective-permute-done | bytes 1064992 | tf_op jit(solution)/shard_map/ppermute | solution.py:35
  110.2 4.5 %collective-permute-start.9 = (bf16[4,80,1664]{2,1,0:T(8,128)(2,1)}, bf16[4,80,1664]{2,1,0:T(8,128)(2,1)}, u32[]{:S(2)}, u32[]{:S(2)}) collective-permute-start(bf16[4,80,1664]{2,1,0:T(8,128)(2,1)} %get-tuple-element.63), channel_id=1, source_target_pairs={{0,8},{8,16},{16,24},{24,0},{1,9},{9,17},{17,25},{25,1},{2,10},{10... | collective-permute-start | bytes 3194888 | tf_op jit(solution)/shard_map/ppermute | solution.py:35
  117.6 24.8 %collective-permute-done.6.refs_8_ = bf16[4,80,1664]{2,1,0:T(8,128)(2,1)S(1)} collective-permute-done((bf16[4,80,1664]{2,1,0:T(8,128)(2,1)}, bf16[4,80,1664]{2,1,0:T(8,128)(2,1)S(1)}, u32[]{:S(2)}, u32[]{:S(2)}) %collective-permute-start.6) | collective-permute-done | bytes 1064992 | tf_op jit(solution)/shard_map/ppermute | solution.py:35
  143.4 11.6 %shard_map.103 = (bf16[400,512]{1,0:T(8,128)(2,1)}, bf16[400,512]{1,0:T(8,128)(2,1)}, bf16[400,512]{1,0:T(8,128)(2,1)}, bf16[400,512]{1,0:T(8,128)(2,1)}, bf16[4...) custom-call(s32[3]{0:T(128)} %pad_add_fusion.pos_ref, ...), custom_call_target="tpu_custom_call" | custom-call | flops 4400000000 | bytes 15000000 | tf_op jit(solution)/shard_map/pallas_call | solution.py:223
  157.1 3.4 %collective-permute-start.14 = (bf16[400,512]{1,0:T(8,128)(2,1)}, bf16[400,512]{1,0:T(8,128)(2,1)S(1)}, u32[]{:S(2)}, u32[]{:S(2)}) collective-permute-start(bf16[400,512]{1,0:T(8,128)(2,1)} %get-tuple-element.68), channel_id=1, source_target_pairs={{0,6},{2,0},{4,2},{6,4},{1,7},{3,1},{5,3},{7,5},{8,14},{10,8},{12,... | collective-permute-start | bytes 1228808 | tf_op jit(solution)/shard_map/ppermute | solution.py:35
  167.8 8.6 %collective-permute-done.14.refs_2_ = bf16[400,512]{1,0:T(8,128)(2,1)S(1)} collective-permute-done((bf16[400,512]{1,0:T(8,128)(2,1)}, bf16[400,512]{1,0:T(8,128)(2,1)S(1)}, u32[]{:S(2)}, u32[]{:S(2)}) %collective-permute-start.14) | collective-permute-done | bytes 409632 | tf_op jit(solution)/shard_map/ppermute | solution.py:35
  176.5 3.3 %collective-permute-done.15.refs_3_ = bf16[400,512]{1,0:T(8,128)(2,1)S(1)} collective-permute-done((bf16[400,512]{1,0:T(8,128)(2,1)}, bf16[400,512]{1,0:T(8,128)(2,1)S(1)}, u32[]{:S(2)}, u32[]{:S(2)}) %collective-permute-start.15) | collective-permute-done | bytes 409632 | tf_op jit(solution)/shard_map/ppermute | solution.py:35
  180.8 4.6 %shard_map.104 = (bf16[400,512]{1,0:T(8,128)(2,1)}, bf16[400,512]{1,0:T(8,128)(2,1)}, bf16[64,16,640]{2,1,0:T(8,128)(2,1)}) custom-call(bf16[400,512]{1,0:T(8,128)(2,1)} %copy-done.11, bf16[400,512]{1,0:T(8,128)(2,1)} %copy-done.12, bf16[400,512]{1,0:T(8,128)(2,1)} %copy-done.13, bf16[400,512]{1,0:T(8,128)(2,1)} %copy-done.14, bf16[400,512]{1,0:T(8,128)(2,1)} %copy-done.15, ...), custom_call_target="tpu_custom_call" | custom-call | flops 1000000000 | bytes 7000000 | tf_op jit(solution)/shard_map/pallas_call | solution.py:268
  185.4 7.7 %all-to-all-start = ((bf16[64,16,640]{2,1,0:T(8,128)(2,1)}), bf16[64,16,640]{2,1,0:T(8,128)(2,1)S(1)}, u32[]{:S(2)}, u32[]{:S(2)}) async-start(bf16[64,16,640]{2,1,0:T(8,128)(2,1)} %get-tuple-element.74), calls=%async_computation | async-start | bytes 2621440 | tf_op jit(solution)/shard_map/all_to_all | solution.py:462
  200.9 14.7 %collective-permute-done.18._.refs_14_ = bf16[400,512]{1,0:T(8,128)(2,1)S(1)} collective-permute-done((bf16[400,512]{1,0:T(8,128)(2,1)S(1)}, bf16[400,512]{1,0:T(8,128)(2,1)S(1)}, u32[]{:S(2)}, u32[]{:S(2)}) %collective-permute-start.18) | collective-permute-done | bytes 409632 | tf_op jit(solution)/shard_map/ppermute | solution.py:35
  222.0 8.7 %all-to-all-start.1 = ((bf16[64,16,512]{2,1,0:T(8,128)(2,1)}), bf16[64,16,512]{2,1,0:T(8,128)(2,1)S(1)}, u32[]{:S(2)}, u32[]{:S(2)}) async-start(bf16[64,16,512]{2,1,0:T(8,128)(2,1)} %get-tuple-element.76), calls=%async_computation.1 | async-start | bytes 2097152 | tf_op jit(solution)/shard_map/all_to_all | solution.py:466
  230.8 11.0 %shard_map.107 = (bf16[4,80,512]{2,1,0:T(8,128)(2,1)}, bf16[4,80,512]{2,1,0:T(8,128)(2,1)}, bf16[4,80,512]{2,1,0:T(8,128)(2,1)}, bf16[4,80,512]{2,1,0:T(8,128)(2...) custom-call(s32[3]{0:T(128)} %pad_add_fusion.pos_ref, ...), custom_call_target="tpu_custom_call" | custom-call | flops 4400000000 | bytes 16000000 | tf_op jit(solution)/shard_map/pallas_call | solution.py:319
  252.8 7.3 %collective-permute-done.25.refs_1_ = bf16[4,80,512]{2,1,0:T(8,128)(2,1)S(1)} collective-permute-done((bf16[4,80,512]{2,1,0:T(8,128)(2,1)}, bf16[4,80,512]{2,1,0:T(8,128)(2,1)S(1)}, u32[]{:S(2)}, u32[]{:S(2)}) %collective-permute-start.25) | collective-permute-done | bytes 327712 | tf_op jit(solution)/shard_map/ppermute | solution.py:35
  276.5 3.6 %shard_map.106 = (bf16[2,400,256]{2,1,0:T(8,128)(2,1)}, f32[2,80,256]{2,1,0:T(8,128)}, f32[2,80,256]{2,1,0:T(8,128)}, bf16[2,512,256]{2,1,0:T(8,128)(2,1)}) custom-call(bf16[64,16,512]{2,1,0:T(8,128)(2,1)} %copy-done.7, bf16[400,512]{1,0:T(8,128)(2,1)} %get-tuple-element.77.sk0_ref.refs_20_, bf16[400,512]{1,0:T(8,128)(2,1)} %get-tuple-element.75.sk1_ref.refs_21_, ...), custom_call_target="tpu_custom_call" | custom-call | flops 500000000 | bytes 4000000 | tf_op jit(solution)/shard_map/pallas_call | solution.py:390
  (134 shorter events, 68.6 us)
Async XLA Ops:
  7.2 135.3 %all-gather.5.cloned.1.call-start = ((), (), s32[]{:S(2)}) async-start(), calls=%async_computation.2 | async-start | bytes 1392640 | tf_op jit(solution)/shard_map/all_gather | solution.py:455
  7.9 134.6 %all-gather.7.cloned.1.call-start = ((), (), s32[]{:S(2)}) async-start(), calls=%async_computation.3 | async-start | bytes 1392640 | tf_op jit(solution)/shard_map/all_gather | solution.py:455
  18.2 30.4 %collective-permute-start = (bf16[4,80,1664]{2,1,0:T(8,128)(2,1)}, bf16[4,80,1664]{2,1,0:T(8,128)(2,1)S(1)}, u32[]{:S(2)}, u32[]{:S(2)}) collective-permute-start(bf16[4,80,1664]{2,1,0:T(8,128)(2,1)} %get-tuple-element.52), channel_id=1, source_target_pairs={{0,96},{32,0},{64,32},{96,64},{1,97},{33,1},{65,33},{97,65},{2,98}... | collective-permute-start | bytes 3194888 | tf_op jit(solution)/shard_map/ppermute | solution.py:35
  22.4 34.4 %collective-permute-start.1 = (bf16[4,80,1664]{2,1,0:T(8,128)(2,1)}, bf16[4,80,1664]{2,1,0:T(8,128)(2,1)S(1)}, u32[]{:S(2)}, u32[]{:S(2)}) collective-permute-start(bf16[4,80,1664]{2,1,0:T(8,128)(2,1)} %get-tuple-element.53), channel_id=1, source_target_pairs={{0,32},{32,64},{64,96},{96,0},{1,33},{33,65},{65,97},{97,1},{2,34}... | collective-permute-start | bytes 3194888 | tf_op jit(solution)/shard_map/ppermute | solution.py:35
  22.4 48.6 %collective-permute-start.2 = (bf16[4,80,1664]{2,1,0:T(8,128)(2,1)}, bf16[4,80,1664]{2,1,0:T(8,128)(2,1)S(1)}, u32[]{:S(2)}, u32[]{:S(2)}) collective-permute-start(bf16[4,80,1664]{2,1,0:T(8,128)(2,1)} %get-tuple-element.54), channel_id=1, source_target_pairs={{0,6},{2,0},{4,2},{6,4},{1,7},{3,1},{5,3},{7,5},{8,14},{10,8},{12,... | collective-permute-start | bytes 3194888 | tf_op jit(solution)/shard_map/ppermute | solution.py:35
  25.4 49.0 %collective-permute-start.3 = (bf16[4,80,1664]{2,1,0:T(8,128)(2,1)}, bf16[4,80,1664]{2,1,0:T(8,128)(2,1)}, u32[]{:S(2)}, u32[]{:S(2)}) collective-permute-start(bf16[4,80,1664]{2,1,0:T(8,128)(2,1)} %get-tuple-element.55), channel_id=1, source_target_pairs={{0,2},{2,4},{4,6},{6,0},{1,3},{3,5},{5,7},{7,1},{8,10},{10,12},{12... | collective-permute-start | bytes 3194888 | tf_op jit(solution)/shard_map/ppermute | solution.py:35
  25.5 49.0 %collective-permute-start.4 = (bf16[4,80,1664]{2,1,0:T(8,128)(2,1)}, bf16[4,80,1664]{2,1,0:T(8,128)(2,1)}, u32[]{:S(2)}, u32[]{:S(2)}) collective-permute-start(bf16[4,80,1664]{2,1,0:T(8,128)(2,1)} %get-tuple-element.56), channel_id=1, source_target_pairs={{0,4},{2,6},{4,0},{6,2},{1,5},{3,7},{5,1},{7,3},{8,12},{10,14},{12... | collective-permute-start | bytes 3194888 | tf_op jit(solution)/shard_map/ppermute | solution.py:35
  48.7 28.8 %collective-permute-start.5 = (bf16[4,80,1664]{2,1,0:T(8,128)(2,1)}, bf16[4,80,1664]{2,1,0:T(8,128)(2,1)}, u32[]{:S(2)}, u32[]{:S(2)}) collective-permute-start(bf16[4,80,1664]{2,1,0:T(8,128)(2,1)} %get-tuple-element.57), channel_id=1, source_target_pairs={{0,64},{32,96},{64,0},{96,32},{1,65},{33,97},{65,1},{97,33},{2,66}... | collective-permute-start | bytes 3194888 | tf_op jit(solution)/shard_map/ppermute | solution.py:35
  83.8 26.5 %collective-permute-start.10 = (bf16[4,80,1664]{2,1,0:T(8,128)(2,1)}, bf16[4,80,1664]{2,1,0:T(8,128)(2,1)S(1)}, u32[]{:S(2)}, u32[]{:S(2)}) collective-permute-start(bf16[4,80,1664]{2,1,0:T(8,128)(2,1)} %get-tuple-element.64), channel_id=1, source_target_pairs={{0,16},{8,24},{16,0},{24,8},{1,17},{9,25},{17,1},{25,9},{2,18},{10... | collective-permute-start | bytes 3194888 | tf_op jit(solution)/shard_map/ppermute | solution.py:35
  88.1 29.5 %collective-permute-start.11 = (bf16[4,80,1664]{2,1,0:T(8,128)(2,1)}, bf16[4,80,1664]{2,1,0:T(8,128)(2,1)S(1)}, u32[]{:S(2)}, u32[]{:S(2)}) collective-permute-start(bf16[4,80,1664]{2,1,0:T(8,128)(2,1)} %get-tuple-element.65), channel_id=1, source_target_pairs={{0,64},{32,96},{64,0},{96,32},{1,65},{33,97},{65,1},{97,33},{2,66}... | collective-permute-start | bytes 3194888 | tf_op jit(solution)/shard_map/ppermute | solution.py:35
  88.3 54.1 %collective-permute-start.6 = (bf16[4,80,1664]{2,1,0:T(8,128)(2,1)}, bf16[4,80,1664]{2,1,0:T(8,128)(2,1)S(1)}, u32[]{:S(2)}, u32[]{:S(2)}) collective-permute-start(bf16[4,80,1664]{2,1,0:T(8,128)(2,1)} %get-tuple-element.60), channel_id=1, source_target_pairs={{0,96},{32,0},{64,32},{96,64},{1,97},{33,1},{65,33},{97,65},{2,98}... | collective-permute-start | bytes 3194888 | tf_op jit(solution)/shard_map/ppermute | solution.py:35
  90.2 52.2 %collective-permute-start.7 = (bf16[4,80,1664]{2,1,0:T(8,128)(2,1)}, bf16[4,80,1664]{2,1,0:T(8,128)(2,1)}, u32[]{:S(2)}, u32[]{:S(2)}) collective-permute-start(bf16[4,80,1664]{2,1,0:T(8,128)(2,1)} %get-tuple-element.61), channel_id=1, source_target_pairs={{0,32},{32,64},{64,96},{96,0},{1,33},{33,65},{65,97},{97,1},{2,34}... | collective-permute-start | bytes 3194888 | tf_op jit(solution)/shard_map/ppermute | solution.py:35
  90.6 51.8 %collective-permute-start.8 = (bf16[4,80,1664]{2,1,0:T(8,128)(2,1)}, bf16[4,80,1664]{2,1,0:T(8,128)(2,1)}, u32[]{:S(2)}, u32[]{:S(2)}) collective-permute-start(bf16[4,80,1664]{2,1,0:T(8,128)(2,1)} %get-tuple-element.62), channel_id=1, source_target_pairs={{0,24},{8,0},{16,8},{24,16},{1,25},{9,1},{17,9},{25,17},{2,26},{10... | collective-permute-start | bytes 3194888 | tf_op jit(solution)/shard_map/ppermute | solution.py:35
  110.2 32.2 %collective-permute-start.9 = (bf16[4,80,1664]{2,1,0:T(8,128)(2,1)}, bf16[4,80,1664]{2,1,0:T(8,128)(2,1)}, u32[]{:S(2)}, u32[]{:S(2)}) collective-permute-start(bf16[4,80,1664]{2,1,0:T(8,128)(2,1)} %get-tuple-element.63), channel_id=1, source_target_pairs={{0,8},{8,16},{16,24},{24,0},{1,9},{9,17},{17,25},{25,1},{2,10},{10... | collective-permute-start | bytes 3194888 | tf_op jit(solution)/shard_map/ppermute | solution.py:35
  157.1 19.3 %collective-permute-start.14 = (bf16[400,512]{1,0:T(8,128)(2,1)}, bf16[400,512]{1,0:T(8,128)(2,1)S(1)}, u32[]{:S(2)}, u32[]{:S(2)}) collective-permute-start(bf16[400,512]{1,0:T(8,128)(2,1)} %get-tuple-element.68), channel_id=1, source_target_pairs={{0,6},{2,0},{4,2},{6,4},{1,7},{3,1},{5,3},{7,5},{8,14},{10,8},{12,... | collective-permute-start | bytes 1228808 | tf_op jit(solution)/shard_map/ppermute | solution.py:35
  160.5 19.2 %collective-permute-start.15 = (bf16[400,512]{1,0:T(8,128)(2,1)}, bf16[400,512]{1,0:T(8,128)(2,1)S(1)}, u32[]{:S(2)}, u32[]{:S(2)}) collective-permute-start(bf16[400,512]{1,0:T(8,128)(2,1)} %get-tuple-element.69), channel_id=1, source_target_pairs={{0,2},{2,4},{4,6},{6,0},{1,3},{3,5},{5,7},{7,1},{8,10},{10,12},{12... | collective-permute-start | bytes 1228808 | tf_op jit(solution)/shard_map/ppermute | solution.py:35
  160.5 19.3 %collective-permute-start.16 = (bf16[400,512]{1,0:T(8,128)(2,1)}, bf16[400,512]{1,0:T(8,128)(2,1)S(1)}, u32[]{:S(2)}, u32[]{:S(2)}) collective-permute-start(bf16[400,512]{1,0:T(8,128)(2,1)} %get-tuple-element.70), channel_id=1, source_target_pairs={{0,4},{2,6},{4,0},{6,2},{1,5},{3,7},{5,1},{7,3},{8,12},{10,14},{12... | collective-permute-start | bytes 1228808 | tf_op jit(solution)/shard_map/ppermute | solution.py:35
  185.4 33.0 %all-to-all-start = ((bf16[64,16,640]{2,1,0:T(8,128)(2,1)}), bf16[64,16,640]{2,1,0:T(8,128)(2,1)S(1)}, u32[]{:S(2)}, u32[]{:S(2)}) async-start(bf16[64,16,640]{2,1,0:T(8,128)(2,1)} %get-tuple-element.74), calls=%async_computation | async-start | bytes 2621440 | tf_op jit(solution)/shard_map/all_to_all | solution.py:462
  193.1 22.6 %collective-permute-start.18 = (bf16[400,512]{1,0:T(8,128)(2,1)S(1)}, bf16[400,512]{1,0:T(8,128)(2,1)S(1)}, u32[]{:S(2)}, u32[]{:S(2)}) collective-permute-start(bf16[400,512]{1,0:T(8,128)(2,1)S(1)} %copy-done.10), channel_id=1, source_target_pairs={{0,24},{8,0},{16,8},{24,16},{1,25},{9,1},{17,9},{25,17},{2,26},{10... | collective-permute-start | bytes 1228808 | tf_op jit(solution)/shard_map/ppermute | solution.py:35
  195.9 34.8 %collective-permute-start.19 = (bf16[400,512]{1,0:T(8,128)(2,1)S(1)}, bf16[400,512]{1,0:T(8,128)(2,1)}, u32[]{:S(2)}, u32[]{:S(2)}) collective-permute-start(bf16[400,512]{1,0:T(8,128)(2,1)S(1)} %copy-done.10), channel_id=1, source_target_pairs={{0,8},{8,16},{16,24},{24,0},{1,9},{9,17},{17,25},{25,1},{2,10},{10... | collective-permute-start | bytes 1228808 | tf_op jit(solution)/shard_map/ppermute | solution.py:35
  195.9 34.8 %collective-permute-start.20 = (bf16[400,512]{1,0:T(8,128)(2,1)S(1)}, bf16[400,512]{1,0:T(8,128)(2,1)}, u32[]{:S(2)}, u32[]{:S(2)}) collective-permute-start(bf16[400,512]{1,0:T(8,128)(2,1)S(1)} %copy-done.9), channel_id=1, source_target_pairs={{0,6},{2,0},{4,2},{6,4},{1,7},{3,1},{5,3},{7,5},{8,14},{10,8},{12,... | collective-permute-start | bytes 1228808 | tf_op jit(solution)/shard_map/ppermute | solution.py:35
  198.6 32.2 %collective-permute-start.21 = (bf16[400,512]{1,0:T(8,128)(2,1)S(1)}, bf16[400,512]{1,0:T(8,128)(2,1)}, u32[]{:S(2)}, u32[]{:S(2)}) collective-permute-start(bf16[400,512]{1,0:T(8,128)(2,1)S(1)} %copy-done.9), channel_id=1, source_target_pairs={{0,2},{2,4},{4,6},{6,0},{1,3},{3,5},{5,7},{7,1},{8,10},{10,12},{12... | collective-permute-start | bytes 1228808 | tf_op jit(solution)/shard_map/ppermute | solution.py:35
  198.6 32.2 %collective-permute-start.22 = (bf16[400,512]{1,0:T(8,128)(2,1)S(1)}, bf16[400,512]{1,0:T(8,128)(2,1)}, u32[]{:S(2)}, u32[]{:S(2)}) collective-permute-start(bf16[400,512]{1,0:T(8,128)(2,1)S(1)} %copy-done.9), channel_id=1, source_target_pairs={{0,4},{2,6},{4,0},{6,2},{1,5},{3,7},{5,1},{7,3},{8,12},{10,14},{12... | collective-permute-start | bytes 1228808 | tf_op jit(solution)/shard_map/ppermute | solution.py:35
  222.0 53.5 %all-to-all-start.1 = ((bf16[64,16,512]{2,1,0:T(8,128)(2,1)}), bf16[64,16,512]{2,1,0:T(8,128)(2,1)S(1)}, u32[]{:S(2)}, u32[]{:S(2)}) async-start(bf16[64,16,512]{2,1,0:T(8,128)(2,1)} %get-tuple-element.76), calls=%async_computation.1 | async-start | bytes 2097152 | tf_op jit(solution)/shard_map/all_to_all | solution.py:466
  (48 other events, 422.4 us)
Sparse Core Ops, SparseCore 0:
  10.1 68.5 all-gather.4
  80.9 60.5 all-gather.6
